TPU v7x, 128 devices: a whole 4x4x4 slice. The times are simulated.
128 devices in a mesh: row: 8 (over y, core), col: 16 (over x, z).
Axes of the slice: x: 4, y: 4, z: 4, core: 2. Of those that a mesh axis runs over, the one named last changes fastest.
Arguments:
- camera_jacobian: float32 [18, 8, 131072], P(None, None, ('row', 'col')), may hold values from -6 to 6
- point_jacobian: float32 [6, 8, 131072], P(None, None, ('row', 'col')), may hold values from -6 to 6
- residuals: float32 [2, 8, 131072], P(None, None, ('row', 'col')), may hold values from -6 to 6
- observed_camera: int32 [8, 131072], P(None, ('row', 'col')), may hold values from 0 to 49151, as said below
- track_length: int32 [131072], P(('row', 'col')), may hold values from 2 to 8
Outputs:
- camera_move: float32 [9, 49152], P(None, ('row', 'col'))
- point_move: float32 [3, 131072], P(None, ('row', 'col'))
Inputs may be any that keep to these rules, and one draw needn't show every extreme that they name: `observed_camera`: the 8 cameras listed for one point are all different.
All inputs are finite; a program needn't handle non-finite values.
Results may differ from a plain program's by a relative error of at most 0.0003.
Values sent between devices are 32-bit elements; how exact they have to be, the bound alone decides.
No kernel may reach another device: no remote copies, remote signals or barrier semaphores. Data moves between devices by JAX's collectives and lax.ppermute only.
A program may use at most 128 MiB of HBM per device.

v0:
```python
import jax
import jax.numpy as jnp
from jax import lax
from jax.sharding import PartitionSpec as P

CAM_DEV = 384
ITERS = 2


damping = 1.0
block_pairs = [(leading, trailing) for leading in range(9) for trailing in range(leading, 9)]


def inverse_small(matrix):
    entries = [[matrix[row_at, col_at] for col_at in range(3)] for row_at in range(3)]
    cofactor = [
        [
            entries[(row_at + 1) % 3][(col_at + 1) % 3]
            * entries[(row_at + 2) % 3][(col_at + 2) % 3]
            - entries[(row_at + 1) % 3][(col_at + 2) % 3]
            * entries[(row_at + 2) % 3][(col_at + 1) % 3]
            for col_at in range(3)
        ]
        for row_at in range(3)
    ]
    determinant = (
        entries[0][0] * cofactor[0][0]
        + entries[0][1] * cofactor[0][1]
        + entries[0][2] * cofactor[0][2]
    )
    return jnp.stack(
        [
            jnp.stack([cofactor[col_at][row_at] / determinant for col_at in range(3)])
            for row_at in range(3)
        ]
    )


def block_inverse(matrix):
    factor = {}
    for col_at in range(9):
        pivot_value = matrix[col_at, col_at]
        for middle in range(col_at):
            pivot_value = pivot_value - factor[col_at, middle] * factor[col_at, middle]
        diagonal_root = jnp.sqrt(pivot_value)
        factor[col_at, col_at] = diagonal_root
        for row_at in range(col_at + 1, 9):
            running = matrix[row_at, col_at]
            for middle in range(col_at):
                running = running - factor[row_at, middle] * factor[col_at, middle]
            factor[row_at, col_at] = running / diagonal_root
    factor_inverse = {}
    for row_at in range(9):
        factor_inverse[row_at, row_at] = 1.0 / factor[row_at, row_at]
        for col_at in range(row_at):
            running = factor[row_at, col_at] * factor_inverse[col_at, col_at]
            for middle in range(col_at + 1, row_at):
                running = running + factor[row_at, middle] * factor_inverse[middle, col_at]
            factor_inverse[row_at, col_at] = -running / factor[row_at, row_at]
    result_rows = []
    for row_at in range(9):
        entries = []
        for col_at in range(9):
            running = (
                factor_inverse[max(row_at, col_at), row_at]
                * factor_inverse[max(row_at, col_at), col_at]
            )
            for middle in range(max(row_at, col_at) + 1, 9):
                running = running + factor_inverse[middle, row_at] * factor_inverse[middle, col_at]
            entries.append(running)
        result_rows.append(jnp.stack(entries))
    return jnp.stack(result_rows)


def assemble(packed):
    positions = {}
    for index_at, pair in enumerate(block_pairs):
        positions[pair[0], pair[1]] = index_at
        positions[pair[1], pair[0]] = index_at
    return jnp.stack(
        [
            jnp.stack(
                [
                    packed[positions[row_at, col_at]] + (damping if row_at == col_at else 0.0)
                    for col_at in range(9)
                ]
            )
            for row_at in range(9)
        ]
    )


def apply_blocks(inverse_blocks, vector):
    return jnp.sum(inverse_blocks * vector[None], axis=1)


def slot_basics(camera_jacobian, point_jacobian, residuals, track_length):
    tracks = camera_jacobian.shape[1]
    in_track = (jnp.arange(tracks, dtype=jnp.int32)[:, None] < track_length[None, :]).astype(
        jnp.float32
    )
    camera_blocks = camera_jacobian.reshape(2, 9, tracks, -1) * in_track
    point_blocks = point_jacobian.reshape(2, 3, tracks, -1) * in_track
    errors = residuals * in_track
    coupling = jnp.sum(camera_blocks[:, :, None] * point_blocks[:, None], axis=0)
    point_system = jnp.sum(point_blocks[:, :, None] * point_blocks[:, None], axis=(0, 3))
    point_system = point_system + damping * jnp.eye(3, dtype=jnp.float32)[:, :, None]
    point_inverse = inverse_small(point_system)
    point_gradient = -jnp.sum(point_blocks * errors[:, None], axis=(0, 2))
    return (camera_blocks, errors, coupling, point_inverse, point_gradient)


def camera_terms(camera_blocks, errors, coupling, point_inverse, point_gradient):
    solved = jnp.sum(point_inverse * point_gradient[None], axis=1)
    scaled = coupling[:, 0][:, None] * point_inverse[0][None, :, None, :]
    for middle in range(1, 3):
        scaled = scaled + coupling[:, middle][:, None] * point_inverse[middle][None, :, None, :]
    packed = []
    for leading, trailing in block_pairs:
        packed.append(
            jnp.sum(camera_blocks[:, leading] * camera_blocks[:, trailing], axis=0)
            - jnp.sum(scaled[leading] * coupling[trailing], axis=0)
        )
    right_side = -jnp.sum(camera_blocks * errors[:, None], axis=0) - jnp.sum(
        coupling * solved[None, :, None], axis=1
    )
    return jnp.concatenate([jnp.stack(packed), right_side], axis=0)


def slot_product(camera_blocks, coupling, point_inverse, gathered):
    projected = jnp.sum(camera_blocks * gathered[None], axis=1)
    pulled = jnp.sum(coupling * gathered[:, None], axis=(0, 2))
    solved = jnp.sum(point_inverse * pulled[None], axis=1)
    return jnp.sum(camera_blocks * projected[:, None], axis=0) - jnp.sum(
        coupling * solved[None, :, None], axis=1
    )


def point_update(coupling, point_inverse, point_gradient, gathered):
    pulled = jnp.sum(coupling * gathered[:, None], axis=(0, 2))
    return jnp.sum(point_inverse * (point_gradient - pulled)[None], axis=1)


def conjugate(right_side, inverse_blocks, product, curvature_sum, energy_sum):
    residual = right_side
    conditioned = apply_blocks(inverse_blocks, residual)
    direction = conditioned
    energy_now = energy_sum(jnp.sum(residual * conditioned))
    camera_step = jnp.zeros_like(right_side)
    taken = []
    for iteration in range(ITERS):
        curved, spread = product(direction)
        step_size = energy_now / curvature_sum(jnp.sum(direction * curved))
        camera_step = camera_step + step_size * direction
        taken.append((step_size, spread))
        if iteration + 1 < ITERS:
            residual = residual - step_size * curved
            conditioned = apply_blocks(inverse_blocks, residual)
            renewed = energy_sum(jnp.sum(residual * conditioned))
            direction = conditioned + renewed / energy_now * direction
            energy_now = renewed
    return (camera_step, taken)


def on_device(camera_jacobian, point_jacobian, residuals, observed_camera, track_length):
    camera_blocks, errors, coupling, point_inverse, point_gradient = slot_basics(
        camera_jacobian, point_jacobian, residuals, track_length
    )
    tracks, points = observed_camera.shape
    cameras = CAM_DEV * lax.axis_size("row") * lax.axis_size("col")
    flat_cameras = observed_camera.reshape(-1)

    def into_cameras(values):
        width = values.shape[0]
        by_camera = (
            jnp.zeros((cameras, width), jnp.float32).at[flat_cameras].add(jnp.transpose(values))
        )
        return jnp.transpose(by_camera)

    def pick_slots(whole):
        slot_rows = jnp.transpose(whole)[flat_cameras]
        return jnp.transpose(slot_rows).reshape(9, tracks, points)

    term_values = camera_terms(
        camera_blocks, errors, coupling, point_inverse, point_gradient
    ).reshape(54, -1)
    local_terms = into_cameras(term_values)
    own_terms = lax.psum_scatter(local_terms, ("row", "col"), scatter_dimension=1, tiled=True)
    inverse_blocks = block_inverse(assemble(own_terms[:45]))
    right_side = own_terms[45:]

    def local_product(whole):
        contrib = slot_product(camera_blocks, coupling, point_inverse, pick_slots(whole))
        return into_cameras(contrib.reshape(9, -1))

    def spread_out(value):
        return lax.all_gather(value, ("row", "col"), axis=1, tiled=True)

    def energy_sum(value):
        return lax.psum(value, ("row", "col"))

    def product(direction):
        whole = spread_out(direction)
        summed = lax.psum_scatter(
            local_product(whole), ("row", "col"), scatter_dimension=1, tiled=True
        )
        return (damping * direction + summed, whole)

    def curvature_sum(value):
        return lax.psum(value, ("row", "col"))

    camera_move, taken = conjugate(right_side, inverse_blocks, product, curvature_sum, energy_sum)
    whole_move = lax.all_gather(camera_move, ("row", "col"), axis=1, tiled=True)
    point_move = point_update(coupling, point_inverse, point_gradient, pick_slots(whole_move))
    return (camera_move, point_move)


def solution(mesh):
    in_specs = (
        P(None, None, ("row", "col")),
        P(None, None, ("row", "col")),
        P(None, None, ("row", "col")),
        P(None, ("row", "col")),
        P(("row", "col")),
    )
    out_specs = (P(None, ("row", "col")), P(None, ("row", "col")))
    return jax.shard_map(
        on_device, mesh=mesh, in_specs=in_specs, out_specs=out_specs, check_vma=False
    )
```

profile of v0, /device:TPU:1, one launch (start us, length us, event | category | flops | bytes accessed | tf_op | source)
XLA Modules:
  0.0 1485.8 jit_solution(15449363772695190828)
XLA Ops:
  40.0 10.2 concatenate.4
  53.2 54.2 %scatter_custom_fusion = f32[49152,54]{1,0:T(8,128)} fusion(s32[8192]{0:T(1024)S(1)} %bitcast.765, f32[8192,54]{1,0:T(8,128)} %copy.775, f32[]{:T(128)} %constant.4.clone.1), kind=kCustom, calls=%fused_computation.10 | custom fusion | flops 442368 | bytes 10617344 | tf_op jit(solution)/shard_map/scatter-add | solution.py:176
  107.4 18.4 %copy.776 = f32[49152,54]{0,1:T(8,128)} copy(f32[49152,54]{1,0:T(8,128)} %scatter_custom_fusion) | data formatting | bytes 21233664 | tf_op jit(solution)/shard_map/scatter-add | solution.py:176
  125.8 220.8 %reduce-scatter.4.cloned.1.call-done = f32[54,384]{1,0:T(8,128)} async-done(((f32[54,49152]{1,0:T(8,128)}), f32[54,384]{1,0:T(8,128)}) %reduce-scatter.4.cloned.1.call-update) | async-done | bytes 82960 | tf_op jit(solution)/shard_map/reduce_scatter | solution.py:188
  358.4 92.8 %all-gather.4.cloned.1.call-done = f32[9,49152]{0,1:T(8,128)} async-done(((f32[9,384]{0,1:T(8,128)}), f32[9,49152]{0,1:T(8,128)}) %all-gather.4.cloned.1.call-update) | async-done | bytes 1769488 | tf_op jit(solution)/shard_map/all_gather | solution.py:197
  451.2 35.9 %gather_fusion = f32[8192,9]{1,0:T(8,128)} fusion(f32[49152,9]{1,0:T(8,128)} %bitcast.704, s32[8192]{0:T(1024)S(1)} %broadcast_clamp_fusion), kind=kCustom, calls=%fused_computation | custom fusion | bytes 622592 | tf_op jit(solution)/shard_map/gather | solution.py:181
  487.1 2.9 copy.779
  493.1 54.2 %scatter_custom_fusion.1 = f32[49152,9]{1,0:T(8,128)} fusion(s32[8192]{0:T(1024)S(1)} %bitcast.767, f32[8192,9]{1,0:T(8,128)} %bitcast.713, f32[]{:T(128)} %constant.4.clone.1), kind=kCustom, calls=%fused_computation.8 | custom fusion | flops 73728 | bytes 1769984 | tf_op jit(solution)/shard_map/scatter-add | solution.py:176
  547.3 15.1 %copy.782 = f32[49152,9]{0,1:T(8,128)} copy(f32[49152,9]{1,0:T(8,128)} %scatter_custom_fusion.1) | data formatting | bytes 3538944 | tf_op jit(solution)/shard_map/scatter-add | solution.py:176
  562.4 206.9 %reduce-scatter.6.cloned.1.call-done = f32[9,384]{1,0:T(8,128)} async-done(((f32[9,49152]{1,0:T(8,128)}), f32[9,384]{1,0:T(8,128)}) %reduce-scatter.6.cloned.1.call-update) | async-done | bytes 13840 | tf_op jit(solution)/shard_map/reduce_scatter | solution.py:204
  770.7 64.6 %all-reduce = (f32[]{:T(128)}, f32[]{:T(128)}) all-reduce(f32[]{:T(128)} %get-tuple-element.103, f32[]{:T(128)} %get-tuple-element.102), channel_id=1, replica_groups=mesh['row'=8,'col'=16] {'row','col'}, use_global_device_ids=true, to_apply=%region_101.0 | all-reduce | flops 2 | bytes 16 | tf_op jit(solution)/shard_map/psum | solution.py:200
  837.3 62.5 %psum.30 = f32[]{:T(128)} all-reduce(f32[]{:T(128)} %multiply_reduce_fusion.107), channel_id=1, replica_groups=mesh['row'=8,'col'=16] {'row','col'}, use_global_device_ids=true, to_apply=%region_113.0 | all-reduce | flops 1 | bytes 8 | tf_op jit(solution)/shard_map/psum | solution.py:200
  901.9 63.7 %all-gather.6.cloned.1.call-done = f32[9,49152]{1,0:T(8,128)} async-done(((f32[9,384]{1,0:T(8,128)}), f32[9,49152]{1,0:T(8,128)}) %all-gather.6.cloned.1.call-update) | async-done | bytes 1769488 | tf_op jit(solution)/shard_map/all_gather | solution.py:197
  965.6 13.4 copy.784
  979.0 35.9 %gather_fusion.1 = f32[8192,9]{1,0:T(8,128)} fusion(f32[49152,9]{1,0:T(8,128)} %copy.784, s32[8192]{0:T(1024)S(1)} %broadcast_clamp_fusion), kind=kCustom, calls=%fused_computation.1 | custom fusion | bytes 622592 | tf_op jit(solution)/shard_map/gather | solution.py:181
  1014.9 2.9 copy.785
  1020.8 54.2 %scatter_custom_fusion.2 = f32[49152,9]{1,0:T(8,128)} fusion(s32[8192]{0:T(1024)S(1)} %bitcast.768, f32[8192,9]{1,0:T(8,128)} %bitcast.712, f32[]{:T(128)} %constant.4.clone.1), kind=kCustom, calls=%fused_computation.6 | custom fusion | flops 73728 | bytes 1769984 | tf_op jit(solution)/shard_map/scatter-add | solution.py:176
  1075.0 15.1 %copy.788 = f32[49152,9]{0,1:T(8,128)} copy(f32[49152,9]{1,0:T(8,128)} %scatter_custom_fusion.2) | data formatting | bytes 3538944 | tf_op jit(solution)/shard_map/scatter-add | solution.py:176
  1090.2 205.1 %reduce-scatter.8.cloned.1.call-done = f32[9,384]{1,0:T(8,128)} async-done(((f32[9,49152]{1,0:T(8,128)}), f32[9,384]{1,0:T(8,128)}) %reduce-scatter.8.cloned.1.call-update) | async-done | bytes 13840 | tf_op jit(solution)/shard_map/reduce_scatter | solution.py:204
  1296.6 64.3 %psum.31 = f32[]{:T(128)} all-reduce(f32[]{:T(128)} %fusion.10), channel_id=1, replica_groups=mesh['row'=8,'col'=16] {'row','col'}, use_global_device_ids=true, to_apply=%region_122.0 | all-reduce | flops 1 | bytes 8 | tf_op jit(solution)/shard_map/psum | solution.py:210
  1362.9 63.1 %all-gather.8.cloned.1.call-done = f32[9,49152]{1,0:T(8,128)} async-done(((f32[9,384]{1,0:T(8,128)}), f32[9,49152]{1,0:T(8,128)}) %all-gather.8.cloned.1.call-update) | async-done | bytes 1769488 | tf_op jit(solution)/shard_map/all_gather | solution.py:213
  1426.0 13.4 copy.789
  1439.4 35.9 %gather_fusion.2 = f32[8192,9]{1,0:T(8,128)} fusion(f32[49152,9]{1,0:T(8,128)} %copy.789, s32[8192]{0:T(1024)S(1)} %broadcast_clamp_fusion), kind=kCustom, calls=%fused_computation.2 | custom fusion | bytes 622592 | tf_op jit(solution)/shard_map/gather | solution.py:181
  1475.3 2.9 copy.790
  (203 shorter events, 58.8 us)
Async XLA Ops:
  7.2 339.4 %reduce-scatter.4.cloned.1.call-start = ((), (), s32[]{:S(2)}) async-start(), calls=%async_computation.3 | async-start | bytes 11096064 | tf_op jit(solution)/shard_map/reduce_scatter | solution.py:188
  11.7 0.9 copy-start
  50.3 2.8 copy-start.3
  125.7 325.5 %all-gather.4.cloned.1.call-start = ((), (), s32[]{:S(2)}) async-start(), calls=%async_computation.4 | async-start | bytes 25362432 | tf_op jit(solution)/shard_map/all_gather | solution.py:197
  358.3 411.0 %reduce-scatter.6.cloned.1.call-start = ((), (), s32[]{:S(2)}) async-start(), calls=%async_computation.5 | async-start | bytes 3170304 | tf_op jit(solution)/shard_map/reduce_scatter | solution.py:204
  547.3 222.1 %copy-start.1 = (f32[54,384]{1,0:T(8,128)S(1)}, f32[54,384]{1,0:T(8,128)}, u32[]{:S(2)}) copy-start(f32[54,384]{1,0:T(8,128)} %reduce-scatter.4.cloned.1.call-done) | copy-start | bytes 248836
  562.4 403.2 %all-gather.6.cloned.1.call-start = ((), (), s32[]{:S(2)}) async-start(), calls=%async_computation.6 | async-start | bytes 3170304 | tf_op jit(solution)/shard_map/all_gather | solution.py:197
  901.8 393.4 %reduce-scatter.8.cloned.1.call-start = ((), (), s32[]{:S(2)}) async-start(), calls=%async_computation.7 | async-start | bytes 3170304 | tf_op jit(solution)/shard_map/reduce_scatter | solution.py:204
  1075.0 220.2 %copy-start.2 = (f32[9,384]{1,0:T(8,128)S(1)}, f32[9,384]{1,0:T(8,128)}, u32[]{:S(2)}) copy-start(f32[9,384]{1,0:T(8,128)} %multiply_add_fusion.2) | copy-start | bytes 41476
  1090.1 335.9 %all-gather.8.cloned.1.call-start = ((), (), s32[]{:S(2)}) async-start(), calls=%async_computation.8 | async-start | bytes 3170304 | tf_op jit(solution)/shard_map/all_gather | solution.py:213
Sparse Core Ops, SparseCore 0:
  125.9 220.6 reduce-scatter.3
  358.5 92.7 all-gather.3
  562.5 206.8 reduce-scatter.5
  902.0 63.6 all-gather.5
  1090.2 204.9 reduce-scatter.7
  1363.0 62.9 all-gather.7
where the time goes:
time: 1490 us
  waiting for transfers between devices  853 us (57%)
  local copies, waits for them, and re-layouts  245 us (16%)
  blocking collectives  191 us (13%)
  other arithmetic  178 us (12%)
  between operations  18.8 us (1%)
    reduce_scatter x2, waiting for transfers between devices, product(): lax.psum_scatter(local_product(whole), ('row', 'col'), scatter_dimension=...  412 us
    reduce_scatter x1, waiting for transfers between devices, on_device(): lax.psum_scatter(local_terms, ('row', 'col'), scatter_dimension=1, tiled=...  221 us
    scatter-add x3, other arithmetic, into_cameras(): jnp.zeros((cameras, width), jnp.float32).at[flat_cameras]  163 us
    all_gather x2, waiting for transfers between devices, spread_out(): return lax.all_gather(value, ('row', 'col'), axis=1, tiled=True)  157 us
    psum x2, blocking collectives, energy_sum(): return lax.psum(value, ('row', 'col'))  127 us
    gather x3, local copies, waits for them, and re-layouts, pick_slots(): slot_rows = jnp.transpose(whole)[flat_cameras]  108 us
    psum x1, blocking collectives, curvature_sum(): return lax.psum(value, ('row', 'col'))  64.3 us
    all_gather x1, waiting for transfers between devices, on_device(): whole_move = lax.all_gather(camera_move, ('row', 'col'), axis=1, tiled=True)  63.1 us
  transfers between devices with their start and end apart: 6, of which 6 were waited for; matrix products, arithmetic and copies ran while one was open for 0% of the time, Pallas kernels for 0%

commit v1 on v0

--- a/solution.py
+++ b/solution.py
@@ -1,14 +1,628 @@
 import jax
 import jax.numpy as jnp
 from jax import lax
+from jax.experimental import pallas as pl
+from jax.experimental.pallas import tpu as pltpu
 from jax.sharding import PartitionSpec as P
 
 CAM_DEV = 384
-ITERS = 2
+TRACK = 8
+PT_DEV = 1024
+OWNERS = 128
+LANES = 128
+WIDTH = 21
+GROUPS = 6
+ROWS = 13
+CAP = GROUPS * ROWS
+SPAN = 80
+FEW = 64
+CAMERA_AT = 20
+ENTRIES = 56
+COUNT_AT = GROUPS * WIDTH
+BLOCKS = TRACK * PT_DEV // LANES
+
+F32 = jnp.float32
+BF16 = jnp.bfloat16
+PARAMS = pltpu.CompilerParams(vmem_limit_bytes=48 * 2**20)
+block_pairs = [(leading, trailing) for leading in range(9) for trailing in range(leading, 9)]
+
+
+def iota(shape, axis):
+    return lax.broadcasted_iota(jnp.int32, shape, axis)
+
+
+def two_parts(value):
+    high = value.astype(BF16)
+    low = (value - high.astype(F32)).astype(BF16)
+    return high, low
+
+
+def dot(left, right):
+    return jnp.dot(left, right, preferred_element_type=F32)
+
+
+def dot_lanes(left, right):
+    return lax.dot_general(left, right, (((1,), (1,)), ((), ())), preferred_element_type=F32)
+
+
+def total(value):
+    return jnp.sum(jnp.sum(value, axis=0, keepdims=True), axis=1, keepdims=True)
+
+
+def over_tracks(value):
+    return jnp.sum(value, axis=0, keepdims=True)
+
+
+def used_slots(length_ref, lanes):
+    return iota((TRACK, LANES), 0) < length_ref[:, lanes]
+
+
+def masked_points(point_ref, used, lanes):
+    return [
+        [jnp.where(used, point_ref[3 * i + a, :, lanes], 0.0) for a in range(3)] for i in range(2)
+    ]
+
+
+def times_inverse(inverse, vector):
+    v00, v01, v02, v11, v12, v22 = inverse
+    x, y, z = vector
+    return [v00 * x + v01 * y + v02 * z, v01 * x + v11 * y + v12 * z, v02 * x + v12 * y + v22 * z]
+
+
+def prepare_kernel(camera_ref, point_ref, error_ref, index_ref, length_ref, pay_ref, code_ref, route_ref, state_ref, root_ref, flag_ref):
+    for chunk in range(PT_DEV // LANES):
+        lanes = slice(chunk * LANES, (chunk + 1) * LANES)
+        used = used_slots(length_ref, lanes)
+        point = masked_points(point_ref, used, lanes)
+        error = [jnp.where(used, error_ref[i, :, lanes], 0.0) for i in range(2)]
+
+        def pair(a, b):
+            return over_tracks(point[0][a] * point[0][b] + point[1][a] * point[1][b])
+
+        s00, s01, s02 = 1.0 + pair(0, 0), pair(0, 1), pair(0, 2)
+        s11, s12, s22 = 1.0 + pair(1, 1), pair(1, 2), 1.0 + pair(2, 2)
+        c00 = s11 * s22 - s12 * s12
+        c01 = s12 * s02 - s01 * s22
+        c02 = s01 * s12 - s11 * s02
+        c11 = s22 * s00 - s02 * s02
+        c12 = s02 * s01 - s12 * s00
+        c22 = s00 * s11 - s01 * s01
+        determinant = s00 * c00 + s01 * c01 + s02 * c02
+        inverse = [c / determinant for c in (c00, c01, c02, c11, c12, c22)]
+        gradient = [
+            -over_tracks(point[0][a] * error[0] + point[1][a] * error[1]) for a in range(3)
+        ]
+        for at, value in enumerate(inverse + gradient):
+            state_ref[at : at + 1, lanes] = value
+        solved = times_inverse(inverse, gradient)
+        u0 = times_inverse(inverse, point[0])
+        u1 = times_inverse(inverse, point[1])
+
+        def along(left, right):
+            return left[0] * right[0] + left[1] * right[1] + left[2] * right[2]
+
+        camera = index_ref[:, lanes]
+        owner = ((camera >> 7) * 171) >> 9
+        local = camera - owner * CAM_DEV
+        b01 = -along(u0, point[1])
+        root0 = jnp.sqrt(1.0 - along(u0, point[0]))
+        root1 = b01 / root0
+        root2 = jnp.sqrt(1.0 - along(u1, point[1]) - root1 * root1)
+        inverse0, inverse2 = 1.0 / root0, 1.0 / root2
+        side0 = (error[0] + along(solved, point[0])) * inverse0
+        side1 = (error[1] + along(solved, point[1]) - root1 * side0) * inverse2
+        values = [root0 * camera_ref[j, :, lanes] + root1 * camera_ref[9 + j, :, lanes] for j in range(9)]
+        values += [root2 * camera_ref[9 + j, :, lanes] for j in range(9)]
+        values += [side0, side1, (local + 1).astype(F32)]
+        for at, value in enumerate((inverse0, root1, inverse2)):
+            root_ref[at * TRACK : (at + 1) * TRACK, lanes] = value
+        for f in range(WIDTH):
+            at = (chunk * WIDTH + f) * TRACK
+            pay_ref[at : at + TRACK, :] = values[f]
+        route_ref[0:TRACK, lanes] = jnp.where(used, owner, OWNERS)
+
+    step = 256
+    earlier = jnp.where(iota((step, step), 0) < iota((step, step), 1), 1.0, 0.0).astype(BF16)
+    everything = jnp.ones((step, step), BF16)
+    before = jnp.zeros((OWNERS, step), F32)
+    names = iota((OWNERS, step), 0)
+    for s in range(TRACK):
+        for chunk in range(PT_DEV // step):
+            lanes = slice(chunk * step, (chunk + 1) * step)
+            chosen = names == route_ref[s : s + 1, lanes]
+            hot = jnp.where(chosen, 1.0, 0.0).astype(BF16)
+            rank = jnp.sum(
+                jnp.where(chosen, dot(hot, earlier) + before, 0.0), axis=0, keepdims=True
+            )
+            before = before + dot(hot, everything)
+            route_ref[TRACK + s : TRACK + s + 1, lanes] = rank.astype(jnp.int32)
+
+    owner = route_ref[0:TRACK, :]
+    rank = route_ref[TRACK : 2 * TRACK, :]
+    fits = (owner < OWNERS) & (rank < CAP)
+    row_at = (rank * 171) >> 10
+    place = (rank - row_at * GROUPS) * (OWNERS * ROWS) + owner * ROWS + row_at
+    code = jnp.where(fits, place, GROUPS * OWNERS * ROWS)
+    for chunk in range(PT_DEV // LANES):
+        code_ref[chunk * TRACK : (chunk + 1) * TRACK, :] = code[:, chunk * LANES : (chunk + 1) * LANES]
+    most = jnp.max(jnp.max(before, axis=0, keepdims=True), axis=1, keepdims=True)
+    lane = iota((OWNERS, LANES), 1)
+    flag_ref[...] = jnp.where(lane > COUNT_AT, most, before[:, 0:LANES])
+
+
+def dispatch_kernel(code_ref, pay_ref, flag_ref, out_ref, slot_ref, block_ref):
+    rows = OWNERS * ROWS
+    zeros = jnp.zeros((8, LANES), F32)
+    slots_ref = slot_ref.reshape(BLOCKS * LANES, LANES)
+    blocks_ref = block_ref.reshape(GROUPS * rows + 8, LANES)
+
+    def clear(at, carry):
+        for j in range(16):
+            blocks_ref[pl.ds(pl.multiple_of(at * 128 + j * 8, 8), 8), :] = zeros
+        return carry
+
+    lax.fori_loop(0, GROUPS * rows // 128, clear, 0)
+    within = iota((LANES, LANES), 1) % WIDTH
+    for first in range(0, BLOCKS, GROUPS):
+        blocks = []
+        for block in range(first, first + GROUPS):
+            chunk, s = divmod(block, TRACK)
+            if block < BLOCKS:
+                blocks.append(pay_ref[pl.ds(chunk * WIDTH * TRACK + s, WIDTH, stride=TRACK), :])
+            else:
+                blocks.append(jnp.zeros((WIDTH, LANES), F32))
+        turned = jnp.transpose(jnp.concatenate(blocks + [zeros[0 : LANES - COUNT_AT]], axis=0))
+        for block in range(first, min(first + GROUPS, BLOCKS)):
+            slots_ref[block * LANES : (block + 1) * LANES, :] = jnp.take_along_axis(
+                turned, within + (block - first) * WIDTH, axis=1, mode="promise_in_bounds"
+            )
+
+    def place(block, carry):
+        for start in range(0, LANES, 32):
+            columns = range(start, start + 32)
+            codes = [code_ref[block, j] for j in columns]
+            slots = [slot_ref[block, j] for j in columns]
+            for code, slot in zip(codes, slots):
+                block_ref[code] = slot
+        return carry
+
+    lax.fori_loop(0, BLOCKS, place, 0)
+    group = iota((8, LANES), 1) // WIDTH
+
+    def merge(at, carry):
+        for j in range(8):
+            start = pl.multiple_of(at * 64 + j * 8, 8)
+            value = zeros
+            for k in range(GROUPS):
+                value = jnp.where(group == k, blocks_ref[pl.ds(k * rows + start, 8), :], value)
+            out_ref[pl.ds(start, 8), :] = value
+        return carry
+
+    lax.fori_loop(0, rows // 64, merge, 0)
+    lane = iota((OWNERS, LANES), 1)
+    leading = pl.ds(0, OWNERS, stride=ROWS)
+    out_ref[leading, :] = jnp.where(lane >= COUNT_AT, flag_ref[...], out_ref[leading, :])
+
+
+def solve(factor, roots, vector):
+    forward = []
+    for i in range(9):
+        value = vector[i]
+        for j in range(i):
+            value = value - factor[i, j] * forward[j]
+        forward.append(value / roots[i])
+    result = [None] * 9
+    for i in reversed(range(9)):
+        value = forward[i]
+        for j in range(i + 1, 9):
+            value = value - factor[j, i] * result[j]
+        result[i] = value / roots[i]
+    return result
+
+
+def hot_cameras(feature_ref, hot_ref, block):
+    names = iota((LANES, LANES), 0)
+    for r in range(8):
+        camera = feature_ref[pl.ds(CAMERA_AT * SPAN + block * 8 + r, 1), :].astype(jnp.int32) - 1
+        hot = jnp.where(names == (camera & (LANES - 1)), 1.0, 0.0).astype(BF16)
+        hot_ref[:, pl.ds(pl.multiple_of(block * PT_DEV + r * LANES, LANES), LANES)] = hot
+
+
+def features_of(feature_ref, f, block):
+    return feature_ref[pl.ds(pl.multiple_of(f * SPAN + block * 8, 8), 8), :]
+
+
+def image_slots(vector, feature_ref, table_ref, image_ref, blocks):
+    for j in range(9):
+        for c in range(3):
+            at = (3 * j + c) * 8
+            table_ref[at : at + 8, :] = jnp.broadcast_to(vector[j][c : c + 1, :], (8, LANES))
+
+    def one(block, carry):
+        camera = features_of(feature_ref, CAMERA_AT, block).astype(jnp.int32) - 1
+        third = camera >> 7
+        lane = camera & (LANES - 1)
+        images = [jnp.zeros((8, LANES), F32)] * 2
+        for j in range(9):
+            found = [
+                jnp.take_along_axis(
+                    table_ref[(3 * j + c) * 8 : (3 * j + c + 1) * 8, :],
+                    lane,
+                    axis=1,
+                    mode="promise_in_bounds",
+                )
+                for c in range(3)
+            ]
+            value = jnp.where(third == 1, found[1], jnp.where(third == 2, found[2], found[0]))
+            for i in range(2):
+                images[i] = images[i] + features_of(feature_ref, 9 * i + j, block) * value
+        for i in range(2):
+            image_ref[pl.ds(pl.multiple_of(i * LANES + block * 8, 8), 8), :] = images[i]
+        return carry
+
+    lax.fori_loop(0, blocks, one, 0)
+
+
+def keep_parts(part_ref, feature_ref, parts_ref, block, count):
+    for r in range(8):
+        lanes = pl.ds(pl.multiple_of(block * PT_DEV + r * LANES, LANES), LANES)
+        camera = feature_ref[pl.ds(CAMERA_AT * SPAN + block * 8 + r, 1), :].astype(jnp.int32) - 1
+        value = part_ref[pl.ds(r, count, stride=8), :]
+        high = value.astype(BF16).astype(F32)
+        both = jnp.concatenate([high, value - high], axis=0).astype(BF16)
+        third = jnp.broadcast_to(camera >> 7, (16, LANES))
+        for c in range(3):
+            inside = jnp.where(third == c, 1.0, 0.0).astype(BF16)
+            inside = jnp.concatenate([inside] * (count // 8), axis=0)
+            parts_ref[2 * c * count : 2 * (c + 1) * count, lanes] = both * inside
+
+
+def camera_sums(parts_ref, hot_ref, part_ref, sum_ref, count, many):
+    few = FEW * LANES
+    sum_ref[...] = dot_lanes(parts_ref[:, 0:few], hot_ref[:, 0:few])
+
+    @pl.when(many)
+    def _():
+        sum_ref[...] += dot_lanes(parts_ref[:, few:], hot_ref[:, few:])
+
+    part_ref[...] = jnp.zeros(part_ref.shape, F32)
+    for c in range(3):
+        at = 2 * c * count
+        part_ref[pl.ds(c, count, stride=8), :] = (
+            sum_ref[at : at + count, :] + sum_ref[at + count : at + 2 * count, :]
+        )
+
+
+def turn_in(got_ref, i):
+    return jnp.transpose(got_ref[pl.ds(i, OWNERS, stride=2), :])
+
+
+def turn_out(image_ref, out_ref):
+    for i in range(2):
+        out_ref[pl.ds(i, OWNERS, stride=2), :] = jnp.transpose(
+            image_ref[i * LANES : (i + 1) * LANES, :]
+        )
+
+
+def first_camera_kernel(got_ref, feature_ref, factor_ref, first_ref, out_ref, flag_ref, hot_ref, parts_ref, table_ref, image_ref, sum_ref, part_ref):
+    image_ref[...] = jnp.zeros((2 * LANES, LANES), F32)
+    feature_ref[...] = jnp.zeros(feature_ref.shape, F32)
+
+    def take_row(q):
+        turned = jnp.transpose(got_ref[pl.ds(q, OWNERS, stride=ROWS), :])
+        for k in range(GROUPS):
+            feature_ref[pl.ds(q * GROUPS + k, WIDTH, stride=SPAN), :] = turned[
+                k * WIDTH : (k + 1) * WIDTH, :
+            ]
+        return turned
+
+    turned = take_row(0)
+    flag_ref[...] = jnp.broadcast_to(
+        jnp.max(turned[COUNT_AT + 1 : COUNT_AT + 2, :], axis=1, keepdims=True), (8, LANES)
+    )
+    most = jnp.max(turned[COUNT_AT : COUNT_AT + 1, :])
+    many = most > FEW
+    blocks = jnp.where(many, SPAN // 8, FEW // 8)
+    few_rows = -(-FEW // GROUPS)
+    for q in range(1, few_rows):
+        take_row(q)
+
+    @pl.when(many)
+    def _():
+        for q in range(few_rows, ROWS):
+            take_row(q)
+
+    part_ref[...] = jnp.zeros((ENTRIES * 8, LANES), F32)
+
+    def gather_terms(block, carry):
+        hot_cameras(feature_ref, hot_ref, block)
+        f = [features_of(feature_ref, at, block) for at in range(20)]
+        for at, (j, k) in enumerate(block_pairs):
+            part_ref[at * 8 : (at + 1) * 8, :] = f[j] * f[k] + f[9 + j] * f[9 + k]
+        for j in range(9):
+            part_ref[(45 + j) * 8 : (46 + j) * 8, :] = -(f[j] * f[18] + f[9 + j] * f[19])
+        keep_parts(part_ref, feature_ref, parts_ref, block, ENTRIES)
+        return carry
+
+    lax.fori_loop(0, blocks, gather_terms, 0)
+    camera_sums(parts_ref, hot_ref, part_ref, sum_ref, ENTRIES, many)
+    matrix = {}
+    for at, (j, k) in enumerate(block_pairs):
+        entry = part_ref[at * 8 : (at + 1) * 8, :]
+        matrix[k, j] = entry + 1.0 if j == k else entry
+    side = [part_ref[(45 + j) * 8 : (46 + j) * 8, :] for j in range(9)]
+    factor, roots = {}, []
+    for j in range(9):
+        pivot = matrix[j, j]
+        for m in range(j):
+            pivot = pivot - factor[j, m] * factor[j, m]
+        roots.append(jnp.sqrt(pivot))
+        for i in range(j + 1, 9):
+            running = matrix[i, j]
+            for m in range(j):
+                running = running - factor[i, m] * factor[j, m]
+            factor[i, j] = running / roots[j]
+    for at, (j, k) in enumerate(block_pairs):
+        factor_ref[at * 8 : (at + 1) * 8, :] = roots[j] if j == k else factor[k, j]
+    first = solve(factor, roots, side)
+    energy = side[0] * first[0]
+    for j in range(1, 9):
+        energy = energy + side[j] * first[j]
+    for j in range(9):
+        first_ref[j * 8 : (j + 1) * 8, :] = first[j]
+    first_ref[72:80, :] = energy
+    first_ref[80:88, :] = jnp.broadcast_to(jnp.max(turned[COUNT_AT : COUNT_AT + 1, :], axis=1, keepdims=True), (8, LANES))
+    image_slots(first, feature_ref, table_ref, image_ref, blocks)
+    turn_out(image_ref, out_ref)
+
+
+def pull_slots(got_ref, route_ref, point_ref, length_ref, state_ref, root_ref, value_ref, pulled_ref, curve_ref, back):
+    images = []
+    for i in range(2):
+        images.append(turn_in(got_ref, i)[0:SPAN, :])
+    high, low = two_parts(jnp.concatenate(images, axis=0))
+    parts = jnp.concatenate([high, low], axis=1)
+    owners = iota((OWNERS, PT_DEV), 0)
+    ranks = iota((SPAN, PT_DEV), 0)
+    for s in range(TRACK):
+        hot = jnp.where(owners == route_ref[s : s + 1, :], 1.0, 0.0).astype(BF16)
+        got = dot(parts, jnp.concatenate([hot, hot], axis=0))
+        here = ranks == route_ref[TRACK + s : TRACK + s + 1, :]
+        for i in range(2):
+            value_ref[i * TRACK + s : i * TRACK + s + 1, :] = jnp.sum(
+                jnp.where(here, got[i * SPAN : (i + 1) * SPAN, :], 0.0), axis=0, keepdims=True
+            )
+    curve = jnp.zeros((TRACK, LANES), F32)
+    for chunk in range(PT_DEV // LANES):
+        lanes = slice(chunk * LANES, (chunk + 1) * LANES)
+        used = used_slots(length_ref, lanes)
+        point = masked_points(point_ref, used, lanes)
+        root = [root_ref[at * TRACK : (at + 1) * TRACK, lanes] for at in range(3)]
+        image1 = value_ref[TRACK : 2 * TRACK, lanes] * root[2]
+        image = [(value_ref[0:TRACK, lanes] - root[1] * image1) * root[0], image1]
+        pulled = [over_tracks(point[0][a] * image[0] + point[1][a] * image[1]) for a in range(3)]
+        inverse = [state_ref[at : at + 1, lanes] for at in range(6)]
+        solved = times_inverse(inverse, pulled)
+        for a in range(3):
+            pulled_ref[a : a + 1, lanes] = pulled[a]
+        result = [
+            image[i] - (point[i][0] * solved[0] + point[i][1] * solved[1] + point[i][2] * solved[2])
+            for i in range(2)
+        ]
+        if back:
+            result0 = result[0] * root[0]
+            value_ref[0:TRACK, lanes] = result0
+            value_ref[TRACK : 2 * TRACK, lanes] = (result[1] - root[1] * result0) * root[2]
+        else:
+            curve = curve + image[0] * result[0] + image[1] * result[1]
+    if not back:
+        curve_ref[...] = curve
+
+
+def first_point_kernel(got_ref, route_ref, point_ref, length_ref, state_ref, root_ref, pulled_ref, out_ref, value_ref, image_ref):
+    pull_slots(got_ref, route_ref, point_ref, length_ref, state_ref, root_ref, value_ref, pulled_ref, None, True)
+    owners = iota((OWNERS, PT_DEV), 0)
+    ranks = iota((SPAN, PT_DEV), 0)
+    sums = jnp.zeros((4 * SPAN, OWNERS), F32)
+    for s in range(TRACK):
+        hot = jnp.where(owners == route_ref[s : s + 1, :], 1.0, 0.0).astype(BF16)
+        here = ranks == route_ref[TRACK + s : TRACK + s + 1, :]
+        spread = []
+        for i in range(2):
+            value = value_ref[i * TRACK + s : i * TRACK + s + 1, :]
+            spread.append(jnp.where(here, value, 0.0))
+        high, low = two_parts(jnp.concatenate(spread, axis=0))
+        sums = sums + dot_lanes(jnp.concatenate([high, low], axis=0), hot)
+    sums = sums[0 : 2 * SPAN] + sums[2 * SPAN :]
+    image_ref[...] = jnp.zeros((2 * LANES, LANES), F32)
+    for i in range(2):
+        image_ref[i * LANES : i * LANES + SPAN, :] = sums[i * SPAN : (i + 1) * SPAN, :]
+    turn_out(image_ref, out_ref)
+
+
+def second_point_kernel(got_ref, route_ref, point_ref, length_ref, state_ref, root_ref, pulled_ref, out_ref, scalar_ref, value_ref, curve_ref):
+    pull_slots(got_ref, route_ref, point_ref, length_ref, state_ref, root_ref, value_ref, pulled_ref, curve_ref, False)
+    out_ref[...] = jnp.broadcast_to(total(curve_ref[...]), (OWNERS, LANES))
+    scalar_ref[...] = jnp.broadcast_to(
+        jnp.sum(got_ref[pl.ds(0, OWNERS, stride=2), :], axis=0, keepdims=True), (8, LANES)
+    )
+
+
+def second_camera_kernel(got_ref, feature_ref, factor_ref, first_ref, second_ref, out_ref, hot_ref, parts_ref, table_ref, image_ref, sum_ref, wide_ref):
+    for i in range(2):
+        image_ref[i * LANES : (i + 1) * LANES, :] = turn_in(got_ref, i)
+    many = jnp.max(first_ref[80:88, :]) > FEW
+    blocks = jnp.where(many, SPAN // 8, FEW // 8)
+    wide_ref[...] = jnp.zeros((LANES, LANES), F32)
+
+    def gather_terms(block, carry):
+        hot_cameras(feature_ref, hot_ref, block)
+        back = [
+            image_ref[pl.ds(pl.multiple_of(i * LANES + block * 8, 8), 8), :] for i in range(2)
+        ]
+        for j in range(9):
+            wide_ref[j * 8 : (j + 1) * 8, :] = (
+                features_of(feature_ref, j, block) * back[0]
+                + features_of(feature_ref, 9 + j, block) * back[1]
+            )
+        keep_parts(wide_ref, feature_ref, parts_ref, block, 16)
+        return carry
+
+    lax.fori_loop(0, blocks, gather_terms, 0)
+    camera_sums(parts_ref, hot_ref, wide_ref, sum_ref, 16, many)
+    first = [first_ref[j * 8 : (j + 1) * 8, :] for j in range(9)]
+    image = [first[j] + wide_ref[j * 8 : (j + 1) * 8, :] for j in range(9)]
+    factor, roots = {}, []
+    for at, (j, k) in enumerate(block_pairs):
+        entry = factor_ref[at * 8 : (at + 1) * 8, :]
+        if j == k:
+            roots.append(entry)
+        else:
+            factor[k, j] = entry
+    second = solve(factor, roots, image)
+    for j in range(9):
+        second_ref[j * 8 : (j + 1) * 8, :] = second[j]
+
+    def inner(left, right):
+        value = left[0] * right[0]
+        for j in range(1, 9):
+            value = value + left[j] * right[j]
+        return value
+
+    image_slots(second, feature_ref, table_ref, image_ref, blocks)
+    scalars = [first_ref[72:80, :], inner(first, image), inner(image, second), inner(second, second)]
+    for at, value in enumerate(scalars):
+        image_ref[SPAN + at : SPAN + at + 1, :] = jnp.broadcast_to(total(value), (1, LANES))
+    turn_out(image_ref, out_ref)
+
+
+def finish_kernel(curve_ref, scalar_ref, first_ref, second_ref, state_ref, first_pulled_ref, second_pulled_ref, camera_out, point_out, camera_ref, point_ref, camera_sem, point_sem):
+    own = jnp.sum(curve_ref[...], axis=0, keepdims=True)[:, 0:1]
+    energy, curvature, crossed, square = [
+        scalar_ref[0:1, SPAN + at : SPAN + at + 1] for at in range(4)
+    ]
+    step_size = energy / curvature
+    renewed = step_size * step_size * crossed - energy
+    ratio = 1.0 + renewed / energy
+    second_step = renewed / (
+        ratio * ratio * curvature
+        - 2.0 * step_size * ratio * crossed
+        + step_size * step_size * (square + own)
+    )
+    first_weight = step_size + second_step * ratio
+    second_weight = -second_step * step_size
+    for c in range(3):
+        camera_ref[:, c * LANES : (c + 1) * LANES] = (
+            first_weight * first_ref[pl.ds(c, 9, stride=8), :]
+            + second_weight * second_ref[pl.ds(c, 9, stride=8), :]
+        )
+    camera_copy = pltpu.make_async_copy(camera_ref, camera_out, camera_sem)
+    camera_copy.start()
+    left = [
+        state_ref[6 + a : 7 + a, :]
+        - first_weight * first_pulled_ref[a : a + 1, :]
+        - second_weight * second_pulled_ref[a : a + 1, :]
+        for a in range(3)
+    ]
+    moved = times_inverse([state_ref[at : at + 1, :] for at in range(6)], left)
+    for a in range(3):
+        point_ref[a : a + 1, :] = moved[a]
+    point_copy = pltpu.make_async_copy(point_ref, point_out, point_sem)
+    point_copy.start()
+    camera_copy.wait()
+    point_copy.wait()
+
+
+def call(kernel, outs, scratch, operands, in_scalar=0):
+    specs = [
+        pl.BlockSpec(memory_space=pltpu.SMEM if at < in_scalar else pltpu.VMEM)
+        for at in range(len(operands))
+    ]
+    return pl.pallas_call(
+        kernel,
+        out_shape=[jax.ShapeDtypeStruct(shape, dtype) for shape, dtype in outs],
+        in_specs=specs,
+        out_specs=[pl.BlockSpec(memory_space=pltpu.VMEM)] * len(outs),
+        scratch_shapes=[pltpu.VMEM(shape, dtype) for shape, dtype in scratch],
+        compiler_params=PARAMS,
+    )(*operands)
+
+
+def exchange(rows):
+    blocks = rows.reshape(OWNERS, 1, -1)
+    blocks = lax.all_to_all(blocks, ("row", "col"), split_axis=0, concat_axis=0, tiled=True)
+    return blocks.reshape(rows.shape)
+
+
+def by_slots(camera_jacobian, point_jacobian, residuals, observed_camera, track_length):
+    lengths = track_length.reshape(1, PT_DEV)
+    pay, code, route, state, root, flag = call(
+        prepare_kernel,
+        [
+            ((WIDTH * PT_DEV * TRACK // LANES, LANES), F32),
+            ((BLOCKS, LANES), jnp.int32),
+            ((2 * TRACK, PT_DEV), jnp.int32),
+            ((16, PT_DEV), F32),
+            ((3 * TRACK, PT_DEV), F32),
+            ((OWNERS, LANES), F32),
+        ],
+        [],
+        (camera_jacobian, point_jacobian, residuals, observed_camera, lengths),
+    )
+    (sent,) = call(
+        dispatch_kernel,
+        [((OWNERS * ROWS, LANES), F32)],
+        [((BLOCKS, LANES, 1, LANES), F32), ((GROUPS * OWNERS * ROWS + 8, 1, LANES), F32)],
+        (code, pay, flag),
+        in_scalar=1,
+    )
+    hot = ((LANES, SPAN * LANES), BF16)
+    table = ((27 * 8, LANES), F32)
+    image = ((2 * LANES, LANES), F32)
+    pair = ((2 * OWNERS, LANES), F32)
+    features, factor, first, out, overflow = call(
+        first_camera_kernel,
+        [((WIDTH * SPAN, LANES), F32), ((45 * 8, LANES), F32), ((88, LANES), F32), pair, ((8, LANES), F32)],
+        [hot, ((6 * ENTRIES, SPAN * LANES), BF16), table, image, ((6 * ENTRIES, LANES), F32), ((ENTRIES * 8, LANES), F32)],
+        (exchange(sent),),
+    )
+    first_pulled, out = call(
+        first_point_kernel,
+        [((8, PT_DEV), F32), pair],
+        [((2 * TRACK, PT_DEV), F32), image],
+        (exchange(out), route, point_jacobian, lengths, state, root),
+    )
+    second, out = call(
+        second_camera_kernel,
+        [((72, LANES), F32), pair],
+        [hot, ((96, SPAN * LANES), BF16), table, image, ((96, LANES), F32), ((LANES, LANES), F32)],
+        (exchange(out), features, factor, first),
+    )
+    second_pulled, curve, scalars = call(
+        second_point_kernel,
+        [((8, PT_DEV), F32), ((OWNERS, LANES), F32), ((8, LANES), F32)],
+        [((2 * TRACK, PT_DEV), F32), ((TRACK, LANES), F32)],
+        (exchange(out), route, point_jacobian, lengths, state, root),
+    )
+    return overflow[0, 0], (exchange(curve), scalars, first, second, state, first_pulled, second_pulled)
+
+
+def finish(*operands):
+    shapes = [(9, CAM_DEV), (3, PT_DEV)]
+    return tuple(
+        pl.pallas_call(
+            finish_kernel,
+            out_shape=[jax.ShapeDtypeStruct(shape, F32) for shape in shapes],
+            in_specs=[pl.BlockSpec(memory_space=pltpu.VMEM)] * len(operands),
+            out_specs=[pl.BlockSpec(memory_space=pltpu.HBM)] * 2,
+            scratch_shapes=[pltpu.VMEM(shape, F32) for shape in shapes]
+            + [pltpu.SemaphoreType.DMA] * 2,
+            compiler_params=PARAMS,
+        )(*operands)
+    )
 
 
 damping = 1.0
-block_pairs = [(leading, trailing) for leading in range(9) for trailing in range(leading, 9)]
 
 
 def inverse_small(matrix):
@@ -136,38 +750,13 @@
     )
 
 
-def point_update(coupling, point_inverse, point_gradient, gathered):
-    pulled = jnp.sum(coupling * gathered[:, None], axis=(0, 2))
-    return jnp.sum(point_inverse * (point_gradient - pulled)[None], axis=1)
-
-
-def conjugate(right_side, inverse_blocks, product, curvature_sum, energy_sum):
-    residual = right_side
-    conditioned = apply_blocks(inverse_blocks, residual)
-    direction = conditioned
-    energy_now = energy_sum(jnp.sum(residual * conditioned))
-    camera_step = jnp.zeros_like(right_side)
-    taken = []
-    for iteration in range(ITERS):
-        curved, spread = product(direction)
-        step_size = energy_now / curvature_sum(jnp.sum(direction * curved))
-        camera_step = camera_step + step_size * direction
-        taken.append((step_size, spread))
-        if iteration + 1 < ITERS:
-            residual = residual - step_size * curved
-            conditioned = apply_blocks(inverse_blocks, residual)
-            renewed = energy_sum(jnp.sum(residual * conditioned))
-            direction = conditioned + renewed / energy_now * direction
-            energy_now = renewed
-    return (camera_step, taken)
-
-
-def on_device(camera_jacobian, point_jacobian, residuals, observed_camera, track_length):
+def by_dense(camera_jacobian, point_jacobian, residuals, observed_camera, track_length):
     camera_blocks, errors, coupling, point_inverse, point_gradient = slot_basics(
         camera_jacobian, point_jacobian, residuals, track_length
     )
     tracks, points = observed_camera.shape
-    cameras = CAM_DEV * lax.axis_size("row") * lax.axis_size("col")
+    rows, cols = lax.axis_size("row"), lax.axis_size("col")
+    cameras = CAM_DEV * rows * cols
     flat_cameras = observed_camera.reshape(-1)
 
     def into_cameras(values):
@@ -181,38 +770,73 @@
         slot_rows = jnp.transpose(whole)[flat_cameras]
         return jnp.transpose(slot_rows).reshape(9, tracks, points)
 
+    def spread_out(value):
+        copies = jnp.broadcast_to(value[:, None], (9, OWNERS, CAM_DEV)).reshape(9, cameras)
+        return lax.all_to_all(copies, ("row", "col"), split_axis=1, concat_axis=1, tiled=True)
+
     term_values = camera_terms(
         camera_blocks, errors, coupling, point_inverse, point_gradient
     ).reshape(54, -1)
-    local_terms = into_cameras(term_values)
-    own_terms = lax.psum_scatter(local_terms, ("row", "col"), scatter_dimension=1, tiled=True)
+    local_terms = into_cameras(term_values).reshape(54, rows * cols, CAM_DEV)
+    own_terms = jnp.sum(
+        lax.all_to_all(local_terms, ("row", "col"), split_axis=1, concat_axis=1, tiled=True), axis=1
+    )
     inverse_blocks = block_inverse(assemble(own_terms[:45]))
     right_side = own_terms[45:]
 
-    def local_product(whole):
-        contrib = slot_product(camera_blocks, coupling, point_inverse, pick_slots(whole))
-        return into_cameras(contrib.reshape(9, -1))
-
-    def spread_out(value):
-        return lax.all_gather(value, ("row", "col"), axis=1, tiled=True)
-
-    def energy_sum(value):
-        return lax.psum(value, ("row", "col"))
-
-    def product(direction):
-        whole = spread_out(direction)
-        summed = lax.psum_scatter(
-            local_product(whole), ("row", "col"), scatter_dimension=1, tiled=True
-        )
-        return (damping * direction + summed, whole)
-
-    def curvature_sum(value):
-        return lax.psum(value, ("row", "col"))
-
-    camera_move, taken = conjugate(right_side, inverse_blocks, product, curvature_sum, energy_sum)
-    whole_move = lax.all_gather(camera_move, ("row", "col"), axis=1, tiled=True)
-    point_move = point_update(coupling, point_inverse, point_gradient, pick_slots(whole_move))
+    first = apply_blocks(inverse_blocks, right_side)
+    first_slots = pick_slots(spread_out(first))
+    first_pulled = jnp.sum(coupling * first_slots[:, None], axis=(0, 2))
+    contrib = slot_product(camera_blocks, coupling, point_inverse, first_slots)
+    local_image = into_cameras(contrib.reshape(9, -1)).reshape(9, OWNERS, CAM_DEV)
+    gathered_image = lax.all_to_all(
+        local_image, ("row", "col"), split_axis=1, concat_axis=1, tiled=True
+    )
+    first_image = damping * first + jnp.sum(gathered_image, axis=1)
+
+    second = apply_blocks(inverse_blocks, first_image)
+    second_slots = pick_slots(spread_out(second))
+    second_pulled = jnp.sum(coupling * second_slots[:, None], axis=(0, 2))
+    projected = jnp.sum(camera_blocks * second_slots[None], axis=1)
+    solved = jnp.sum(point_inverse * second_pulled[None], axis=1)
+    own_sums = jnp.stack(
+        [
+            jnp.sum(right_side * first),
+            jnp.sum(first * first_image),
+            jnp.sum(first_image * second),
+            jnp.sum(second * second)
+            + jnp.sum(projected * projected)
+            - jnp.sum(second_pulled * solved),
+        ]
+    )
+    spread = jnp.broadcast_to(own_sums[None], (OWNERS, 4))
+    energy, curvature, crossed, second_curvature = jnp.sum(exchange(spread), axis=0)
+    step_size = energy / curvature
+    renewed = step_size * step_size * crossed - energy
+    ratio = 1.0 + renewed / energy
+    second_step = renewed / (
+        ratio * ratio * curvature
+        - 2.0 * step_size * ratio * crossed
+        + step_size * step_size * second_curvature
+    )
+    first_weight = step_size + second_step * ratio
+    second_weight = -second_step * step_size
+    camera_move = first_weight * first + second_weight * second
+    pulled = first_weight * first_pulled + second_weight * second_pulled
+    point_move = jnp.sum(point_inverse * (point_gradient - pulled)[None], axis=1)
     return (camera_move, point_move)
+
+
+def on_device(camera_jacobian, point_jacobian, residuals, observed_camera, track_length):
+    operands = (camera_jacobian, point_jacobian, residuals, observed_camera, track_length)
+    overflow, kept = by_slots(*operands)
+    return lax.cond(
+        overflow > CAP,
+        lambda given, unused: by_dense(*given),
+        lambda unused, found: finish(*found),
+        operands,
+        kept,
+    )
 
 
 def solution(mesh):

time: 1490 us -> 117 us (0.08)
  waiting for transfers between devices: 853 us -> 8.43 us
  local copies, waits for them, and re-layouts: 245 us -> 1.74 us
  other arithmetic: 178 us -> 0 us
  blocking collectives: 191 us -> 72.4 us
  Pallas kernels: 0 us -> 28.8 us
  between operations: 18.8 us -> 1.37 us
    reduce_scatter x3 -> x0, waiting for transfers between devices: 633 us -> none  [the longest x2 412 us: product(): lax.psum_scatter(local_product(whole), ('row', 'col'), scatter_dimension=...]
    all_gather x3 -> x0, waiting for transfers between devices: 220 us -> none  [the longest x2 157 us: spread_out(): return lax.all_gather(value, ('row', 'col'), axis=1, tiled=True)]
    psum x3 -> x0, blocking collectives: 191 us -> none  [the longest x2 127 us: energy_sum(): return lax.psum(value, ('row', 'col'))]
    scatter-add x3 -> x0, other arithmetic: 163 us -> none  [into_cameras(): jnp.zeros((cameras, width), jnp.float32).at[flat_cameras]]
    gather x3 -> x0, local copies, waits for them, and re-layouts: 108 us -> none  [pick_slots(): slot_rows = jnp.transpose(whole)[flat_cameras]]
    all_to_all x0 -> x4, blocking collectives: none -> 72.4 us  [exchange(): lax.all_to_all(blocks, ('row', 'col'), split_axis=0, concat_axis=0, tiled...]
    scatter-add x3 -> x0, local copies, waits for them, and re-layouts: 48.5 us -> none  [into_cameras(): jnp.zeros((cameras, width), jnp.float32).at[flat_cameras]]
    transpose x3 -> x0, local copies, waits for them, and re-layouts: 29.5 us -> none  [the longest x2 26.7 us: pick_slots(): slot_rows = jnp.transpose(whole)[flat_cameras]]
  transfers between devices with their start and end apart: 6 -> 1, of which waited for: 6 -> 1; matrix products, arithmetic and copies ran while one was open for 0% -> 0% of each run, Pallas kernels for 0% -> 0%
where the time goes in v1:
time: 117 us
  blocking collectives  72.4 us (62%)
  Pallas kernels  28.8 us (25%)
  waiting for transfers between devices  8.43 us (7%)
  starting transfers between devices  4.22 us (4%)
  local copies, waits for them, and re-layouts  1.74 us (1%)
  between operations  1.37 us (1%)
    all_to_all x4, blocking collectives, exchange(): lax.all_to_all(blocks, ('row', 'col'), split_axis=0, concat_axis=0, tiled...  72.4 us
    pallas_call x6, Pallas kernels, call(): pl.pallas_call(kernel, out_shape=[jax.ShapeDtypeStruct(shape, dtype) for...  28.4 us
    all_to_all x1, waiting for transfers between devices, exchange(): lax.all_to_all(blocks, ('row', 'col'), split_axis=0, concat_axis=0, tiled...  8.43 us
    all_to_all x1, starting transfers between devices, exchange(): lax.all_to_all(blocks, ('row', 'col'), split_axis=0, concat_axis=0, tiled...  4.22 us
  transfers between devices with their start and end apart: 1, of which 1 were waited for; matrix products, arithmetic and copies ran while one was open for 0% of the time, Pallas kernels for 0%

profile of v1, /device:TPU:1, one launch (start us, length us, event | category | flops | bytes accessed | tf_op | source)
XLA Modules:
  0.0 117.2 jit_solution(8026478410836732299)
XLA Ops:
  0.6 0.0 copy-start.5
  0.6 0.0 copy-start
  0.7 0.0 copy-start.1
  0.7 0.0 copy-start.2
  0.7 3.1 %shard_map.72 = (f32[1344,128]{1,0:T(8,128)S(1)}, s32[64,128]{1,0:T(8,128)S(1)}, s32[16,1024]{1,0:T(8,128)S(1)}, f32[16,1024]{1,0:T(8,128)S(1)}, f32[24,1024]{1,0:T(8,128)S(1)}, /*index=5*/f32[128,128]{1,0:T(8,128)S(1)}) custom-call(f32[18,8,1024]{2,1,0:T(8,128)} %camera_ref.1, f32[6,8,1024]{2,1,0:T(8,128)} %point_ref.5, f32[2,8,1024]{2,1,0:T(8,128)} %error_ref.1, ...), custom_call_target="tpu_custom_call" | custom-call | tf_op jit(solution)/shard_map/pallas_call | solution.py:541
  3.7 10.1 %shard_map.73 = f32[1664,128]{1,0:T(8,128)S(1)} custom-call(s32[64,128]{1,0:T(8,128)S(1)} %get-tuple-element.57.code_ref, f32[1344,128]{1,0:T(8,128)S(1)} %get-tuple-element.58.pay_ref, f32[128,128]{1,0:T(8,128)S(1)} %get-tuple-element.59.flag_ref), custom_call_target="tpu_custom_call" | custom-call | tf_op jit(solution)/shard_map/pallas_call | solution.py:541
  13.9 27.9 %all_to_all.54 = f32[128,1,1664]{2,1,0:T(1,128)S(1)} all-to-all(f32[128,1,1664]{2,1,0:T(1,128)S(1)} %bitcast.727), channel_id=1, replica_groups=mesh['row'=8,'col'=16] {'row','col'}, dimensions={0} | all-to-all | bytes 1703936 | tf_op jit(solution)/shard_map/all_to_all | solution.py:553
  41.8 5.6 %shard_map.74 = (f32[1680,128]{1,0:T(8,128)S(1)}, f32[360,128]{1,0:T(8,128)S(1)}, f32[88,128]{1,0:T(8,128)S(1)}, f32[256,128]{1,0:T(8,128)S(1)}, f32[8,128]{1,0:T(8,128)S(1)}) custom-call(f32[1664,128]{1,0:T(8,128)S(1)} %bitcast.728), custom_call_target="tpu_custom_call" | custom-call | tf_op jit(solution)/shard_map/pallas_call | solution.py:541
  47.4 15.9 %all_to_all.55 = f32[128,1,256]{2,1,0:T(1,128)S(1)} all-to-all(f32[128,1,256]{2,1,0:T(1,128)S(1)} %bitcast.732), channel_id=1, replica_groups=mesh['row'=8,'col'=16] {'row','col'}, dimensions={0} | all-to-all | bytes 262144 | tf_op jit(solution)/shard_map/all_to_all | solution.py:553
  63.3 0.0 copy-done
  63.3 3.7 %shard_map.75 = (f32[8,1024]{1,0:T(8,128)S(1)}, f32[256,128]{1,0:T(8,128)S(1)}) custom-call(f32[256,128]{1,0:T(8,128)S(1)} %bitcast.731, s32[16,1024]{1,0:T(8,128)S(1)} %get-tuple-element.62.route_ref, f32[6,8,1024]{2,1,0:T(8,128)S(1)} %copy-done, s32[1,1024]{1,0:T(1,128)S(1)} %bitcast.799, f32[16,1024]{1,0:T(8,128)S(1)} %get-tuple-element.63.state_ref, ...), custom_call_target="tpu_custom_call" | custom-call | tf_op jit(solution)/shard_map/pallas_call | solution.py:541
  67.0 14.2 %all_to_all.56 = f32[128,1,256]{2,1,0:T(1,128)S(1)} all-to-all(f32[128,1,256]{2,1,0:T(1,128)S(1)} %bitcast.734), channel_id=1, replica_groups=mesh['row'=8,'col'=16] {'row','col'}, dimensions={0} | all-to-all | bytes 262144 | tf_op jit(solution)/shard_map/all_to_all | solution.py:553
  81.2 3.4 %shard_map.76 = (f32[72,128]{1,0:T(8,128)S(1)}, f32[256,128]{1,0:T(8,128)S(1)}) custom-call(f32[256,128]{1,0:T(8,128)S(1)} %bitcast.730, f32[1680,128]{1,0:T(8,128)S(1)} %get-tuple-element.66.feature_ref, f32[360,128]{1,0:T(8,128)S(1)} %get-tuple-element.67.factor_ref, f32[88,128]{1,0:T(8,128)S(1)} %get-tuple-element.68.first_ref), custom_call_target="tpu_custom_call" | custom-call | tf_op jit(solution)/shard_map/pallas_call | solution.py:541
  84.6 14.4 %all_to_all.57 = f32[128,1,256]{2,1,0:T(1,128)S(1)} all-to-all(f32[128,1,256]{2,1,0:T(1,128)S(1)} %bitcast.733), channel_id=1, replica_groups=mesh['row'=8,'col'=16] {'row','col'}, dimensions={0} | all-to-all | bytes 262144 | tf_op jit(solution)/shard_map/all_to_all | solution.py:553
  98.9 2.5 %shard_map.77 = (f32[8,1024]{1,0:T(8,128)S(1)}, f32[128,128]{1,0:T(8,128)}, f32[8,128]{1,0:T(8,128)S(1)}) custom-call(f32[256,128]{1,0:T(8,128)S(1)} %bitcast.729, s32[16,1024]{1,0:T(8,128)S(1)} %get-tuple-element.62.route_ref, f32[6,8,1024]{2,1,0:T(8,128)S(1)} %copy-done, s32[1,1024]{1,0:T(1,128)S(1)} %bitcast.800, ...), custom_call_target="tpu_custom_call" | custom-call | tf_op jit(solution)/shard_map/pallas_call | solution.py:541
  101.5 4.2 %all-to-all-start.9 = ((f32[128,1,128]{2,1,0:T(1,128)}), f32[128,1,128]{2,1,0:T(1,128)S(1)}, u32[]{:S(2)}, u32[]{:S(2)}) async-start(f32[128,1,128]{2,1,0:T(1,128)} %bitcast.125), calls=%async_computation.9 | async-start | bytes 131072 | tf_op jit(solution)/shard_map/all_to_all | solution.py:553
  105.7 0.5 slice.649
  106.9 8.4 %all-to-all-done.9 = f32[128,1,128]{2,1,0:T(1,128)S(1)} async-done(((f32[128,1,128]{2,1,0:T(1,128)}), f32[128,1,128]{2,1,0:T(1,128)S(1)}, u32[]{:S(2)}, u32[]{:S(2)}) %all-to-all-start.9) | async-done | bytes 65568 | tf_op jit(solution)/shard_map/all_to_all | solution.py:553
  115.3 0.0 copy-done.2
  115.3 0.7 conditional.1
  115.3 0.4 branch_0_fun.1
  116.0 0.0 copy-start.6
  116.0 0.6 copy-done.6
  116.6 0.6 copy-done.7
  (3 shorter events, 0.0 us)
Async XLA Ops:
  0.6 62.6 %copy-start.5 = (s32[1024]{0:T(1024)S(1)}, s32[1024]{0:T(1024)}, u32[]{:S(2)}) copy-start(s32[1024]{0:T(1024)} %param.11) | copy-start | bytes 12292
  0.6 62.6 %copy-start = (f32[6,8,1024]{2,1,0:T(8,128)S(1)}, f32[6,8,1024]{2,1,0:T(8,128)}, u32[]{:S(2)}) copy-start(f32[6,8,1024]{2,1,0:T(8,128)} %point_ref.5) | copy-start | bytes 589828
  0.7 114.7 %copy-start.1 = (f32[18,8,1024]{2,1,0:T(8,128)S(1)}, f32[18,8,1024]{2,1,0:T(8,128)}, u32[]{:S(2)}) copy-start(f32[18,8,1024]{2,1,0:T(8,128)} %camera_ref.1) | copy-start | bytes 1769476
  0.7 114.6 %copy-start.2 = (f32[2,8,1024]{2,1,0:T(8,128)S(1)}, f32[2,8,1024]{2,1,0:T(8,128)}, u32[]{:S(2)}) copy-start(f32[2,8,1024]{2,1,0:T(8,128)} %error_ref.1) | copy-start | bytes 196612
  101.5 13.8 %all-to-all-start.9 = ((f32[128,1,128]{2,1,0:T(1,128)}), f32[128,1,128]{2,1,0:T(1,128)S(1)}, u32[]{:S(2)}, u32[]{:S(2)}) async-start(f32[128,1,128]{2,1,0:T(1,128)} %bitcast.125), calls=%async_computation.9 | async-start | bytes 131072 | tf_op jit(solution)/shard_map/all_to_all | solution.py:553
  116.0 0.6 copy-start.6
  116.6 0.6 copy-start.7

commit v2 on v1

--- a/solution.py
+++ b/solution.py
@@ -69,7 +69,48 @@
     return [v00 * x + v01 * y + v02 * z, v01 * x + v11 * y + v12 * z, v02 * x + v12 * y + v22 * z]
 
 
-def prepare_kernel(camera_ref, point_ref, error_ref, index_ref, length_ref, pay_ref, code_ref, route_ref, state_ref, root_ref, flag_ref):
+def owner_of(camera):
+    return ((camera >> 7) * 171) >> 9
+
+
+def prepare_kernel(camera_in, point_in, error_in, index_ref, length_ref, pay_ref, code_ref, route_ref, state_ref, root_ref, flag_ref, camera_ref, point_ref, error_ref, camera_sem, point_sem, error_sem):
+    copies = [
+        pltpu.make_async_copy(camera_in, camera_ref, camera_sem),
+        pltpu.make_async_copy(point_in, point_ref, point_sem),
+        pltpu.make_async_copy(error_in, error_ref, error_sem),
+    ]
+    for copy in copies:
+        copy.start()
+    used = iota((TRACK, PT_DEV), 0) < length_ref[...]
+    route_ref[0:TRACK, :] = jnp.where(used, owner_of(index_ref[...]), OWNERS)
+
+    step = 256
+    upto = jnp.where(iota((step, step), 0) <= iota((step, step), 1), 1.0, 0.0).astype(BF16)
+    before = jnp.zeros((OWNERS, step), F32)
+    names = iota((OWNERS, step), 0)
+    for s in range(TRACK):
+        for chunk in range(PT_DEV // step):
+            lanes = slice(chunk * step, (chunk + 1) * step)
+            chosen = names == route_ref[s : s + 1, lanes]
+            hot = jnp.where(chosen, 1.0, 0.0).astype(BF16)
+            counts = dot(hot, upto)
+            rank = jnp.sum(jnp.where(chosen, counts + before, 0.0), axis=0, keepdims=True) - 1.0
+            before = before + jnp.broadcast_to(counts[:, step - 1 : step], (OWNERS, step))
+            route_ref[TRACK + s : TRACK + s + 1, lanes] = rank.astype(jnp.int32)
+
+    owner = route_ref[0:TRACK, :]
+    rank = route_ref[TRACK : 2 * TRACK, :]
+    fits = (owner < OWNERS) & (rank < CAP)
+    row_at = (rank * 171) >> 10
+    place = (rank - row_at * GROUPS) * (OWNERS * ROWS) + owner * ROWS + row_at
+    code = jnp.where(fits, place, GROUPS * OWNERS * ROWS)
+    for chunk in range(PT_DEV // LANES):
+        code_ref[chunk * TRACK : (chunk + 1) * TRACK, :] = code[:, chunk * LANES : (chunk + 1) * LANES]
+    most = jnp.max(jnp.max(before, axis=0, keepdims=True), axis=1, keepdims=True)
+    lane = iota((OWNERS, LANES), 1)
+    flag_ref[...] = jnp.where(lane > COUNT_AT, most, before[:, 0:LANES])
+    for copy in copies:
+        copy.wait()
     for chunk in range(PT_DEV // LANES):
         lanes = slice(chunk * LANES, (chunk + 1) * LANES)
         used = used_slots(length_ref, lanes)
@@ -102,7 +143,7 @@
             return left[0] * right[0] + left[1] * right[1] + left[2] * right[2]
 
         camera = index_ref[:, lanes]
-        owner = ((camera >> 7) * 171) >> 9
+        owner = owner_of(camera)
         local = camera - owner * CAM_DEV
         b01 = -along(u0, point[1])
         root0 = jnp.sqrt(1.0 - along(u0, point[0]))
@@ -119,35 +160,6 @@
         for f in range(WIDTH):
             at = (chunk * WIDTH + f) * TRACK
             pay_ref[at : at + TRACK, :] = values[f]
-        route_ref[0:TRACK, lanes] = jnp.where(used, owner, OWNERS)
-
-    step = 256
-    earlier = jnp.where(iota((step, step), 0) < iota((step, step), 1), 1.0, 0.0).astype(BF16)
-    everything = jnp.ones((step, step), BF16)
-    before = jnp.zeros((OWNERS, step), F32)
-    names = iota((OWNERS, step), 0)
-    for s in range(TRACK):
-        for chunk in range(PT_DEV // step):
-            lanes = slice(chunk * step, (chunk + 1) * step)
-            chosen = names == route_ref[s : s + 1, lanes]
-            hot = jnp.where(chosen, 1.0, 0.0).astype(BF16)
-            rank = jnp.sum(
-                jnp.where(chosen, dot(hot, earlier) + before, 0.0), axis=0, keepdims=True
-            )
-            before = before + dot(hot, everything)
-            route_ref[TRACK + s : TRACK + s + 1, lanes] = rank.astype(jnp.int32)
-
-    owner = route_ref[0:TRACK, :]
-    rank = route_ref[TRACK : 2 * TRACK, :]
-    fits = (owner < OWNERS) & (rank < CAP)
-    row_at = (rank * 171) >> 10
-    place = (rank - row_at * GROUPS) * (OWNERS * ROWS) + owner * ROWS + row_at
-    code = jnp.where(fits, place, GROUPS * OWNERS * ROWS)
-    for chunk in range(PT_DEV // LANES):
-        code_ref[chunk * TRACK : (chunk + 1) * TRACK, :] = code[:, chunk * LANES : (chunk + 1) * LANES]
-    most = jnp.max(jnp.max(before, axis=0, keepdims=True), axis=1, keepdims=True)
-    lane = iota((OWNERS, LANES), 1)
-    flag_ref[...] = jnp.where(lane > COUNT_AT, most, before[:, 0:LANES])
 
 
 def dispatch_kernel(code_ref, pay_ref, flag_ref, out_ref, slot_ref, block_ref):
@@ -376,21 +388,27 @@
     turn_out(image_ref, out_ref)
 
 
-def pull_slots(got_ref, route_ref, point_ref, length_ref, state_ref, root_ref, value_ref, pulled_ref, curve_ref, back):
+def either_span(flag_ref, work):
+    many = jnp.max(flag_ref[0:8, :]) > FEW
+    pl.when(many)(lambda: work(SPAN))
+    pl.when(jnp.logical_not(many))(lambda: work(FEW))
+
+
+def pull_slots(got_ref, route_ref, point_ref, length_ref, state_ref, root_ref, value_ref, pulled_ref, curve_ref, span, back):
     images = []
     for i in range(2):
-        images.append(turn_in(got_ref, i)[0:SPAN, :])
+        images.append(turn_in(got_ref, i)[0:span, :])
     high, low = two_parts(jnp.concatenate(images, axis=0))
     parts = jnp.concatenate([high, low], axis=1)
     owners = iota((OWNERS, PT_DEV), 0)
-    ranks = iota((SPAN, PT_DEV), 0)
+    ranks = iota((span, PT_DEV), 0)
     for s in range(TRACK):
         hot = jnp.where(owners == route_ref[s : s + 1, :], 1.0, 0.0).astype(BF16)
         got = dot(parts, jnp.concatenate([hot, hot], axis=0))
         here = ranks == route_ref[TRACK + s : TRACK + s + 1, :]
         for i in range(2):
             value_ref[i * TRACK + s : i * TRACK + s + 1, :] = jnp.sum(
-                jnp.where(here, got[i * SPAN : (i + 1) * SPAN, :], 0.0), axis=0, keepdims=True
+                jnp.where(here, got[i * span : (i + 1) * span, :], 0.0), axis=0, keepdims=True
             )
     curve = jnp.zeros((TRACK, LANES), F32)
     for chunk in range(PT_DEV // LANES):
@@ -419,29 +437,36 @@
         curve_ref[...] = curve
 
 
-def first_point_kernel(got_ref, route_ref, point_ref, length_ref, state_ref, root_ref, pulled_ref, out_ref, value_ref, image_ref):
-    pull_slots(got_ref, route_ref, point_ref, length_ref, state_ref, root_ref, value_ref, pulled_ref, None, True)
+def first_point_kernel(got_ref, route_ref, point_ref, length_ref, state_ref, root_ref, flag_ref, pulled_ref, out_ref, value_ref, image_ref):
+    image_ref[...] = jnp.zeros((2 * LANES, LANES), F32)
     owners = iota((OWNERS, PT_DEV), 0)
-    ranks = iota((SPAN, PT_DEV), 0)
-    sums = jnp.zeros((4 * SPAN, OWNERS), F32)
-    for s in range(TRACK):
-        hot = jnp.where(owners == route_ref[s : s + 1, :], 1.0, 0.0).astype(BF16)
-        here = ranks == route_ref[TRACK + s : TRACK + s + 1, :]
-        spread = []
+
+    def work(span):
+        pull_slots(got_ref, route_ref, point_ref, length_ref, state_ref, root_ref, value_ref, pulled_ref, None, span, True)
+        ranks = iota((span, PT_DEV), 0)
+        sums = jnp.zeros((4 * span, OWNERS), F32)
+        for s in range(TRACK):
+            hot = jnp.where(owners == route_ref[s : s + 1, :], 1.0, 0.0).astype(BF16)
+            here = ranks == route_ref[TRACK + s : TRACK + s + 1, :]
+            spread = []
+            for i in range(2):
+                value = value_ref[i * TRACK + s : i * TRACK + s + 1, :]
+                spread.append(jnp.where(here, value, 0.0))
+            high, low = two_parts(jnp.concatenate(spread, axis=0))
+            sums = sums + dot_lanes(jnp.concatenate([high, low], axis=0), hot)
+        sums = sums[0 : 2 * span] + sums[2 * span :]
         for i in range(2):
-            value = value_ref[i * TRACK + s : i * TRACK + s + 1, :]
-            spread.append(jnp.where(here, value, 0.0))
-        high, low = two_parts(jnp.concatenate(spread, axis=0))
-        sums = sums + dot_lanes(jnp.concatenate([high, low], axis=0), hot)
-    sums = sums[0 : 2 * SPAN] + sums[2 * SPAN :]
-    image_ref[...] = jnp.zeros((2 * LANES, LANES), F32)
-    for i in range(2):
-        image_ref[i * LANES : i * LANES + SPAN, :] = sums[i * SPAN : (i + 1) * SPAN, :]
+            image_ref[i * LANES : i * LANES + span, :] = sums[i * span : (i + 1) * span, :]
+
+    either_span(flag_ref, work)
     turn_out(image_ref, out_ref)
 
 
-def second_point_kernel(got_ref, route_ref, point_ref, length_ref, state_ref, root_ref, pulled_ref, out_ref, scalar_ref, value_ref, curve_ref):
-    pull_slots(got_ref, route_ref, point_ref, length_ref, state_ref, root_ref, value_ref, pulled_ref, curve_ref, False)
+def second_point_kernel(got_ref, route_ref, point_ref, length_ref, state_ref, root_ref, flag_ref, pulled_ref, out_ref, scalar_ref, value_ref, curve_ref):
+    def work(span):
+        pull_slots(got_ref, route_ref, point_ref, length_ref, state_ref, root_ref, value_ref, pulled_ref, curve_ref, span, False)
+
+    either_span(flag_ref, work)
     out_ref[...] = jnp.broadcast_to(total(curve_ref[...]), (OWNERS, LANES))
     scalar_ref[...] = jnp.broadcast_to(
         jnp.sum(got_ref[pl.ds(0, OWNERS, stride=2), :], axis=0, keepdims=True), (8, LANES)
@@ -496,7 +521,8 @@
     turn_out(image_ref, out_ref)
 
 
-def finish_kernel(curve_ref, scalar_ref, first_ref, second_ref, state_ref, first_pulled_ref, second_pulled_ref, camera_out, point_out, camera_ref, point_ref, camera_sem, point_sem):
+def finish_kernel(curve_ref, scalar_ref, first_ref, second_ref, state_ref, first_pulled_ref, second_pulled_ref, flag_ref, dense_camera_ref, dense_point_ref, camera_out, point_out, camera_ref, point_ref, camera_sem, point_sem):
+    over = flag_ref[0:1, 0:1] > CAP
     own = jnp.sum(curve_ref[...], axis=0, keepdims=True)[:, 0:1]
     energy, curvature, crossed, square = [
         scalar_ref[0:1, SPAN + at : SPAN + at + 1] for at in range(4)
@@ -512,10 +538,12 @@
     first_weight = step_size + second_step * ratio
     second_weight = -second_step * step_size
     for c in range(3):
-        camera_ref[:, c * LANES : (c + 1) * LANES] = (
+        moved = (
             first_weight * first_ref[pl.ds(c, 9, stride=8), :]
             + second_weight * second_ref[pl.ds(c, 9, stride=8), :]
         )
+        lanes = slice(c * LANES, (c + 1) * LANES)
+        camera_ref[:, lanes] = jnp.where(over, dense_camera_ref[:, lanes], moved)
     camera_copy = pltpu.make_async_copy(camera_ref, camera_out, camera_sem)
     camera_copy.start()
     left = [
@@ -526,7 +554,7 @@
     ]
     moved = times_inverse([state_ref[at : at + 1, :] for at in range(6)], left)
     for a in range(3):
-        point_ref[a : a + 1, :] = moved[a]
+        point_ref[a : a + 1, :] = jnp.where(over, dense_point_ref[a : a + 1, :], moved[a])
     point_copy = pltpu.make_async_copy(point_ref, point_out, point_sem)
     point_copy.start()
     camera_copy.wait()
@@ -556,19 +584,25 @@
 
 def by_slots(camera_jacobian, point_jacobian, residuals, observed_camera, track_length):
     lengths = track_length.reshape(1, PT_DEV)
-    pay, code, route, state, root, flag = call(
+    in_vmem = [pl.BlockSpec(memory_space=pltpu.VMEM)]
+    held = [(18, TRACK, PT_DEV), (6, TRACK, PT_DEV), (2, TRACK, PT_DEV)]
+    outs = [
+        ((WIDTH * PT_DEV * TRACK // LANES, LANES), F32),
+        ((BLOCKS, LANES), jnp.int32),
+        ((2 * TRACK, PT_DEV), jnp.int32),
+        ((16, PT_DEV), F32),
+        ((3 * TRACK, PT_DEV), F32),
+        ((OWNERS, LANES), F32),
+    ]
+    pay, code, route, state, root, flag = pl.pallas_call(
         prepare_kernel,
-        [
-            ((WIDTH * PT_DEV * TRACK // LANES, LANES), F32),
-            ((BLOCKS, LANES), jnp.int32),
-            ((2 * TRACK, PT_DEV), jnp.int32),
-            ((16, PT_DEV), F32),
-            ((3 * TRACK, PT_DEV), F32),
-            ((OWNERS, LANES), F32),
-        ],
-        [],
-        (camera_jacobian, point_jacobian, residuals, observed_camera, lengths),
-    )
+        out_shape=[jax.ShapeDtypeStruct(shape, dtype) for shape, dtype in outs],
+        in_specs=[pl.BlockSpec(memory_space=pl.ANY)] * 3 + in_vmem * 2,
+        out_specs=in_vmem * len(outs),
+        scratch_shapes=[pltpu.VMEM(shape, F32) for shape in held]
+        + [pltpu.SemaphoreType.DMA] * 3,
+        compiler_params=PARAMS,
+    )(camera_jacobian, point_jacobian, residuals, observed_camera, lengths)
     (sent,) = call(
         dispatch_kernel,
         [((OWNERS * ROWS, LANES), F32)],
@@ -590,7 +624,7 @@
         first_point_kernel,
         [((8, PT_DEV), F32), pair],
         [((2 * TRACK, PT_DEV), F32), image],
-        (exchange(out), route, point_jacobian, lengths, state, root),
+        (exchange(out), route, point_jacobian, lengths, state, root, flag),
     )
     second, out = call(
         second_camera_kernel,
@@ -602,9 +636,9 @@
         second_point_kernel,
         [((8, PT_DEV), F32), ((OWNERS, LANES), F32), ((8, LANES), F32)],
         [((2 * TRACK, PT_DEV), F32), ((TRACK, LANES), F32)],
-        (exchange(out), route, point_jacobian, lengths, state, root),
-    )
-    return overflow[0, 0], (exchange(curve), scalars, first, second, state, first_pulled, second_pulled)
+        (exchange(out), route, point_jacobian, lengths, state, root, flag),
+    )
+    return overflow, (exchange(curve), scalars, first, second, state, first_pulled, second_pulled)
 
 
 def finish(*operands):
@@ -830,13 +864,13 @@
 def on_device(camera_jacobian, point_jacobian, residuals, observed_camera, track_length):
     operands = (camera_jacobian, point_jacobian, residuals, observed_camera, track_length)
     overflow, kept = by_slots(*operands)
-    return lax.cond(
-        overflow > CAP,
-        lambda given, unused: by_dense(*given),
-        lambda unused, found: finish(*found),
-        operands,
-        kept,
-    )
+    dense = lax.cond(
+        overflow[0, 0] > CAP,
+        lambda *given: by_dense(*given),
+        lambda *given: (jnp.zeros((9, CAM_DEV), F32), jnp.zeros((3, PT_DEV), F32)),
+        *operands,
+    )
+    return finish(*kept, overflow, *dense)
 
 
 def solution(mesh):

time: 117 us -> 116 us (level)
  blocking collectives: 72.4 us -> 56.4 us
  waiting for transfers between devices: 8.43 us -> 16.6 us
  starting transfers between devices: 4.22 us -> 11.5 us
  local copies, waits for them, and re-layouts: 1.74 us -> 0.54 us
    all_to_all x4, blocking collectives: 72.4 us -> 56.4 us  [exchange(): lax.all_to_all(blocks, ('row', 'col'), split_axis=0, concat_axis=0, tiled...]
    all_to_all x1, waiting for transfers between devices: 8.43 us -> 16.6 us  [exchange(): lax.all_to_all(blocks, ('row', 'col'), split_axis=0, concat_axis=0, tiled...]
    all_to_all x1, starting transfers between devices: 4.22 us -> 11.5 us  [exchange(): lax.all_to_all(blocks, ('row', 'col'), split_axis=0, concat_axis=0, tiled...]
    pallas_call x6 -> x5, Pallas kernels: 28.4 us -> 25.1 us  [call(): pl.pallas_call(kernel, out_shape=[jax.ShapeDtypeStruct(shape, dtype) for...]
    pallas_call x0 -> x1, Pallas kernels: none -> 2.49 us  [by_slots(): pl.pallas_call(prepare_kernel, out_shape=[jax.ShapeDtypeStruct(shape, dty...]
    pallas_call x1, Pallas kernels: 0.43 us -> 1.65 us  [finish(): pl.pallas_call(finish_kernel, out_shape=[jax.ShapeDtypeStruct(shape, F32)...]
    unnamed x12 -> x8, local copies, waits for them, and re-layouts: 1.22 us -> 0.02 us
where the time goes in v2:
time: 116 us
  blocking collectives  56.4 us (49%)
  Pallas kernels  29.2 us (25%)
  waiting for transfers between devices  16.6 us (14%)
  starting transfers between devices  11.5 us (10%)
  between operations  1.57 us (1%)
    all_to_all x4, blocking collectives, exchange(): lax.all_to_all(blocks, ('row', 'col'), split_axis=0, concat_axis=0, tiled...  56.4 us
    pallas_call x5, Pallas kernels, call(): pl.pallas_call(kernel, out_shape=[jax.ShapeDtypeStruct(shape, dtype) for...  25.1 us
    all_to_all x1, waiting for transfers between devices, exchange(): lax.all_to_all(blocks, ('row', 'col'), split_axis=0, concat_axis=0, tiled...  16.6 us
    all_to_all x1, starting transfers between devices, exchange(): lax.all_to_all(blocks, ('row', 'col'), split_axis=0, concat_axis=0, tiled...  11.5 us
    pallas_call x1, Pallas kernels, by_slots(): pl.pallas_call(prepare_kernel, out_shape=[jax.ShapeDtypeStruct(shape, dty...  2.49 us
  transfers between devices with their start and end apart: 1, of which 1 were waited for; matrix products, arithmetic and copies ran while one was open for 0% of the time, Pallas kernels for 0%

profile of v2, /device:TPU:1, one launch (start us, length us, event | category | flops | bytes accessed | tf_op | source)
XLA Modules:
  0.0 116.1 jit_solution(1471041523006112554)
XLA Ops:
  0.6 0.0 copy-start.14
  0.6 0.0 copy-start
  0.7 0.0 copy-start.9
  0.7 2.5 %shard_map.68 = (f32[1344,128]{1,0:T(8,128)S(1)}, s32[64,128]{1,0:T(8,128)S(1)}, s32[16,1024]{1,0:T(8,128)S(1)}, f32[16,1024]{1,0:T(8,128)S(1)}, f32[24,1024]{1,0:T(8,128)S(1)}, /*index=5*/f32[128,128]{1,0:T(8,128)S(1)}) custom-call(f32[18,8,1024]{2,1,0:T(8,128)} %camera_in.1, f32[6,8,1024]{2,1,0:T(8,128)} %point_ref.3, f32[2,8,1024]{2,1,0:T(8,128)} %error_in.1, ...), custom_call_target="tpu_custom_call" | custom-call | tf_op jit(solution)/shard_map/pallas_call | solution.py:597
  3.2 11.0 %shard_map.69 = f32[1664,128]{1,0:T(8,128)} custom-call(s32[64,128]{1,0:T(8,128)S(1)} %get-tuple-element.37.code_ref, f32[1344,128]{1,0:T(8,128)S(1)} %get-tuple-element.38.pay_ref, f32[128,128]{1,0:T(8,128)S(1)} %get-tuple-element.39.flag_ref), custom_call_target="tpu_custom_call" | custom-call | tf_op jit(solution)/shard_map/pallas_call | solution.py:569
  14.2 11.5 %all-to-all-start.5 = ((f32[128,1,1664]{2,1,0:T(1,128)}), f32[128,1,1664]{2,1,0:T(1,128)S(1)}, u32[]{:S(2)}, u32[]{:S(2)}) async-start(f32[128,1,1664]{2,1,0:T(1,128)} %bitcast.113), calls=%async_computation.5 | async-start | bytes 1703936 | tf_op jit(solution)/shard_map/all_to_all | solution.py:581
  25.7 16.6 %all-to-all-done.5 = f32[128,1,1664]{2,1,0:T(1,128)S(1)} async-done(((f32[128,1,1664]{2,1,0:T(1,128)}), f32[128,1,1664]{2,1,0:T(1,128)S(1)}, u32[]{:S(2)}, u32[]{:S(2)}) %all-to-all-start.5) | async-done | bytes 852000 | tf_op jit(solution)/shard_map/all_to_all | solution.py:581
  42.3 5.6 %shard_map.70 = (f32[1680,128]{1,0:T(8,128)S(1)}, f32[360,128]{1,0:T(8,128)S(1)}, f32[88,128]{1,0:T(8,128)S(1)}, f32[256,128]{1,0:T(8,128)S(1)}, f32[8,128]{1,0:T(8,128)S(1)}) custom-call(f32[1664,128]{1,0:T(8,128)S(1)} %bitcast.726), custom_call_target="tpu_custom_call" | custom-call | tf_op jit(solution)/shard_map/pallas_call | solution.py:569
  47.9 0.5 slice.649
  49.1 0.0 copy-done.14
  49.1 0.0 copy-done
  49.1 0.0 copy-done.9
  49.1 0.3 conditional.1
  49.4 0.0 copy-start.13
  49.4 14.5 %all_to_all.54 = f32[128,1,256]{2,1,0:T(1,128)S(1)} all-to-all(f32[128,1,256]{2,1,0:T(1,128)S(1)} %bitcast.731), channel_id=1, replica_groups=mesh['row'=8,'col'=16] {'row','col'}, dimensions={0} | all-to-all | bytes 262144 | tf_op jit(solution)/shard_map/all_to_all | solution.py:581
  63.9 0.0 copy-done.13
  63.9 3.5 %shard_map.71 = (f32[8,1024]{1,0:T(8,128)S(1)}, f32[256,128]{1,0:T(8,128)S(1)}) custom-call(f32[256,128]{1,0:T(8,128)S(1)} %bitcast.729, s32[16,1024]{1,0:T(8,128)S(1)} %get-tuple-element.41.route_ref, f32[6,8,1024]{2,1,0:T(8,128)S(1)} %copy-done, s32[1,1024]{1,0:T(1,128)S(1)} %bitcast.798, f32[16,1024]{1,0:T(8,128)S(1)} %get-tuple-element.42.state_ref, ...), custom_call_target="tpu_custom_call" | custom-call | tf_op jit(solution)/shard_map/pallas_call | solution.py:569
  67.4 14.2 %all_to_all.55 = f32[128,1,256]{2,1,0:T(1,128)S(1)} all-to-all(f32[128,1,256]{2,1,0:T(1,128)S(1)} %bitcast.733), channel_id=1, replica_groups=mesh['row'=8,'col'=16] {'row','col'}, dimensions={0} | all-to-all | bytes 262144 | tf_op jit(solution)/shard_map/all_to_all | solution.py:581
  81.6 3.2 %shard_map.72 = (f32[72,128]{1,0:T(8,128)S(1)}, f32[256,128]{1,0:T(8,128)S(1)}) custom-call(f32[256,128]{1,0:T(8,128)S(1)} %bitcast.728, f32[1680,128]{1,0:T(8,128)S(1)} %get-tuple-element.45.feature_ref, f32[360,128]{1,0:T(8,128)S(1)} %get-tuple-element.46.factor_ref, f32[88,128]{1,0:T(8,128)S(1)} %get-tuple-element.47.first_ref), custom_call_target="tpu_custom_call" | custom-call | tf_op jit(solution)/shard_map/pallas_call | solution.py:569
  84.8 14.2 %all_to_all.56 = f32[128,1,256]{2,1,0:T(1,128)S(1)} all-to-all(f32[128,1,256]{2,1,0:T(1,128)S(1)} %bitcast.732), channel_id=1, replica_groups=mesh['row'=8,'col'=16] {'row','col'}, dimensions={0} | all-to-all | bytes 262144 | tf_op jit(solution)/shard_map/all_to_all | solution.py:581
  98.9 1.8 %shard_map.73 = (f32[8,1024]{1,0:T(8,128)S(1)}, f32[128,128]{1,0:T(8,128)S(1)}, f32[8,128]{1,0:T(8,128)S(1)}) custom-call(f32[256,128]{1,0:T(8,128)S(1)} %bitcast.727, s32[16,1024]{1,0:T(8,128)S(1)} %get-tuple-element.41.route_ref, f32[6,8,1024]{2,1,0:T(8,128)S(1)} %copy-done, s32[1,1024]{1,0:T(1,128)S(1)} %bitcast.799, ...), custom_call_target="tpu_custom_call" | custom-call | tf_op jit(solution)/shard_map/pallas_call | solution.py:569
  100.7 13.6 %all_to_all.57 = f32[128,1,128]{2,1,0:T(1,128)S(1)} all-to-all(f32[128,1,128]{2,1,0:T(1,128)S(1)} %bitcast.734), channel_id=1, replica_groups=mesh['row'=8,'col'=16] {'row','col'}, dimensions={0} | all-to-all | bytes 131072 | tf_op jit(solution)/shard_map/all_to_all | solution.py:581
  114.3 1.6 %shard_map.74 = (f32[9,384]{1,0:T(8,128)}, f32[3,1024]{1,0:T(4,128)}) custom-call(f32[128,128]{1,0:T(8,128)S(1)} %bitcast.730, f32[8,128]{1,0:T(8,128)S(1)} %get-tuple-element.50.scalar_ref, f32[88,128]{1,0:T(8,128)S(1)} %get-tuple-element.47.first_ref, f32[72,128]{1,0:T(8,128)S(1)} %get-tuple-element.51.second_ref, ...), custom_call_target="tpu_custom_call" | custom-call | tf_op jit(solution)/shard_map/pallas_call | solution.py:647
  (2 shorter events, 0.0 us)
Async XLA Ops:
  0.6 48.5 %copy-start.14 = (s32[1024]{0:T(1024)S(1)}, s32[1024]{0:T(1024)}, u32[]{:S(2)}) copy-start(s32[1024]{0:T(1024)} %param.11) | copy-start | bytes 12292
  0.6 48.5 %copy-start = (f32[6,8,1024]{2,1,0:T(8,128)S(1)}, f32[6,8,1024]{2,1,0:T(8,128)}, u32[]{:S(2)}) copy-start(f32[6,8,1024]{2,1,0:T(8,128)} %point_ref.3) | copy-start | bytes 589828
  0.7 48.5 %copy-start.9 = (f32[2,8,1024]{2,1,0:T(8,128)S(1)}, f32[2,8,1024]{2,1,0:T(8,128)}, u32[]{:S(2)}) copy-start(f32[2,8,1024]{2,1,0:T(8,128)} %error_in.1) | copy-start | bytes 196612
  14.2 28.1 %all-to-all-start.5 = ((f32[128,1,1664]{2,1,0:T(1,128)}), f32[128,1,1664]{2,1,0:T(1,128)S(1)}, u32[]{:S(2)}, u32[]{:S(2)}) async-start(f32[128,1,1664]{2,1,0:T(1,128)} %bitcast.113), calls=%async_computation.5 | async-start | bytes 1703936 | tf_op jit(solution)/shard_map/all_to_all | solution.py:581
  49.4 14.5 %copy-start.13 = (f32[9,384]{1,0:T(8,128)}, f32[9,384]{1,0:T(8,128)S(1)}, u32[]{:S(2)}) copy-start(f32[9,384]{1,0:T(8,128)S(1)} %get-tuple-element.55.dense_camera_ref) | copy-start | bytes 41476

commit v3 on v2

--- a/solution.py
+++ b/solution.py
@@ -168,12 +168,7 @@
     slots_ref = slot_ref.reshape(BLOCKS * LANES, LANES)
     blocks_ref = block_ref.reshape(GROUPS * rows + 8, LANES)
 
-    def clear(at, carry):
-        for j in range(16):
-            blocks_ref[pl.ds(pl.multiple_of(at * 128 + j * 8, 8), 8), :] = zeros
-        return carry
-
-    lax.fori_loop(0, GROUPS * rows // 128, clear, 0)
+    share = -(-GROUPS * rows // (BLOCKS * 8)) * 8
     within = iota((LANES, LANES), 1) % WIDTH
     for first in range(0, BLOCKS, GROUPS):
         blocks = []
@@ -188,14 +183,22 @@
             slots_ref[block * LANES : (block + 1) * LANES, :] = jnp.take_along_axis(
                 turned, within + (block - first) * WIDTH, axis=1, mode="promise_in_bounds"
             )
+            start = min(block * share, GROUPS * rows)
+            count = min(share, GROUPS * rows - start)
+            if count:
+                blocks_ref[start : start + count, :] = jnp.zeros((count, LANES), F32)
 
     def place(block, carry):
-        for start in range(0, LANES, 32):
-            columns = range(start, start + 32)
-            codes = [code_ref[block, j] for j in columns]
-            slots = [slot_ref[block, j] for j in columns]
-            for code, slot in zip(codes, slots):
+        def load(start):
+            columns = range(start, min(start + 16, LANES))
+            return [(code_ref[block, j], slot_ref[block, j]) for j in columns]
+
+        ready = load(0)
+        for start in range(16, LANES + 16, 16):
+            coming = load(start)
+            for code, slot in ready:
                 block_ref[code] = slot
+            ready = coming
         return carry
 
     lax.fori_loop(0, BLOCKS, place, 0)
@@ -521,8 +524,7 @@
     turn_out(image_ref, out_ref)
 
 
-def finish_kernel(curve_ref, scalar_ref, first_ref, second_ref, state_ref, first_pulled_ref, second_pulled_ref, flag_ref, dense_camera_ref, dense_point_ref, camera_out, point_out, camera_ref, point_ref, camera_sem, point_sem):
-    over = flag_ref[0:1, 0:1] > CAP
+def finish_kernel(curve_ref, scalar_ref, first_ref, second_ref, state_ref, first_pulled_ref, second_pulled_ref, camera_out, point_out, camera_ref, point_ref, camera_sem, point_sem):
     own = jnp.sum(curve_ref[...], axis=0, keepdims=True)[:, 0:1]
     energy, curvature, crossed, square = [
         scalar_ref[0:1, SPAN + at : SPAN + at + 1] for at in range(4)
@@ -538,12 +540,10 @@
     first_weight = step_size + second_step * ratio
     second_weight = -second_step * step_size
     for c in range(3):
-        moved = (
+        camera_ref[:, c * LANES : (c + 1) * LANES] = (
             first_weight * first_ref[pl.ds(c, 9, stride=8), :]
             + second_weight * second_ref[pl.ds(c, 9, stride=8), :]
         )
-        lanes = slice(c * LANES, (c + 1) * LANES)
-        camera_ref[:, lanes] = jnp.where(over, dense_camera_ref[:, lanes], moved)
     camera_copy = pltpu.make_async_copy(camera_ref, camera_out, camera_sem)
     camera_copy.start()
     left = [
@@ -554,7 +554,7 @@
     ]
     moved = times_inverse([state_ref[at : at + 1, :] for at in range(6)], left)
     for a in range(3):
-        point_ref[a : a + 1, :] = jnp.where(over, dense_point_ref[a : a + 1, :], moved[a])
+        point_ref[a : a + 1, :] = moved[a]
     point_copy = pltpu.make_async_copy(point_ref, point_out, point_sem)
     point_copy.start()
     camera_copy.wait()
@@ -638,7 +638,7 @@
         [((2 * TRACK, PT_DEV), F32), ((TRACK, LANES), F32)],
         (exchange(out), route, point_jacobian, lengths, state, root, flag),
     )
-    return overflow, (exchange(curve), scalars, first, second, state, first_pulled, second_pulled)
+    return overflow[0, 0], (exchange(curve), scalars, first, second, state, first_pulled, second_pulled)
 
 
 def finish(*operands):
@@ -864,13 +864,13 @@
 def on_device(camera_jacobian, point_jacobian, residuals, observed_camera, track_length):
     operands = (camera_jacobian, point_jacobian, residuals, observed_camera, track_length)
     overflow, kept = by_slots(*operands)
-    dense = lax.cond(
-        overflow[0, 0] > CAP,
-        lambda *given: by_dense(*given),
-        lambda *given: (jnp.zeros((9, CAM_DEV), F32), jnp.zeros((3, PT_DEV), F32)),
-        *operands,
-    )
-    return finish(*kept, overflow, *dense)
+    return lax.cond(
+        overflow > CAP,
+        lambda given, unused: by_dense(*given),
+        lambda unused, found: finish(*found),
+        operands,
+        kept,
+    )
 
 
 def solution(mesh):

time: 116 us -> 115 us (level)
  blocking collectives: 56.4 us -> 70.8 us
  waiting for transfers between devices: 16.6 us -> 8.43 us
  starting transfers between devices: 11.5 us -> 4.23 us
  Pallas kernels: 29.2 us -> 27.7 us
  local copies, waits for them, and re-layouts: 0.54 us -> 1.74 us
    all_to_all x4, blocking collectives: 56.4 us -> 70.8 us  [exchange(): lax.all_to_all(blocks, ('row', 'col'), split_axis=0, concat_axis=0, tiled...]
    all_to_all x1, waiting for transfers between devices: 16.6 us -> 8.43 us  [exchange(): lax.all_to_all(blocks, ('row', 'col'), split_axis=0, concat_axis=0, tiled...]
    all_to_all x1, starting transfers between devices: 11.5 us -> 4.23 us  [exchange(): lax.all_to_all(blocks, ('row', 'col'), split_axis=0, concat_axis=0, tiled...]
    pallas_call x1, Pallas kernels: 1.65 us -> 0.43 us  [finish(): pl.pallas_call(finish_kernel, out_shape=[jax.ShapeDtypeStruct(shape, F32)...]
    unnamed x8 -> x12, local copies, waits for them, and re-layouts: 0.02 us -> 1.22 us
where the time goes in v3:
time: 115 us
  blocking collectives  70.8 us (62%)
  Pallas kernels  27.7 us (24%)
  waiting for transfers between devices  8.43 us (7%)
  starting transfers between devices  4.23 us (4%)
  local copies, waits for them, and re-layouts  1.74 us (2%)
  between operations  1.39 us (1%)
    all_to_all x4, blocking collectives, exchange(): lax.all_to_all(blocks, ('row', 'col'), split_axis=0, concat_axis=0, tiled...  70.8 us
    pallas_call x5, Pallas kernels, call(): pl.pallas_call(kernel, out_shape=[jax.ShapeDtypeStruct(shape, dtype) for...  24.7 us
    all_to_all x1, waiting for transfers between devices, exchange(): lax.all_to_all(blocks, ('row', 'col'), split_axis=0, concat_axis=0, tiled...  8.43 us
    all_to_all x1, starting transfers between devices, exchange(): lax.all_to_all(blocks, ('row', 'col'), split_axis=0, concat_axis=0, tiled...  4.23 us
    pallas_call x1, Pallas kernels, by_slots(): pl.pallas_call(prepare_kernel, out_shape=[jax.ShapeDtypeStruct(shape, dty...  2.52 us
  transfers between devices with their start and end apart: 1, of which 1 were waited for; matrix products, arithmetic and copies ran while one was open for 0% of the time, Pallas kernels for 0%

profile of v3, /device:TPU:1, one launch (start us, length us, event | category | flops | bytes accessed | tf_op | source)
XLA Modules:
  0.0 114.5 jit_solution(8884387200201541953)
XLA Ops:
  0.6 0.0 copy-start.5
  0.6 0.0 copy-start
  0.7 0.0 copy-start.1
  0.7 0.0 copy-start.2
  0.7 2.5 %shard_map.72 = (f32[1344,128]{1,0:T(8,128)S(1)}, s32[64,128]{1,0:T(8,128)S(1)}, s32[16,1024]{1,0:T(8,128)S(1)}, f32[16,1024]{1,0:T(8,128)S(1)}, f32[24,1024]{1,0:T(8,128)S(1)}, /*index=5*/f32[128,128]{1,0:T(8,128)S(1)}) custom-call(f32[18,8,1024]{2,1,0:T(8,128)} %camera_in.1, f32[6,8,1024]{2,1,0:T(8,128)} %point_ref.3, f32[2,8,1024]{2,1,0:T(8,128)} %error_in.1, ...), custom_call_target="tpu_custom_call" | custom-call | tf_op jit(solution)/shard_map/pallas_call | solution.py:597
  3.2 9.9 %shard_map.73 = f32[1664,128]{1,0:T(8,128)S(1)} custom-call(s32[64,128]{1,0:T(8,128)S(1)} %get-tuple-element.57.code_ref, f32[1344,128]{1,0:T(8,128)S(1)} %get-tuple-element.58.pay_ref, f32[128,128]{1,0:T(8,128)S(1)} %get-tuple-element.59.flag_ref), custom_call_target="tpu_custom_call" | custom-call | tf_op jit(solution)/shard_map/pallas_call | solution.py:569
  13.1 27.9 %all_to_all.54 = f32[128,1,1664]{2,1,0:T(1,128)S(1)} all-to-all(f32[128,1,1664]{2,1,0:T(1,128)S(1)} %bitcast.727), channel_id=1, replica_groups=mesh['row'=8,'col'=16] {'row','col'}, dimensions={0} | all-to-all | bytes 1703936 | tf_op jit(solution)/shard_map/all_to_all | solution.py:581
  41.0 5.6 %shard_map.74 = (f32[1680,128]{1,0:T(8,128)S(1)}, f32[360,128]{1,0:T(8,128)S(1)}, f32[88,128]{1,0:T(8,128)S(1)}, f32[256,128]{1,0:T(8,128)S(1)}, f32[8,128]{1,0:T(8,128)S(1)}) custom-call(f32[1664,128]{1,0:T(8,128)S(1)} %bitcast.728), custom_call_target="tpu_custom_call" | custom-call | tf_op jit(solution)/shard_map/pallas_call | solution.py:569
  46.6 14.5 %all_to_all.55 = f32[128,1,256]{2,1,0:T(1,128)S(1)} all-to-all(f32[128,1,256]{2,1,0:T(1,128)S(1)} %bitcast.732), channel_id=1, replica_groups=mesh['row'=8,'col'=16] {'row','col'}, dimensions={0} | all-to-all | bytes 262144 | tf_op jit(solution)/shard_map/all_to_all | solution.py:581
  61.1 0.0 copy-done.5
  61.1 3.7 %shard_map.75 = (f32[8,1024]{1,0:T(8,128)S(1)}, f32[256,128]{1,0:T(8,128)S(1)}) custom-call(f32[256,128]{1,0:T(8,128)S(1)} %bitcast.731, s32[16,1024]{1,0:T(8,128)S(1)} %get-tuple-element.62.route_ref, f32[6,8,1024]{2,1,0:T(8,128)S(1)} %copy-done, s32[1,1024]{1,0:T(1,128)S(1)} %bitcast.799, f32[16,1024]{1,0:T(8,128)S(1)} %get-tuple-element.63.state_ref, ...), custom_call_target="tpu_custom_call" | custom-call | tf_op jit(solution)/shard_map/pallas_call | solution.py:569
  64.8 14.2 %all_to_all.56 = f32[128,1,256]{2,1,0:T(1,128)S(1)} all-to-all(f32[128,1,256]{2,1,0:T(1,128)S(1)} %bitcast.734), channel_id=1, replica_groups=mesh['row'=8,'col'=16] {'row','col'}, dimensions={0} | all-to-all | bytes 262144 | tf_op jit(solution)/shard_map/all_to_all | solution.py:581
  79.0 3.2 %shard_map.76 = (f32[72,128]{1,0:T(8,128)S(1)}, f32[256,128]{1,0:T(8,128)S(1)}) custom-call(f32[256,128]{1,0:T(8,128)S(1)} %bitcast.730, f32[1680,128]{1,0:T(8,128)S(1)} %get-tuple-element.66.feature_ref, f32[360,128]{1,0:T(8,128)S(1)} %get-tuple-element.67.factor_ref, f32[88,128]{1,0:T(8,128)S(1)} %get-tuple-element.68.first_ref), custom_call_target="tpu_custom_call" | custom-call | tf_op jit(solution)/shard_map/pallas_call | solution.py:569
  82.2 14.2 %all_to_all.57 = f32[128,1,256]{2,1,0:T(1,128)S(1)} all-to-all(f32[128,1,256]{2,1,0:T(1,128)S(1)} %bitcast.733), channel_id=1, replica_groups=mesh['row'=8,'col'=16] {'row','col'}, dimensions={0} | all-to-all | bytes 262144 | tf_op jit(solution)/shard_map/all_to_all | solution.py:581
  96.4 2.4 %shard_map.77 = (f32[8,1024]{1,0:T(8,128)S(1)}, f32[128,128]{1,0:T(8,128)}, f32[8,128]{1,0:T(8,128)S(1)}) custom-call(f32[256,128]{1,0:T(8,128)S(1)} %bitcast.729, s32[16,1024]{1,0:T(8,128)S(1)} %get-tuple-element.62.route_ref, f32[6,8,1024]{2,1,0:T(8,128)S(1)} %copy-done, s32[1,1024]{1,0:T(1,128)S(1)} %bitcast.800, ...), custom_call_target="tpu_custom_call" | custom-call | tf_op jit(solution)/shard_map/pallas_call | solution.py:569
  98.8 4.2 %all-to-all-start.9 = ((f32[128,1,128]{2,1,0:T(1,128)}), f32[128,1,128]{2,1,0:T(1,128)S(1)}, u32[]{:S(2)}, u32[]{:S(2)}) async-start(f32[128,1,128]{2,1,0:T(1,128)} %bitcast.125), calls=%async_computation.9 | async-start | bytes 131072 | tf_op jit(solution)/shard_map/all_to_all | solution.py:581
  103.0 0.5 slice.649
  104.2 8.4 %all-to-all-done.9 = f32[128,1,128]{2,1,0:T(1,128)S(1)} async-done(((f32[128,1,128]{2,1,0:T(1,128)}), f32[128,1,128]{2,1,0:T(1,128)S(1)}, u32[]{:S(2)}, u32[]{:S(2)}) %all-to-all-start.9) | async-done | bytes 65568 | tf_op jit(solution)/shard_map/all_to_all | solution.py:581
  112.6 0.0 copy-done.1
  112.6 0.7 conditional.1
  112.6 0.4 branch_0_fun.1
  113.3 0.0 copy-start.6
  113.3 0.6 copy-done.6
  113.9 0.6 copy-done.7
  (3 shorter events, 0.0 us)
Async XLA Ops:
  0.6 60.5 %copy-start.5 = (s32[1024]{0:T(1024)S(1)}, s32[1024]{0:T(1024)}, u32[]{:S(2)}) copy-start(s32[1024]{0:T(1024)} %param.11) | copy-start | bytes 12292
  0.6 60.5 %copy-start = (f32[6,8,1024]{2,1,0:T(8,128)S(1)}, f32[6,8,1024]{2,1,0:T(8,128)}, u32[]{:S(2)}) copy-start(f32[6,8,1024]{2,1,0:T(8,128)} %point_ref.3) | copy-start | bytes 589828
  0.7 111.9 %copy-start.1 = (f32[18,8,1024]{2,1,0:T(8,128)S(1)}, f32[18,8,1024]{2,1,0:T(8,128)}, u32[]{:S(2)}) copy-start(f32[18,8,1024]{2,1,0:T(8,128)} %camera_in.1) | copy-start | bytes 1769476
  0.7 111.9 %copy-start.2 = (f32[2,8,1024]{2,1,0:T(8,128)S(1)}, f32[2,8,1024]{2,1,0:T(8,128)}, u32[]{:S(2)}) copy-start(f32[2,8,1024]{2,1,0:T(8,128)} %error_in.1) | copy-start | bytes 196612
  98.8 13.8 %all-to-all-start.9 = ((f32[128,1,128]{2,1,0:T(1,128)}), f32[128,1,128]{2,1,0:T(1,128)S(1)}, u32[]{:S(2)}, u32[]{:S(2)}) async-start(f32[128,1,128]{2,1,0:T(1,128)} %bitcast.125), calls=%async_computation.9 | async-start | bytes 131072 | tf_op jit(solution)/shard_map/all_to_all | solution.py:581
  113.3 0.6 copy-start.6
  113.9 0.6 copy-start.7

commit v4 on v3

--- a/solution.py
+++ b/solution.py
@@ -73,7 +73,7 @@
     return ((camera >> 7) * 171) >> 9
 
 
-def prepare_kernel(camera_in, point_in, error_in, index_ref, length_ref, pay_ref, code_ref, route_ref, state_ref, root_ref, flag_ref, camera_ref, point_ref, error_ref, camera_sem, point_sem, error_sem):
+def prepare_kernel(camera_in, point_in, error_in, index_ref, length_ref, pay_ref, code_ref, route_ref, state_ref, root_ref, flag_ref, owned_ref, camera_ref, point_ref, error_ref, camera_sem, point_sem, error_sem):
     copies = [
         pltpu.make_async_copy(camera_in, camera_ref, camera_sem),
         pltpu.make_async_copy(point_in, point_ref, point_sem),
@@ -93,6 +93,7 @@
             lanes = slice(chunk * step, (chunk + 1) * step)
             chosen = names == route_ref[s : s + 1, lanes]
             hot = jnp.where(chosen, 1.0, 0.0).astype(BF16)
+            owned_ref[s, :, lanes] = hot
             counts = dot(hot, upto)
             rank = jnp.sum(jnp.where(chosen, counts + before, 0.0), axis=0, keepdims=True) - 1.0
             before = before + jnp.broadcast_to(counts[:, step - 1 : step], (OWNERS, step))
@@ -162,7 +163,9 @@
             pay_ref[at : at + TRACK, :] = values[f]
 
 
-def dispatch_kernel(code_ref, pay_ref, flag_ref, out_ref, slot_ref, block_ref):
+def dispatch_kernel(code_in, pay_ref, flag_ref, out_ref, code_ref, slot_ref, block_ref, code_sem):
+    copy = pltpu.make_async_copy(code_in, code_ref, code_sem)
+    copy.start()
     rows = OWNERS * ROWS
     zeros = jnp.zeros((8, LANES), F32)
     slots_ref = slot_ref.reshape(BLOCKS * LANES, LANES)
@@ -188,6 +191,8 @@
             if count:
                 blocks_ref[start : start + count, :] = jnp.zeros((count, LANES), F32)
 
+    copy.wait()
+
     def place(block, carry):
         def load(start):
             columns = range(start, min(start + 16, LANES))
@@ -240,11 +245,12 @@
     for r in range(8):
         camera = feature_ref[pl.ds(CAMERA_AT * SPAN + block * 8 + r, 1), :].astype(jnp.int32) - 1
         hot = jnp.where(names == (camera & (LANES - 1)), 1.0, 0.0).astype(BF16)
-        hot_ref[:, pl.ds(pl.multiple_of(block * PT_DEV + r * LANES, LANES), LANES)] = hot
+        hot_ref[:, block * PT_DEV + r * LANES : block * PT_DEV + (r + 1) * LANES] = hot
 
 
 def features_of(feature_ref, f, block):
-    return feature_ref[pl.ds(pl.multiple_of(f * SPAN + block * 8, 8), 8), :]
+    start = f * SPAN + block * 8
+    return feature_ref[pl.ds(start if isinstance(block, int) else pl.multiple_of(start, 8), 8), :]
 
 
 def image_slots(vector, feature_ref, table_ref, image_ref, blocks):
@@ -280,7 +286,7 @@
 
 def keep_parts(part_ref, feature_ref, parts_ref, block, count):
     for r in range(8):
-        lanes = pl.ds(pl.multiple_of(block * PT_DEV + r * LANES, LANES), LANES)
+        lanes = slice(block * PT_DEV + r * LANES, block * PT_DEV + (r + 1) * LANES)
         camera = feature_ref[pl.ds(CAMERA_AT * SPAN + block * 8 + r, 1), :].astype(jnp.int32) - 1
         value = part_ref[pl.ds(r, count, stride=8), :]
         high = value.astype(BF16).astype(F32)
@@ -292,13 +298,21 @@
             parts_ref[2 * c * count : 2 * (c + 1) * count, lanes] = both * inside
 
 
-def camera_sums(parts_ref, hot_ref, part_ref, sum_ref, count, many):
-    few = FEW * LANES
-    sum_ref[...] = dot_lanes(parts_ref[:, 0:few], hot_ref[:, 0:few])
+def camera_sums(terms, parts_ref, hot_ref, part_ref, sum_ref, count, many):
+    def block_sums(block):
+        terms(block)
+        lanes = slice(block * PT_DEV, (block + 1) * PT_DEV)
+        return dot_lanes(parts_ref[:, lanes], hot_ref[:, lanes])
+
+    sums = block_sums(0)
+    for block in range(1, FEW // 8):
+        sums = sums + block_sums(block)
+    sum_ref[...] = sums
 
     @pl.when(many)
     def _():
-        sum_ref[...] += dot_lanes(parts_ref[:, few:], hot_ref[:, few:])
+        for block in range(FEW // 8, SPAN // 8):
+            sum_ref[...] += block_sums(block)
 
     part_ref[...] = jnp.zeros(part_ref.shape, F32)
     for c in range(3):
@@ -332,9 +346,8 @@
         return turned
 
     turned = take_row(0)
-    flag_ref[...] = jnp.broadcast_to(
-        jnp.max(turned[COUNT_AT + 1 : COUNT_AT + 2, :], axis=1, keepdims=True), (8, LANES)
-    )
+    worst = jnp.max(turned[COUNT_AT + 1 : COUNT_AT + 2, :])
+    flag_ref[0, 0] = jnp.where(worst > CAP, 1, 0)
     most = jnp.max(turned[COUNT_AT : COUNT_AT + 1, :])
     many = most > FEW
     blocks = jnp.where(many, SPAN // 8, FEW // 8)
@@ -349,7 +362,7 @@
 
     part_ref[...] = jnp.zeros((ENTRIES * 8, LANES), F32)
 
-    def gather_terms(block, carry):
+    def gather_terms(block):
         hot_cameras(feature_ref, hot_ref, block)
         f = [features_of(feature_ref, at, block) for at in range(20)]
         for at, (j, k) in enumerate(block_pairs):
@@ -357,10 +370,8 @@
         for j in range(9):
             part_ref[(45 + j) * 8 : (46 + j) * 8, :] = -(f[j] * f[18] + f[9 + j] * f[19])
         keep_parts(part_ref, feature_ref, parts_ref, block, ENTRIES)
-        return carry
-
-    lax.fori_loop(0, blocks, gather_terms, 0)
-    camera_sums(parts_ref, hot_ref, part_ref, sum_ref, ENTRIES, many)
+
+    camera_sums(gather_terms, parts_ref, hot_ref, part_ref, sum_ref, ENTRIES, many)
     matrix = {}
     for at, (j, k) in enumerate(block_pairs):
         entry = part_ref[at * 8 : (at + 1) * 8, :]
@@ -397,16 +408,15 @@
     pl.when(jnp.logical_not(many))(lambda: work(FEW))
 
 
-def pull_slots(got_ref, route_ref, point_ref, length_ref, state_ref, root_ref, value_ref, pulled_ref, curve_ref, span, back):
+def pull_slots(got_ref, route_ref, point_ref, length_ref, state_ref, root_ref, owned_ref, value_ref, pulled_ref, curve_ref, span, back):
     images = []
     for i in range(2):
         images.append(turn_in(got_ref, i)[0:span, :])
     high, low = two_parts(jnp.concatenate(images, axis=0))
     parts = jnp.concatenate([high, low], axis=1)
-    owners = iota((OWNERS, PT_DEV), 0)
     ranks = iota((span, PT_DEV), 0)
     for s in range(TRACK):
-        hot = jnp.where(owners == route_ref[s : s + 1, :], 1.0, 0.0).astype(BF16)
+        hot = owned_ref[s]
         got = dot(parts, jnp.concatenate([hot, hot], axis=0))
         here = ranks == route_ref[TRACK + s : TRACK + s + 1, :]
         for i in range(2):
@@ -440,23 +450,21 @@
         curve_ref[...] = curve
 
 
-def first_point_kernel(got_ref, route_ref, point_ref, length_ref, state_ref, root_ref, flag_ref, pulled_ref, out_ref, value_ref, image_ref):
+def first_point_kernel(got_ref, route_ref, point_ref, length_ref, state_ref, root_ref, flag_ref, owned_ref, pulled_ref, out_ref, value_ref, image_ref):
     image_ref[...] = jnp.zeros((2 * LANES, LANES), F32)
-    owners = iota((OWNERS, PT_DEV), 0)
 
     def work(span):
-        pull_slots(got_ref, route_ref, point_ref, length_ref, state_ref, root_ref, value_ref, pulled_ref, None, span, True)
+        pull_slots(got_ref, route_ref, point_ref, length_ref, state_ref, root_ref, owned_ref, value_ref, pulled_ref, None, span, True)
         ranks = iota((span, PT_DEV), 0)
         sums = jnp.zeros((4 * span, OWNERS), F32)
         for s in range(TRACK):
-            hot = jnp.where(owners == route_ref[s : s + 1, :], 1.0, 0.0).astype(BF16)
             here = ranks == route_ref[TRACK + s : TRACK + s + 1, :]
             spread = []
             for i in range(2):
                 value = value_ref[i * TRACK + s : i * TRACK + s + 1, :]
                 spread.append(jnp.where(here, value, 0.0))
             high, low = two_parts(jnp.concatenate(spread, axis=0))
-            sums = sums + dot_lanes(jnp.concatenate([high, low], axis=0), hot)
+            sums = sums + dot_lanes(jnp.concatenate([high, low], axis=0), owned_ref[s])
         sums = sums[0 : 2 * span] + sums[2 * span :]
         for i in range(2):
             image_ref[i * LANES : i * LANES + span, :] = sums[i * span : (i + 1) * span, :]
@@ -465,9 +473,9 @@
     turn_out(image_ref, out_ref)
 
 
-def second_point_kernel(got_ref, route_ref, point_ref, length_ref, state_ref, root_ref, flag_ref, pulled_ref, out_ref, scalar_ref, value_ref, curve_ref):
+def second_point_kernel(got_ref, route_ref, point_ref, length_ref, state_ref, root_ref, flag_ref, owned_ref, pulled_ref, out_ref, scalar_ref, value_ref, curve_ref):
     def work(span):
-        pull_slots(got_ref, route_ref, point_ref, length_ref, state_ref, root_ref, value_ref, pulled_ref, curve_ref, span, False)
+        pull_slots(got_ref, route_ref, point_ref, length_ref, state_ref, root_ref, owned_ref, value_ref, pulled_ref, curve_ref, span, False)
 
     either_span(flag_ref, work)
     out_ref[...] = jnp.broadcast_to(total(curve_ref[...]), (OWNERS, LANES))
@@ -483,10 +491,10 @@
     blocks = jnp.where(many, SPAN // 8, FEW // 8)
     wide_ref[...] = jnp.zeros((LANES, LANES), F32)
 
-    def gather_terms(block, carry):
+    def gather_terms(block):
         hot_cameras(feature_ref, hot_ref, block)
         back = [
-            image_ref[pl.ds(pl.multiple_of(i * LANES + block * 8, 8), 8), :] for i in range(2)
+            image_ref[i * LANES + block * 8 : i * LANES + (block + 1) * 8, :] for i in range(2)
         ]
         for j in range(9):
             wide_ref[j * 8 : (j + 1) * 8, :] = (
@@ -494,10 +502,8 @@
                 + features_of(feature_ref, 9 + j, block) * back[1]
             )
         keep_parts(wide_ref, feature_ref, parts_ref, block, 16)
-        return carry
-
-    lax.fori_loop(0, blocks, gather_terms, 0)
-    camera_sums(parts_ref, hot_ref, wide_ref, sum_ref, 16, many)
+
+    camera_sums(gather_terms, parts_ref, hot_ref, wide_ref, sum_ref, 16, many)
     first = [first_ref[j * 8 : (j + 1) * 8, :] for j in range(9)]
     image = [first[j] + wide_ref[j * 8 : (j + 1) * 8, :] for j in range(9)]
     factor, roots = {}, []
@@ -570,7 +576,10 @@
         kernel,
         out_shape=[jax.ShapeDtypeStruct(shape, dtype) for shape, dtype in outs],
         in_specs=specs,
-        out_specs=[pl.BlockSpec(memory_space=pltpu.VMEM)] * len(outs),
+        out_specs=[
+            pl.BlockSpec(memory_space=pltpu.SMEM if shape == (1, 1) else pltpu.VMEM)
+            for shape, unused in outs
+        ],
         scratch_shapes=[pltpu.VMEM(shape, dtype) for shape, dtype in scratch],
         compiler_params=PARAMS,
     )(*operands)
@@ -593,8 +602,9 @@
         ((16, PT_DEV), F32),
         ((3 * TRACK, PT_DEV), F32),
         ((OWNERS, LANES), F32),
+        ((TRACK, OWNERS, PT_DEV), BF16),
     ]
-    pay, code, route, state, root, flag = pl.pallas_call(
+    pay, code, route, state, root, flag, owned = pl.pallas_call(
         prepare_kernel,
         out_shape=[jax.ShapeDtypeStruct(shape, dtype) for shape, dtype in outs],
         in_specs=[pl.BlockSpec(memory_space=pl.ANY)] * 3 + in_vmem * 2,
@@ -603,20 +613,26 @@
         + [pltpu.SemaphoreType.DMA] * 3,
         compiler_params=PARAMS,
     )(camera_jacobian, point_jacobian, residuals, observed_camera, lengths)
-    (sent,) = call(
+    sent = pl.pallas_call(
         dispatch_kernel,
-        [((OWNERS * ROWS, LANES), F32)],
-        [((BLOCKS, LANES, 1, LANES), F32), ((GROUPS * OWNERS * ROWS + 8, 1, LANES), F32)],
-        (code, pay, flag),
-        in_scalar=1,
-    )
+        out_shape=jax.ShapeDtypeStruct((OWNERS * ROWS, LANES), F32),
+        in_specs=in_vmem * 3,
+        out_specs=in_vmem[0],
+        scratch_shapes=[
+            pltpu.SMEM((BLOCKS, LANES), jnp.int32),
+            pltpu.VMEM((BLOCKS, LANES, 1, LANES), F32),
+            pltpu.VMEM((GROUPS * OWNERS * ROWS + 8, 1, LANES), F32),
+            pltpu.SemaphoreType.DMA,
+        ],
+        compiler_params=PARAMS,
+    )(code, pay, flag)
     hot = ((LANES, SPAN * LANES), BF16)
     table = ((27 * 8, LANES), F32)
     image = ((2 * LANES, LANES), F32)
     pair = ((2 * OWNERS, LANES), F32)
     features, factor, first, out, overflow = call(
         first_camera_kernel,
-        [((WIDTH * SPAN, LANES), F32), ((45 * 8, LANES), F32), ((88, LANES), F32), pair, ((8, LANES), F32)],
+        [((WIDTH * SPAN, LANES), F32), ((45 * 8, LANES), F32), ((88, LANES), F32), pair, ((1, 1), jnp.int32)],
         [hot, ((6 * ENTRIES, SPAN * LANES), BF16), table, image, ((6 * ENTRIES, LANES), F32), ((ENTRIES * 8, LANES), F32)],
         (exchange(sent),),
     )
@@ -624,7 +640,7 @@
         first_point_kernel,
         [((8, PT_DEV), F32), pair],
         [((2 * TRACK, PT_DEV), F32), image],
-        (exchange(out), route, point_jacobian, lengths, state, root, flag),
+        (exchange(out), route, point_jacobian, lengths, state, root, flag, owned),
     )
     second, out = call(
         second_camera_kernel,
@@ -636,7 +652,7 @@
         second_point_kernel,
         [((8, PT_DEV), F32), ((OWNERS, LANES), F32), ((8, LANES), F32)],
         [((2 * TRACK, PT_DEV), F32), ((TRACK, LANES), F32)],
-        (exchange(out), route, point_jacobian, lengths, state, root, flag),
+        (exchange(out), route, point_jacobian, lengths, state, root, flag, owned),
     )
     return overflow[0, 0], (exchange(curve), scalars, first, second, state, first_pulled, second_pulled)
 
@@ -865,7 +881,7 @@
     operands = (camera_jacobian, point_jacobian, residuals, observed_camera, track_length)
     overflow, kept = by_slots(*operands)
     return lax.cond(
-        overflow > CAP,
+        overflow > 0,
         lambda given, unused: by_dense(*given),
         lambda unused, found: finish(*found),
         operands,

time: 115 us -> 111 us (0.965)
  Pallas kernels: 27.7 us -> 24.3 us
    pallas_call x5 -> x4, Pallas kernels: 24.7 us -> 12.4 us  [call(): pl.pallas_call(kernel, out_shape=[jax.ShapeDtypeStruct(shape, dtype) for...]
    pallas_call x0 -> x1, Pallas kernels: none -> 8.82 us  [by_slots(): pl.pallas_call(dispatch_kernel, out_shape=jax.ShapeDtypeStruct((OWNERS *...]
where the time goes in v4:
time: 111 us
  blocking collectives  70.8 us (64%)
  Pallas kernels  24.3 us (22%)
  waiting for transfers between devices  8.95 us (8%)
  starting transfers between devices  4.22 us (4%)
  between operations  1.37 us (1%)
  local copies, waits for them, and re-layouts  1.22 us (1%)
    all_to_all x4, blocking collectives, exchange(): lax.all_to_all(blocks, ('row', 'col'), split_axis=0, concat_axis=0, tiled...  70.8 us
    pallas_call x4, Pallas kernels, call(): pl.pallas_call(kernel, out_shape=[jax.ShapeDtypeStruct(shape, dtype) for...  12.4 us
    all_to_all x1, waiting for transfers between devices, exchange(): lax.all_to_all(blocks, ('row', 'col'), split_axis=0, concat_axis=0, tiled...  8.95 us
    pallas_call x1, Pallas kernels, by_slots(): pl.pallas_call(dispatch_kernel, out_shape=jax.ShapeDtypeStruct((OWNERS *...  8.82 us
    all_to_all x1, starting transfers between devices, exchange(): lax.all_to_all(blocks, ('row', 'col'), split_axis=0, concat_axis=0, tiled...  4.22 us
    pallas_call x1, Pallas kernels, by_slots(): pl.pallas_call(prepare_kernel, out_shape=[jax.ShapeDtypeStruct(shape, dty...  2.7 us
  transfers between devices with their start and end apart: 1, of which 1 were waited for; matrix products, arithmetic and copies ran while one was open for 0% of the time, Pallas kernels for 0%

profile of v4, /device:TPU:1, one launch (start us, length us, event | category | flops | bytes accessed | tf_op | source)
XLA Modules:
  0.0 111.2 jit_solution(7214584852805971969)
XLA Ops:
  0.6 0.0 copy-start.5
  0.6 0.0 copy-start
  0.6 2.7 %shard_map.72 = (f32[1344,128]{1,0:T(8,128)S(1)}, s32[64,128]{1,0:T(8,128)S(1)}, s32[16,1024]{1,0:T(8,128)S(1)}, f32[16,1024]{1,0:T(8,128)S(1)}, f32[24,1024]{1,...) custom-call(f32[18,8,1024]{2,1,0:T(8,128)} %camera_in.1, f32[6,8,1024]{2,1,0:T(8,128)} %point_ref.3, ...), custom_call_target="tpu_custom_call" | custom-call | tf_op jit(solution)/shard_map/pallas_call | solution.py:607
  3.4 8.8 %shard_map.73 = f32[1664,128]{1,0:T(8,128)S(1)} custom-call(s32[64,128]{1,0:T(8,128)S(1)} %get-tuple-element.58.code_in, f32[1344,128]{1,0:T(8,128)S(1)} %get-tuple-element.59.pay_ref, f32[128,128]{1,0:T(8,128)S(1)} %get-tuple-element.60.flag_ref), custom_call_target="tpu_custom_call" | custom-call | tf_op jit(solution)/shard_map/pallas_call | solution.py:616
  12.2 27.9 %all_to_all.54 = f32[128,1,1664]{2,1,0:T(1,128)S(1)} all-to-all(f32[128,1,1664]{2,1,0:T(1,128)S(1)} %bitcast.727), channel_id=1, replica_groups=mesh['row'=8,'col'=16] {'row','col'}, dimensions={0} | all-to-all | bytes 1703936 | tf_op jit(solution)/shard_map/all_to_all | solution.py:590
  40.1 0.0 copy-start.1
  40.1 5.1 %shard_map.74 = (f32[1680,128]{1,0:T(8,128)S(1)}, f32[360,128]{1,0:T(8,128)S(1)}, f32[88,128]{1,0:T(8,128)S(1)}, f32[256,128]{1,0:T(8,128)S(1)}, s32[1,1]{1,0:T(1,128)}) custom-call(f32[1664,128]{1,0:T(8,128)S(1)} %bitcast.728), custom_call_target="tpu_custom_call" | custom-call | tf_op jit(solution)/shard_map/pallas_call | solution.py:575
  45.2 14.5 %all_to_all.55 = f32[128,1,256]{2,1,0:T(1,128)S(1)} all-to-all(f32[128,1,256]{2,1,0:T(1,128)S(1)} %bitcast.732), channel_id=1, replica_groups=mesh['row'=8,'col'=16] {'row','col'}, dimensions={0} | all-to-all | bytes 262144 | tf_op jit(solution)/shard_map/all_to_all | solution.py:590
  59.7 0.0 copy-done.5
  59.7 0.0 copy-done
  59.7 2.7 %shard_map.75 = (f32[8,1024]{1,0:T(8,128)S(1)}, f32[256,128]{1,0:T(8,128)S(1)}) custom-call(f32[256,128]{1,0:T(8,128)S(1)} %bitcast.731, s32[16,1024]{1,0:T(8,128)S(1)} %get-tuple-element.63.route_ref, f32[6,8,1024]{2,1,0:T(8,128)S(1)} %copy-done, s32[1,1024]{1,0:T(1,128)S(1)} %bitcast.799, f32[16,1024]{1,0:T(8,128)S(1)} %get-tuple-element.64.state_ref, ...), custom_call_target="tpu_custom_call" | custom-call | tf_op jit(solution)/shard_map/pallas_call | solution.py:575
  62.4 14.2 %all_to_all.56 = f32[128,1,256]{2,1,0:T(1,128)S(1)} all-to-all(f32[128,1,256]{2,1,0:T(1,128)S(1)} %bitcast.734), channel_id=1, replica_groups=mesh['row'=8,'col'=16] {'row','col'}, dimensions={0} | all-to-all | bytes 262144 | tf_op jit(solution)/shard_map/all_to_all | solution.py:590
  76.6 2.7 %shard_map.76 = (f32[72,128]{1,0:T(8,128)S(1)}, f32[256,128]{1,0:T(8,128)S(1)}) custom-call(f32[256,128]{1,0:T(8,128)S(1)} %bitcast.729, f32[1680,128]{1,0:T(8,128)S(1)} %get-tuple-element.68.feature_ref, f32[360,128]{1,0:T(8,128)S(1)} %get-tuple-element.69.factor_ref, f32[88,128]{1,0:T(8,128)S(1)} %get-tuple-element.70.first_ref), custom_call_target="tpu_custom_call" | custom-call | tf_op jit(solution)/shard_map/pallas_call | solution.py:575
  79.3 14.2 %all_to_all.57 = f32[128,1,256]{2,1,0:T(1,128)S(1)} all-to-all(f32[128,1,256]{2,1,0:T(1,128)S(1)} %bitcast.733), channel_id=1, replica_groups=mesh['row'=8,'col'=16] {'row','col'}, dimensions={0} | all-to-all | bytes 262144 | tf_op jit(solution)/shard_map/all_to_all | solution.py:590
  93.5 1.9 %shard_map.77 = (f32[8,1024]{1,0:T(8,128)S(1)}, f32[128,128]{1,0:T(8,128)}, f32[8,128]{1,0:T(8,128)S(1)}) custom-call(f32[256,128]{1,0:T(8,128)S(1)} %bitcast.730, s32[16,1024]{1,0:T(8,128)S(1)} %get-tuple-element.63.route_ref, f32[6,8,1024]{2,1,0:T(8,128)S(1)} %copy-done, s32[1,1024]{1,0:T(1,128)S(1)} %bitcast.800, ...), custom_call_target="tpu_custom_call" | custom-call | tf_op jit(solution)/shard_map/pallas_call | solution.py:575
  95.4 4.2 %all-to-all-start.9 = ((f32[128,1,128]{2,1,0:T(1,128)}), f32[128,1,128]{2,1,0:T(1,128)S(1)}, u32[]{:S(2)}, u32[]{:S(2)}) async-start(f32[128,1,128]{2,1,0:T(1,128)} %bitcast.125), calls=%async_computation.9 | async-start | bytes 131072 | tf_op jit(solution)/shard_map/all_to_all | solution.py:590
  100.3 9.0 %all-to-all-done.9 = f32[128,1,128]{2,1,0:T(1,128)S(1)} async-done(((f32[128,1,128]{2,1,0:T(1,128)}), f32[128,1,128]{2,1,0:T(1,128)S(1)}, u32[]{:S(2)}, u32[]{:S(2)}) %all-to-all-start.9) | async-done | bytes 65568 | tf_op jit(solution)/shard_map/all_to_all | solution.py:590
  109.2 0.0 copy-done.1
  109.2 0.0 copy-done.2
  109.2 0.7 conditional.1
  109.2 0.4 branch_0_fun.1
  109.9 0.0 copy-start.6
  110.0 0.6 copy-done.6
  110.6 0.6 copy-done.7
  (2 shorter events, 0.0 us)
Async XLA Ops:
  0.6 59.1 %copy-start.5 = (s32[1024]{0:T(1024)S(1)}, s32[1024]{0:T(1024)}, u32[]{:S(2)}) copy-start(s32[1024]{0:T(1024)} %param.11) | copy-start | bytes 12292
  0.6 59.1 %copy-start = (f32[6,8,1024]{2,1,0:T(8,128)S(1)}, f32[6,8,1024]{2,1,0:T(8,128)}, u32[]{:S(2)}) copy-start(f32[6,8,1024]{2,1,0:T(8,128)} %point_ref.3) | copy-start | bytes 589828
  40.1 69.1 %copy-start.1 = (f32[18,8,1024]{2,1,0:T(8,128)S(1)}, f32[18,8,1024]{2,1,0:T(8,128)}, u32[]{:S(2)}) copy-start(f32[18,8,1024]{2,1,0:T(8,128)} %camera_in.1) | copy-start | bytes 1769476
  40.1 69.1 %copy-start.2 = (f32[2,8,1024]{2,1,0:T(8,128)S(1)}, f32[2,8,1024]{2,1,0:T(8,128)}, u32[]{:S(2)}) copy-start(f32[2,8,1024]{2,1,0:T(8,128)} %error_in.1) | copy-start | bytes 196612
  95.4 13.8 %all-to-all-start.9 = ((f32[128,1,128]{2,1,0:T(1,128)}), f32[128,1,128]{2,1,0:T(1,128)S(1)}, u32[]{:S(2)}, u32[]{:S(2)}) async-start(f32[128,1,128]{2,1,0:T(1,128)} %bitcast.125), calls=%async_computation.9 | async-start | bytes 131072 | tf_op jit(solution)/shard_map/all_to_all | solution.py:590
  109.9 0.6 copy-start.6
  110.6 0.6 copy-start.7

commit v5 on v4

--- a/solution.py
+++ b/solution.py
@@ -73,7 +73,7 @@
     return ((camera >> 7) * 171) >> 9
 
 
-def prepare_kernel(camera_in, point_in, error_in, index_ref, length_ref, pay_ref, code_ref, route_ref, state_ref, root_ref, flag_ref, owned_ref, camera_ref, point_ref, error_ref, camera_sem, point_sem, error_sem):
+def prepare_kernel(camera_in, point_in, error_in, index_ref, length_ref, out_ref, route_ref, state_ref, root_ref, flag_ref, owned_ref, camera_ref, point_ref, error_ref, pay_ref, code_ref, near_ref, slot_ref, block_ref, camera_sem, point_sem, error_sem, code_sem):
     copies = [
         pltpu.make_async_copy(camera_in, camera_ref, camera_sem),
         pltpu.make_async_copy(point_in, point_ref, point_sem),
@@ -107,6 +107,8 @@
     code = jnp.where(fits, place, GROUPS * OWNERS * ROWS)
     for chunk in range(PT_DEV // LANES):
         code_ref[chunk * TRACK : (chunk + 1) * TRACK, :] = code[:, chunk * LANES : (chunk + 1) * LANES]
+    code_copy = pltpu.make_async_copy(code_ref, near_ref, code_sem)
+    code_copy.start()
     most = jnp.max(jnp.max(before, axis=0, keepdims=True), axis=1, keepdims=True)
     lane = iota((OWNERS, LANES), 1)
     flag_ref[...] = jnp.where(lane > COUNT_AT, most, before[:, 0:LANES])
@@ -130,7 +132,8 @@
         c12 = s02 * s01 - s12 * s00
         c22 = s00 * s11 - s01 * s01
         determinant = s00 * c00 + s01 * c01 + s02 * c02
-        inverse = [c / determinant for c in (c00, c01, c02, c11, c12, c22)]
+        scale = 1.0 / determinant
+        inverse = [c * scale for c in (c00, c01, c02, c11, c12, c22)]
         gradient = [
             -over_tracks(point[0][a] * error[0] + point[1][a] * error[1]) for a in range(3)
         ]
@@ -161,11 +164,10 @@
         for f in range(WIDTH):
             at = (chunk * WIDTH + f) * TRACK
             pay_ref[at : at + TRACK, :] = values[f]
-
-
-def dispatch_kernel(code_in, pay_ref, flag_ref, out_ref, code_ref, slot_ref, block_ref, code_sem):
-    copy = pltpu.make_async_copy(code_in, code_ref, code_sem)
-    copy.start()
+    dispatch(near_ref, pay_ref, flag_ref, out_ref, slot_ref, block_ref, code_copy)
+
+
+def dispatch(code_ref, pay_ref, flag_ref, out_ref, slot_ref, block_ref, code_copy):
     rows = OWNERS * ROWS
     zeros = jnp.zeros((8, LANES), F32)
     slots_ref = slot_ref.reshape(BLOCKS * LANES, LANES)
@@ -191,7 +193,7 @@
             if count:
                 blocks_ref[start : start + count, :] = jnp.zeros((count, LANES), F32)
 
-    copy.wait()
+    code_copy.wait()
 
     def place(block, carry):
         def load(start):
@@ -224,19 +226,19 @@
     out_ref[leading, :] = jnp.where(lane >= COUNT_AT, flag_ref[...], out_ref[leading, :])
 
 
-def solve(factor, roots, vector):
+def solve(factor, scales, vector):
     forward = []
     for i in range(9):
         value = vector[i]
         for j in range(i):
             value = value - factor[i, j] * forward[j]
-        forward.append(value / roots[i])
+        forward.append(value * scales[i])
     result = [None] * 9
     for i in reversed(range(9)):
         value = forward[i]
         for j in range(i + 1, 9):
             value = value - factor[j, i] * result[j]
-        result[i] = value / roots[i]
+        result[i] = value * scales[i]
     return result
 
 
@@ -250,16 +252,16 @@
 
 def features_of(feature_ref, f, block):
     start = f * SPAN + block * 8
-    return feature_ref[pl.ds(start if isinstance(block, int) else pl.multiple_of(start, 8), 8), :]
-
-
-def image_slots(vector, feature_ref, table_ref, image_ref, blocks):
+    return feature_ref[start : start + 8, :]
+
+
+def image_slots(vector, feature_ref, table_ref, image_ref, many):
     for j in range(9):
         for c in range(3):
             at = (3 * j + c) * 8
             table_ref[at : at + 8, :] = jnp.broadcast_to(vector[j][c : c + 1, :], (8, LANES))
 
-    def one(block, carry):
+    def one(block):
         camera = features_of(feature_ref, CAMERA_AT, block).astype(jnp.int32) - 1
         third = camera >> 7
         lane = camera & (LANES - 1)
@@ -278,10 +280,16 @@
             for i in range(2):
                 images[i] = images[i] + features_of(feature_ref, 9 * i + j, block) * value
         for i in range(2):
-            image_ref[pl.ds(pl.multiple_of(i * LANES + block * 8, 8), 8), :] = images[i]
-        return carry
-
-    lax.fori_loop(0, blocks, one, 0)
+            start = i * LANES + block * 8
+            image_ref[start : start + 8, :] = images[i]
+
+    for block in range(FEW // 8):
+        one(block)
+
+    @pl.when(many)
+    def _():
+        for block in range(FEW // 8, SPAN // 8):
+            one(block)
 
 
 def keep_parts(part_ref, feature_ref, parts_ref, block, count):
@@ -350,7 +358,6 @@
     flag_ref[0, 0] = jnp.where(worst > CAP, 1, 0)
     most = jnp.max(turned[COUNT_AT : COUNT_AT + 1, :])
     many = most > FEW
-    blocks = jnp.where(many, SPAN // 8, FEW // 8)
     few_rows = -(-FEW // GROUPS)
     for q in range(1, few_rows):
         take_row(q)
@@ -377,20 +384,20 @@
         entry = part_ref[at * 8 : (at + 1) * 8, :]
         matrix[k, j] = entry + 1.0 if j == k else entry
     side = [part_ref[(45 + j) * 8 : (46 + j) * 8, :] for j in range(9)]
-    factor, roots = {}, []
+    factor, scales = {}, []
     for j in range(9):
         pivot = matrix[j, j]
         for m in range(j):
             pivot = pivot - factor[j, m] * factor[j, m]
-        roots.append(jnp.sqrt(pivot))
+        scales.append(1.0 / jnp.sqrt(pivot))
         for i in range(j + 1, 9):
             running = matrix[i, j]
             for m in range(j):
                 running = running - factor[i, m] * factor[j, m]
-            factor[i, j] = running / roots[j]
+            factor[i, j] = running * scales[j]
     for at, (j, k) in enumerate(block_pairs):
-        factor_ref[at * 8 : (at + 1) * 8, :] = roots[j] if j == k else factor[k, j]
-    first = solve(factor, roots, side)
+        factor_ref[at * 8 : (at + 1) * 8, :] = scales[j] if j == k else factor[k, j]
+    first = solve(factor, scales, side)
     energy = side[0] * first[0]
     for j in range(1, 9):
         energy = energy + side[j] * first[j]
@@ -398,7 +405,7 @@
         first_ref[j * 8 : (j + 1) * 8, :] = first[j]
     first_ref[72:80, :] = energy
     first_ref[80:88, :] = jnp.broadcast_to(jnp.max(turned[COUNT_AT : COUNT_AT + 1, :], axis=1, keepdims=True), (8, LANES))
-    image_slots(first, feature_ref, table_ref, image_ref, blocks)
+    image_slots(first, feature_ref, table_ref, image_ref, many)
     turn_out(image_ref, out_ref)
 
 
@@ -488,7 +495,6 @@
     for i in range(2):
         image_ref[i * LANES : (i + 1) * LANES, :] = turn_in(got_ref, i)
     many = jnp.max(first_ref[80:88, :]) > FEW
-    blocks = jnp.where(many, SPAN // 8, FEW // 8)
     wide_ref[...] = jnp.zeros((LANES, LANES), F32)
 
     def gather_terms(block):
@@ -506,14 +512,14 @@
     camera_sums(gather_terms, parts_ref, hot_ref, wide_ref, sum_ref, 16, many)
     first = [first_ref[j * 8 : (j + 1) * 8, :] for j in range(9)]
     image = [first[j] + wide_ref[j * 8 : (j + 1) * 8, :] for j in range(9)]
-    factor, roots = {}, []
+    factor, scales = {}, []
     for at, (j, k) in enumerate(block_pairs):
         entry = factor_ref[at * 8 : (at + 1) * 8, :]
         if j == k:
-            roots.append(entry)
+            scales.append(entry)
         else:
             factor[k, j] = entry
-    second = solve(factor, roots, image)
+    second = solve(factor, scales, image)
     for j in range(9):
         second_ref[j * 8 : (j + 1) * 8, :] = second[j]
 
@@ -523,7 +529,7 @@
             value = value + left[j] * right[j]
         return value
 
-    image_slots(second, feature_ref, table_ref, image_ref, blocks)
+    image_slots(second, feature_ref, table_ref, image_ref, many)
     scalars = [first_ref[72:80, :], inner(first, image), inner(image, second), inner(second, second)]
     for at, value in enumerate(scalars):
         image_ref[SPAN + at : SPAN + at + 1, :] = jnp.broadcast_to(total(value), (1, LANES))
@@ -596,36 +602,29 @@
     in_vmem = [pl.BlockSpec(memory_space=pltpu.VMEM)]
     held = [(18, TRACK, PT_DEV), (6, TRACK, PT_DEV), (2, TRACK, PT_DEV)]
     outs = [
-        ((WIDTH * PT_DEV * TRACK // LANES, LANES), F32),
-        ((BLOCKS, LANES), jnp.int32),
+        ((OWNERS * ROWS, LANES), F32),
         ((2 * TRACK, PT_DEV), jnp.int32),
         ((16, PT_DEV), F32),
         ((3 * TRACK, PT_DEV), F32),
         ((OWNERS, LANES), F32),
         ((TRACK, OWNERS, PT_DEV), BF16),
     ]
-    pay, code, route, state, root, flag, owned = pl.pallas_call(
+    sent, route, state, root, flag, owned = pl.pallas_call(
         prepare_kernel,
         out_shape=[jax.ShapeDtypeStruct(shape, dtype) for shape, dtype in outs],
         in_specs=[pl.BlockSpec(memory_space=pl.ANY)] * 3 + in_vmem * 2,
         out_specs=in_vmem * len(outs),
         scratch_shapes=[pltpu.VMEM(shape, F32) for shape in held]
-        + [pltpu.SemaphoreType.DMA] * 3,
-        compiler_params=PARAMS,
-    )(camera_jacobian, point_jacobian, residuals, observed_camera, lengths)
-    sent = pl.pallas_call(
-        dispatch_kernel,
-        out_shape=jax.ShapeDtypeStruct((OWNERS * ROWS, LANES), F32),
-        in_specs=in_vmem * 3,
-        out_specs=in_vmem[0],
-        scratch_shapes=[
+        + [
+            pltpu.VMEM((WIDTH * BLOCKS, LANES), F32),
+            pltpu.VMEM((BLOCKS, LANES), jnp.int32),
             pltpu.SMEM((BLOCKS, LANES), jnp.int32),
             pltpu.VMEM((BLOCKS, LANES, 1, LANES), F32),
             pltpu.VMEM((GROUPS * OWNERS * ROWS + 8, 1, LANES), F32),
-            pltpu.SemaphoreType.DMA,
-        ],
+        ]
+        + [pltpu.SemaphoreType.DMA] * 4,
         compiler_params=PARAMS,
-    )(code, pay, flag)
+    )(camera_jacobian, point_jacobian, residuals, observed_camera, lengths)
     hot = ((LANES, SPAN * LANES), BF16)
     table = ((27 * 8, LANES), F32)
     image = ((2 * LANES, LANES), F32)

time: 111 us -> 112 us (level)
    pallas_call x1, Pallas kernels: 2.7 us -> 11.6 us  [by_slots(): pl.pallas_call(prepare_kernel, out_shape=[jax.ShapeDtypeStruct(shape, dty...]
    pallas_call x1 -> x0, Pallas kernels: 8.82 us -> none  [by_slots(): pl.pallas_call(dispatch_kernel, out_shape=jax.ShapeDtypeStruct((OWNERS *...]
where the time goes in v5:
time: 112 us; the launch traced here: 111 us
  blocking collectives  70.8 us (63%)
  Pallas kernels  24.5 us (22%)
  waiting for transfers between devices  8.95 us (8%)
  starting transfers between devices  4.22 us (4%)
  between operations  1.36 us (1%)
  local copies, waits for them, and re-layouts  1.23 us (1%)
    all_to_all x4, blocking collectives, exchange(): lax.all_to_all(blocks, ('row', 'col'), split_axis=0, concat_axis=0, tiled...  70.8 us
    pallas_call x4, Pallas kernels, call(): pl.pallas_call(kernel, out_shape=[jax.ShapeDtypeStruct(shape, dtype) for...  12.4 us
    pallas_call x1, Pallas kernels, by_slots(): pl.pallas_call(prepare_kernel, out_shape=[jax.ShapeDtypeStruct(shape, dty...  11.6 us
    all_to_all x1, waiting for transfers between devices, exchange(): lax.all_to_all(blocks, ('row', 'col'), split_axis=0, concat_axis=0, tiled...  8.95 us
    all_to_all x1, starting transfers between devices, exchange(): lax.all_to_all(blocks, ('row', 'col'), split_axis=0, concat_axis=0, tiled...  4.22 us
  transfers between devices with their start and end apart: 1, of which 1 were waited for; matrix products, arithmetic and copies ran while one was open for 0% of the time, Pallas kernels for 0%

profile of v5, /device:TPU:1, one launch (start us, length us, event | category | flops | bytes accessed | tf_op | source)
XLA Modules:
  0.0 111.3 jit_solution(17093792267555105416)
XLA Ops:
  0.6 0.0 copy-start.5
  0.6 0.0 copy-start
  0.7 11.6 %shard_map.72 = (f32[1664,128]{1,0:T(8,128)S(1)}, s32[16,1024]{1,0:T(8,128)S(1)}, f32[16,1024]{1,0:T(8,128)S(1)}, f32[24,1024]{1,0:T(8,128)S(1)}, f32[128,128]{1...) custom-call(f32[18,8,1024]{2,1,0:T(8,128)} %camera_in.1, f32[6,8,1024]{2,1,0:T(8,128)} %point_ref.3, f32[2,8,1024]{2,1,0:T(8,128)} %error_in.1, ...), custom_call_target="tpu_custom_call" | custom-call | tf_op jit(solution)/shard_map/pallas_call | solution.py:612
  12.3 27.9 %all_to_all.54 = f32[128,1,1664]{2,1,0:T(1,128)S(1)} all-to-all(f32[128,1,1664]{2,1,0:T(1,128)S(1)} %bitcast.728), channel_id=1, replica_groups=mesh['row'=8,'col'=16] {'row','col'}, dimensions={0} | all-to-all | bytes 1703936 | tf_op jit(solution)/shard_map/all_to_all | solution.py:596
  40.2 0.0 copy-start.1
  40.2 0.0 copy-start.2
  40.2 4.7 %shard_map.73 = (f32[1680,128]{1,0:T(8,128)S(1)}, f32[360,128]{1,0:T(8,128)S(1)}, f32[88,128]{1,0:T(8,128)S(1)}, f32[256,128]{1,0:T(8,128)S(1)}, s32[1,1]{1,0:T(1,128)}) custom-call(f32[1664,128]{1,0:T(8,128)S(1)} %bitcast.727), custom_call_target="tpu_custom_call" | custom-call | tf_op jit(solution)/shard_map/pallas_call | solution.py:581
  45.0 14.5 %all_to_all.55 = f32[128,1,256]{2,1,0:T(1,128)S(1)} all-to-all(f32[128,1,256]{2,1,0:T(1,128)S(1)} %bitcast.732), channel_id=1, replica_groups=mesh['row'=8,'col'=16] {'row','col'}, dimensions={0} | all-to-all | bytes 262144 | tf_op jit(solution)/shard_map/all_to_all | solution.py:596
  59.5 3.6 %shard_map.74 = (f32[8,1024]{1,0:T(8,128)S(1)}, f32[256,128]{1,0:T(8,128)S(1)}) custom-call(f32[256,128]{1,0:T(8,128)S(1)} %bitcast.731, s32[16,1024]{1,0:T(8,128)S(1)} %get-tuple-element.60.route_ref, f32[6,8,1024]{2,1,0:T(8,128)} %point_ref.3, s32[1,1024]{1,0:T(1,128)} %bitcast.799, f32[16,1024]{1,0:T(8,128)S(1)} %get-tuple-element.61.state_ref, ...), custom_call_target="tpu_custom_call" | custom-call | tf_op jit(solution)/shard_map/pallas_call | solution.py:581
  63.1 14.2 %all_to_all.56 = f32[128,1,256]{2,1,0:T(1,128)S(1)} all-to-all(f32[128,1,256]{2,1,0:T(1,128)S(1)} %bitcast.734), channel_id=1, replica_groups=mesh['row'=8,'col'=16] {'row','col'}, dimensions={0} | all-to-all | bytes 262144 | tf_op jit(solution)/shard_map/all_to_all | solution.py:596
  77.3 2.2 %shard_map.75 = (f32[72,128]{1,0:T(8,128)S(1)}, f32[256,128]{1,0:T(8,128)S(1)}) custom-call(f32[256,128]{1,0:T(8,128)S(1)} %bitcast.729, f32[1680,128]{1,0:T(8,128)S(1)} %get-tuple-element.66.feature_ref, f32[360,128]{1,0:T(8,128)S(1)} %get-tuple-element.67.factor_ref, f32[88,128]{1,0:T(8,128)S(1)} %get-tuple-element.68.first_ref), custom_call_target="tpu_custom_call" | custom-call | tf_op jit(solution)/shard_map/pallas_call | solution.py:581
  79.5 14.2 %all_to_all.57 = f32[128,1,256]{2,1,0:T(1,128)S(1)} all-to-all(f32[128,1,256]{2,1,0:T(1,128)S(1)} %bitcast.733), channel_id=1, replica_groups=mesh['row'=8,'col'=16] {'row','col'}, dimensions={0} | all-to-all | bytes 262144 | tf_op jit(solution)/shard_map/all_to_all | solution.py:596
  93.6 0.0 copy-done.5
  93.6 0.0 copy-done
  93.6 1.9 %shard_map.76 = (f32[8,1024]{1,0:T(8,128)S(1)}, f32[128,128]{1,0:T(8,128)}, f32[8,128]{1,0:T(8,128)S(1)}) custom-call(f32[256,128]{1,0:T(8,128)S(1)} %bitcast.730, s32[16,1024]{1,0:T(8,128)S(1)} %get-tuple-element.60.route_ref, f32[6,8,1024]{2,1,0:T(8,128)S(1)} %copy-done, s32[1,1024]{1,0:T(1,128)S(1)} %bitcast.800, ...), custom_call_target="tpu_custom_call" | custom-call | tf_op jit(solution)/shard_map/pallas_call | solution.py:581
  95.5 4.2 %all-to-all-start.9 = ((f32[128,1,128]{2,1,0:T(1,128)}), f32[128,1,128]{2,1,0:T(1,128)S(1)}, u32[]{:S(2)}, u32[]{:S(2)}) async-start(f32[128,1,128]{2,1,0:T(1,128)} %bitcast.125), calls=%async_computation.9 | async-start | bytes 131072 | tf_op jit(solution)/shard_map/all_to_all | solution.py:596
  100.4 8.9 %all-to-all-done.9 = f32[128,1,128]{2,1,0:T(1,128)S(1)} async-done(((f32[128,1,128]{2,1,0:T(1,128)}), f32[128,1,128]{2,1,0:T(1,128)S(1)}, u32[]{:S(2)}, u32[]{:S(2)}) %all-to-all-start.9) | async-done | bytes 65568 | tf_op jit(solution)/shard_map/all_to_all | solution.py:596
  109.3 0.0 copy-done.1
  109.3 0.0 copy-done.2
  109.3 0.7 conditional.1
  109.3 0.4 branch_0_fun.1
  110.0 0.0 copy-start.6
  110.1 0.6 copy-done.6
  110.7 0.6 copy-done.7
  (1 shorter events, 0.0 us)
Async XLA Ops:
  0.6 93.0 %copy-start.5 = (s32[1024]{0:T(1024)S(1)}, s32[1024]{0:T(1024)}, u32[]{:S(2)}) copy-start(s32[1024]{0:T(1024)} %param.11) | copy-start | bytes 12292
  0.6 93.0 %copy-start = (f32[6,8,1024]{2,1,0:T(8,128)S(1)}, f32[6,8,1024]{2,1,0:T(8,128)}, u32[]{:S(2)}) copy-start(f32[6,8,1024]{2,1,0:T(8,128)} %point_ref.3) | copy-start | bytes 589828
  40.2 69.1 %copy-start.1 = (f32[18,8,1024]{2,1,0:T(8,128)S(1)}, f32[18,8,1024]{2,1,0:T(8,128)}, u32[]{:S(2)}) copy-start(f32[18,8,1024]{2,1,0:T(8,128)} %camera_in.1) | copy-start | bytes 1769476
  40.2 69.1 %copy-start.2 = (f32[2,8,1024]{2,1,0:T(8,128)S(1)}, f32[2,8,1024]{2,1,0:T(8,128)}, u32[]{:S(2)}) copy-start(f32[2,8,1024]{2,1,0:T(8,128)} %error_in.1) | copy-start | bytes 196612
  95.5 13.8 %all-to-all-start.9 = ((f32[128,1,128]{2,1,0:T(1,128)}), f32[128,1,128]{2,1,0:T(1,128)S(1)}, u32[]{:S(2)}, u32[]{:S(2)}) async-start(f32[128,1,128]{2,1,0:T(1,128)} %bitcast.125), calls=%async_computation.9 | async-start | bytes 131072 | tf_op jit(solution)/shard_map/all_to_all | solution.py:596
  110.0 0.6 copy-start.6
  110.7 0.6 copy-start.7

commit v6 on v5

--- a/solution.py
+++ b/solution.py
@@ -57,12 +57,6 @@
     return iota((TRACK, LANES), 0) < length_ref[:, lanes]
 
 
-def masked_points(point_ref, used, lanes):
-    return [
-        [jnp.where(used, point_ref[3 * i + a, :, lanes], 0.0) for a in range(3)] for i in range(2)
-    ]
-
-
 def times_inverse(inverse, vector):
     v00, v01, v02, v11, v12, v22 = inverse
     x, y, z = vector
@@ -73,7 +67,7 @@
     return ((camera >> 7) * 171) >> 9
 
 
-def prepare_kernel(camera_in, point_in, error_in, index_ref, length_ref, out_ref, route_ref, state_ref, root_ref, flag_ref, owned_ref, camera_ref, point_ref, error_ref, pay_ref, code_ref, near_ref, slot_ref, block_ref, camera_sem, point_sem, error_sem, code_sem):
+def prepare_kernel(camera_in, point_in, error_in, index_ref, length_ref, out_ref, route_ref, state_ref, root_ref, flag_ref, owned_ref, masked_ref, camera_ref, point_ref, error_ref, pay_ref, code_ref, near_ref, slot_ref, block_ref, camera_sem, point_sem, error_sem, code_sem):
     copies = [
         pltpu.make_async_copy(camera_in, camera_ref, camera_sem),
         pltpu.make_async_copy(point_in, point_ref, point_sem),
@@ -117,7 +111,12 @@
     for chunk in range(PT_DEV // LANES):
         lanes = slice(chunk * LANES, (chunk + 1) * LANES)
         used = used_slots(length_ref, lanes)
-        point = masked_points(point_ref, used, lanes)
+        point = [
+            [jnp.where(used, point_ref[3 * i + a, :, lanes], 0.0) for a in range(3)] for i in range(2)
+        ]
+        for i in range(2):
+            for a in range(3):
+                masked_ref[3 * i + a, :, lanes] = point[i][a]
         error = [jnp.where(used, error_ref[i, :, lanes], 0.0) for i in range(2)]
 
         def pair(a, b):
@@ -415,7 +414,7 @@
     pl.when(jnp.logical_not(many))(lambda: work(FEW))
 
 
-def pull_slots(got_ref, route_ref, point_ref, length_ref, state_ref, root_ref, owned_ref, value_ref, pulled_ref, curve_ref, span, back):
+def pull_slots(got_ref, route_ref, masked_ref, state_ref, root_ref, owned_ref, value_ref, pulled_ref, curve_ref, span, back):
     images = []
     for i in range(2):
         images.append(turn_in(got_ref, i)[0:span, :])
@@ -433,8 +432,7 @@
     curve = jnp.zeros((TRACK, LANES), F32)
     for chunk in range(PT_DEV // LANES):
         lanes = slice(chunk * LANES, (chunk + 1) * LANES)
-        used = used_slots(length_ref, lanes)
-        point = masked_points(point_ref, used, lanes)
+        point = [[masked_ref[3 * i + a, :, lanes] for a in range(3)] for i in range(2)]
         root = [root_ref[at * TRACK : (at + 1) * TRACK, lanes] for at in range(3)]
         image1 = value_ref[TRACK : 2 * TRACK, lanes] * root[2]
         image = [(value_ref[0:TRACK, lanes] - root[1] * image1) * root[0], image1]
@@ -457,11 +455,11 @@
         curve_ref[...] = curve
 
 
-def first_point_kernel(got_ref, route_ref, point_ref, length_ref, state_ref, root_ref, flag_ref, owned_ref, pulled_ref, out_ref, value_ref, image_ref):
+def first_point_kernel(got_ref, route_ref, masked_ref, state_ref, root_ref, flag_ref, owned_ref, pulled_ref, out_ref, value_ref, image_ref):
     image_ref[...] = jnp.zeros((2 * LANES, LANES), F32)
 
     def work(span):
-        pull_slots(got_ref, route_ref, point_ref, length_ref, state_ref, root_ref, owned_ref, value_ref, pulled_ref, None, span, True)
+        pull_slots(got_ref, route_ref, masked_ref, state_ref, root_ref, owned_ref, value_ref, pulled_ref, None, span, True)
         ranks = iota((span, PT_DEV), 0)
         sums = jnp.zeros((4 * span, OWNERS), F32)
         for s in range(TRACK):
@@ -480,9 +478,9 @@
     turn_out(image_ref, out_ref)
 
 
-def second_point_kernel(got_ref, route_ref, point_ref, length_ref, state_ref, root_ref, flag_ref, owned_ref, pulled_ref, out_ref, scalar_ref, value_ref, curve_ref):
+def second_point_kernel(got_ref, route_ref, masked_ref, state_ref, root_ref, flag_ref, owned_ref, pulled_ref, out_ref, scalar_ref, value_ref, curve_ref):
     def work(span):
-        pull_slots(got_ref, route_ref, point_ref, length_ref, state_ref, root_ref, owned_ref, value_ref, pulled_ref, curve_ref, span, False)
+        pull_slots(got_ref, route_ref, masked_ref, state_ref, root_ref, owned_ref, value_ref, pulled_ref, curve_ref, span, False)
 
     either_span(flag_ref, work)
     out_ref[...] = jnp.broadcast_to(total(curve_ref[...]), (OWNERS, LANES))
@@ -608,8 +606,9 @@
         ((3 * TRACK, PT_DEV), F32),
         ((OWNERS, LANES), F32),
         ((TRACK, OWNERS, PT_DEV), BF16),
+        ((6, TRACK, PT_DEV), F32),
     ]
-    sent, route, state, root, flag, owned = pl.pallas_call(
+    sent, route, state, root, flag, owned, masked = pl.pallas_call(
         prepare_kernel,
         out_shape=[jax.ShapeDtypeStruct(shape, dtype) for shape, dtype in outs],
         in_specs=[pl.BlockSpec(memory_space=pl.ANY)] * 3 + in_vmem * 2,
@@ -639,7 +638,7 @@
         first_point_kernel,
         [((8, PT_DEV), F32), pair],
         [((2 * TRACK, PT_DEV), F32), image],
-        (exchange(out), route, point_jacobian, lengths, state, root, flag, owned),
+        (exchange(out), route, masked, state, root, flag, owned),
     )
     second, out = call(
         second_camera_kernel,
@@ -651,7 +650,7 @@
         second_point_kernel,
         [((8, PT_DEV), F32), ((OWNERS, LANES), F32), ((8, LANES), F32)],
         [((2 * TRACK, PT_DEV), F32), ((TRACK, LANES), F32)],
-        (exchange(out), route, point_jacobian, lengths, state, root, flag, owned),
+        (exchange(out), route, masked, state, root, flag, owned),
     )
     return overflow[0, 0], (exchange(curve), scalars, first, second, state, first_pulled, second_pulled)
 

time: 112 us -> 111 us (level); the launches traced: 111 us -> 112 us
  blocking collectives: 70.8 us -> 72.3 us
    all_to_all x4, blocking collectives: 70.8 us -> 72.3 us  [exchange(): lax.all_to_all(blocks, ('row', 'col'), split_axis=0, concat_axis=0, tiled...]
where the time goes in v6:
time: 111 us; the launch traced here: 112 us
  blocking collectives  72.3 us (65%)
  Pallas kernels  23.5 us (21%)
  waiting for transfers between devices  8.95 us (8%)
  starting transfers between devices  4.22 us (4%)
  between operations  1.35 us (1%)
  local copies, waits for them, and re-layouts  1.22 us (1%)
    all_to_all x4, blocking collectives, exchange(): lax.all_to_all(blocks, ('row', 'col'), split_axis=0, concat_axis=0, tiled...  72.3 us
    pallas_call x1, Pallas kernels, by_slots(): pl.pallas_call(prepare_kernel, out_shape=[jax.ShapeDtypeStruct(shape, dty...  11.6 us
    pallas_call x4, Pallas kernels, call(): pl.pallas_call(kernel, out_shape=[jax.ShapeDtypeStruct(shape, dtype) for...  11.5 us
    all_to_all x1, waiting for transfers between devices, exchange(): lax.all_to_all(blocks, ('row', 'col'), split_axis=0, concat_axis=0, tiled...  8.95 us
    all_to_all x1, starting transfers between devices, exchange(): lax.all_to_all(blocks, ('row', 'col'), split_axis=0, concat_axis=0, tiled...  4.22 us
  transfers between devices with their start and end apart: 1, of which 1 were waited for; matrix products, arithmetic and copies ran while one was open for 0% of the time, Pallas kernels for 0%

profile of v6, /device:TPU:1, one launch (start us, length us, event | category | flops | bytes accessed | tf_op | source)
XLA Modules:
  0.0 111.9 jit_solution(5611345116188204415)
XLA Ops:
  0.6 11.6 %shard_map.72 = (f32[1664,128]{1,0:T(8,128)S(1)}, s32[16,1024]{1,0:T(8,128)S(1)}, f32[16,1024]{1,0:T(8,128)S(1)}, f32[24,1024]{1,0:T(8,128)S(1)}, f32[128,128]{1...) custom-call(f32[18,8,1024]{2,1,0:T(8,128)} %camera_in.1, f32[6,8,1024]{2,1,0:T(8,128)} %point_in.1, ...), custom_call_target="tpu_custom_call" | custom-call | tf_op jit(solution)/shard_map/pallas_call | solution.py:611
  12.2 27.9 %all_to_all.54 = f32[128,1,1664]{2,1,0:T(1,128)S(1)} all-to-all(f32[128,1,1664]{2,1,0:T(1,128)S(1)} %bitcast.728), channel_id=1, replica_groups=mesh['row'=8,'col'=16] {'row','col'}, dimensions={0} | all-to-all | bytes 1703936 | tf_op jit(solution)/shard_map/all_to_all | solution.py:594
  40.2 0.0 copy-start
  40.2 0.0 copy-start.2
  40.2 0.0 copy-start.5
  40.2 4.7 %shard_map.73 = (f32[1680,128]{1,0:T(8,128)S(1)}, f32[360,128]{1,0:T(8,128)S(1)}, f32[88,128]{1,0:T(8,128)S(1)}, f32[256,128]{1,0:T(8,128)S(1)}, s32[1,1]{1,0:T(1,128)}) custom-call(f32[1664,128]{1,0:T(8,128)S(1)} %bitcast.727), custom_call_target="tpu_custom_call" | custom-call | tf_op jit(solution)/shard_map/pallas_call | solution.py:579
  44.9 15.4 %all_to_all.55 = f32[128,1,256]{2,1,0:T(1,128)S(1)} all-to-all(f32[128,1,256]{2,1,0:T(1,128)S(1)} %bitcast.732), channel_id=1, replica_groups=mesh['row'=8,'col'=16] {'row','col'}, dimensions={0} | all-to-all | bytes 262144 | tf_op jit(solution)/shard_map/all_to_all | solution.py:594
  60.4 2.7 %shard_map.74 = (f32[8,1024]{1,0:T(8,128)S(1)}, f32[256,128]{1,0:T(8,128)S(1)}) custom-call(f32[256,128]{1,0:T(8,128)S(1)} %bitcast.731, s32[16,1024]{1,0:T(8,128)S(1)} %get-tuple-element.61.route_ref, f32[6,8,1024]{2,1,0:T(8,128)S(1)} %get-tuple-element.62.masked_ref, f32[16,1024]{1,0:T(8,128)S(1)} %get-tuple-element.63.state_ref, ...), custom_call_target="tpu_custom_call" | custom-call | tf_op jit(solution)/shard_map/pallas_call | solution.py:579
  63.1 14.2 %all_to_all.56 = f32[128,1,256]{2,1,0:T(1,128)S(1)} all-to-all(f32[128,1,256]{2,1,0:T(1,128)S(1)} %bitcast.734), channel_id=1, replica_groups=mesh['row'=8,'col'=16] {'row','col'}, dimensions={0} | all-to-all | bytes 262144 | tf_op jit(solution)/shard_map/all_to_all | solution.py:594
  77.2 2.2 %shard_map.75 = (f32[72,128]{1,0:T(8,128)S(1)}, f32[256,128]{1,0:T(8,128)S(1)}) custom-call(f32[256,128]{1,0:T(8,128)S(1)} %bitcast.729, f32[1680,128]{1,0:T(8,128)S(1)} %get-tuple-element.68.feature_ref, f32[360,128]{1,0:T(8,128)S(1)} %get-tuple-element.69.factor_ref, f32[88,128]{1,0:T(8,128)S(1)} %get-tuple-element.70.first_ref), custom_call_target="tpu_custom_call" | custom-call | tf_op jit(solution)/shard_map/pallas_call | solution.py:579
  79.4 14.8 %all_to_all.57 = f32[128,1,256]{2,1,0:T(1,128)S(1)} all-to-all(f32[128,1,256]{2,1,0:T(1,128)S(1)} %bitcast.733), channel_id=1, replica_groups=mesh['row'=8,'col'=16] {'row','col'}, dimensions={0} | all-to-all | bytes 262144 | tf_op jit(solution)/shard_map/all_to_all | solution.py:594
  94.2 1.9 %shard_map.76 = (f32[8,1024]{1,0:T(8,128)S(1)}, f32[128,128]{1,0:T(8,128)}, f32[8,128]{1,0:T(8,128)S(1)}) custom-call(f32[256,128]{1,0:T(8,128)S(1)} %bitcast.730, s32[16,1024]{1,0:T(8,128)S(1)} %get-tuple-element.61.route_ref, f32[6,8,1024]{2,1,0:T(8,128)S(1)} %get-tuple-element.62.masked_ref, f32[16,1024]{1,0:T(8,128)S(1)} %get-tuple-element.63.state_ref, ...), custom_call_target="tpu_custom_call" | custom-call | tf_op jit(solution)/shard_map/pallas_call | solution.py:579
  96.1 4.2 %all-to-all-start.9 = ((f32[128,1,128]{2,1,0:T(1,128)}), f32[128,1,128]{2,1,0:T(1,128)S(1)}, u32[]{:S(2)}, u32[]{:S(2)}) async-start(f32[128,1,128]{2,1,0:T(1,128)} %bitcast.125), calls=%async_computation.9 | async-start | bytes 131072 | tf_op jit(solution)/shard_map/all_to_all | solution.py:594
  100.9 9.0 %all-to-all-done.9 = f32[128,1,128]{2,1,0:T(1,128)S(1)} async-done(((f32[128,1,128]{2,1,0:T(1,128)}), f32[128,1,128]{2,1,0:T(1,128)S(1)}, u32[]{:S(2)}, u32[]{:S(2)}) %all-to-all-start.9) | async-done | bytes 65568 | tf_op jit(solution)/shard_map/all_to_all | solution.py:594
  109.9 0.0 copy-done
  109.9 0.0 copy-done.1
  109.9 0.0 copy-done.2
  109.9 0.0 copy-done.5
  109.9 0.7 conditional.1
  109.9 0.4 branch_0_fun.1
  110.6 0.0 copy-start.6
  110.6 0.6 copy-done.6
  111.2 0.0 copy-start.7
  111.2 0.6 copy-done.7
  (1 shorter events, 0.0 us)
Async XLA Ops:
  40.2 69.7 %copy-start = (f32[18,8,1024]{2,1,0:T(8,128)S(1)}, f32[18,8,1024]{2,1,0:T(8,128)}, u32[]{:S(2)}) copy-start(f32[18,8,1024]{2,1,0:T(8,128)} %camera_in.1) | copy-start | bytes 1769476
  40.2 69.7 %copy-start.1 = (f32[6,8,1024]{2,1,0:T(8,128)S(1)}, f32[6,8,1024]{2,1,0:T(8,128)}, u32[]{:S(2)}) copy-start(f32[6,8,1024]{2,1,0:T(8,128)} %point_in.1) | copy-start | bytes 589828
  40.2 69.7 %copy-start.2 = (f32[2,8,1024]{2,1,0:T(8,128)S(1)}, f32[2,8,1024]{2,1,0:T(8,128)}, u32[]{:S(2)}) copy-start(f32[2,8,1024]{2,1,0:T(8,128)} %error_in.1) | copy-start | bytes 196612
  40.2 69.7 %copy-start.5 = (s32[1024]{0:T(1024)S(1)}, s32[1024]{0:T(1024)}, u32[]{:S(2)}) copy-start(s32[1024]{0:T(1024)} %param.11) | copy-start | bytes 12292
  96.1 13.8 %all-to-all-start.9 = ((f32[128,1,128]{2,1,0:T(1,128)}), f32[128,1,128]{2,1,0:T(1,128)S(1)}, u32[]{:S(2)}, u32[]{:S(2)}) async-start(f32[128,1,128]{2,1,0:T(1,128)} %bitcast.125), calls=%async_computation.9 | async-start | bytes 131072 | tf_op jit(solution)/shard_map/all_to_all | solution.py:594
  110.6 0.6 copy-start.6
  111.2 0.6 copy-start.7

commit v7 on v6

--- a/solution.py
+++ b/solution.py
@@ -82,15 +82,17 @@
     upto = jnp.where(iota((step, step), 0) <= iota((step, step), 1), 1.0, 0.0).astype(BF16)
     before = jnp.zeros((OWNERS, step), F32)
     names = iota((OWNERS, step), 0)
-    for s in range(TRACK):
-        for chunk in range(PT_DEV // step):
-            lanes = slice(chunk * step, (chunk + 1) * step)
-            chosen = names == route_ref[s : s + 1, lanes]
-            hot = jnp.where(chosen, 1.0, 0.0).astype(BF16)
-            owned_ref[s, :, lanes] = hot
-            counts = dot(hot, upto)
-            rank = jnp.sum(jnp.where(chosen, counts + before, 0.0), axis=0, keepdims=True) - 1.0
-            before = before + jnp.broadcast_to(counts[:, step - 1 : step], (OWNERS, step))
+    for chunk in range(PT_DEV // step):
+        lanes = slice(chunk * step, (chunk + 1) * step)
+        chosen = [names == route_ref[s : s + 1, lanes] for s in range(TRACK)]
+        hot = [jnp.where(here, 1.0, 0.0).astype(BF16) for here in chosen]
+        for s in range(TRACK):
+            owned_ref[s, :, lanes] = hot[s]
+        counts = dot(jnp.concatenate(hot, axis=0), upto)
+        for s in range(TRACK):
+            own = counts[s * OWNERS : (s + 1) * OWNERS, :]
+            rank = jnp.sum(jnp.where(chosen[s], own + before, 0.0), axis=0, keepdims=True) - 1.0
+            before = before + jnp.broadcast_to(own[:, step - 1 : step], (OWNERS, step))
             route_ref[TRACK + s : TRACK + s + 1, lanes] = rank.astype(jnp.int32)
 
     owner = route_ref[0:TRACK, :]
@@ -403,7 +405,11 @@
     for j in range(9):
         first_ref[j * 8 : (j + 1) * 8, :] = first[j]
     first_ref[72:80, :] = energy
-    first_ref[80:88, :] = jnp.broadcast_to(jnp.max(turned[COUNT_AT : COUNT_AT + 1, :], axis=1, keepdims=True), (8, LANES))
+    first_ref[80:88, :] = jnp.where(
+        iota((8, LANES), 0) < 4,
+        jnp.max(turned[COUNT_AT : COUNT_AT + 1, :], axis=1, keepdims=True),
+        jnp.max(turned[COUNT_AT + 1 : COUNT_AT + 2, :], axis=1, keepdims=True),
+    )
     image_slots(first, feature_ref, table_ref, image_ref, many)
     turn_out(image_ref, out_ref)
 
@@ -492,7 +498,7 @@
 def second_camera_kernel(got_ref, feature_ref, factor_ref, first_ref, second_ref, out_ref, hot_ref, parts_ref, table_ref, image_ref, sum_ref, wide_ref):
     for i in range(2):
         image_ref[i * LANES : (i + 1) * LANES, :] = turn_in(got_ref, i)
-    many = jnp.max(first_ref[80:88, :]) > FEW
+    many = jnp.max(first_ref[80:84, :]) > FEW
     wide_ref[...] = jnp.zeros((LANES, LANES), F32)
 
     def gather_terms(block):
@@ -534,7 +540,7 @@
     turn_out(image_ref, out_ref)
 
 
-def finish_kernel(curve_ref, scalar_ref, first_ref, second_ref, state_ref, first_pulled_ref, second_pulled_ref, camera_out, point_out, camera_ref, point_ref, camera_sem, point_sem):
+def finish_kernel(curve_ref, scalar_ref, first_ref, second_ref, state_ref, first_pulled_ref, second_pulled_ref, dense_camera, dense_point, camera_out, point_out, camera_ref, point_ref, camera_sem, point_sem):
     own = jnp.sum(curve_ref[...], axis=0, keepdims=True)[:, 0:1]
     energy, curvature, crossed, square = [
         scalar_ref[0:1, SPAN + at : SPAN + at + 1] for at in range(4)
@@ -554,8 +560,6 @@
             first_weight * first_ref[pl.ds(c, 9, stride=8), :]
             + second_weight * second_ref[pl.ds(c, 9, stride=8), :]
         )
-    camera_copy = pltpu.make_async_copy(camera_ref, camera_out, camera_sem)
-    camera_copy.start()
     left = [
         state_ref[6 + a : 7 + a, :]
         - first_weight * first_pulled_ref[a : a + 1, :]
@@ -565,10 +569,20 @@
     moved = times_inverse([state_ref[at : at + 1, :] for at in range(6)], left)
     for a in range(3):
         point_ref[a : a + 1, :] = moved[a]
-    point_copy = pltpu.make_async_copy(point_ref, point_out, point_sem)
-    point_copy.start()
-    camera_copy.wait()
-    point_copy.wait()
+
+    def send(camera, point):
+        copies = [
+            pltpu.make_async_copy(camera, camera_out, camera_sem),
+            pltpu.make_async_copy(point, point_out, point_sem),
+        ]
+        for copy in copies:
+            copy.start()
+        for copy in copies:
+            copy.wait()
+
+    over = jnp.max(first_ref[84:88, :]) > CAP
+    pl.when(over)(lambda: send(dense_camera, dense_point))
+    pl.when(jnp.logical_not(over))(lambda: send(camera_ref, point_ref))
 
 
 def call(kernel, outs, scratch, operands, in_scalar=0):
@@ -652,7 +666,8 @@
         [((2 * TRACK, PT_DEV), F32), ((TRACK, LANES), F32)],
         (exchange(out), route, masked, state, root, flag, owned),
     )
-    return overflow[0, 0], (exchange(curve), scalars, first, second, state, first_pulled, second_pulled)
+    overflow, curve = lax.optimization_barrier((overflow, exchange(curve)))
+    return overflow[0, 0], (curve, scalars, first, second, state, first_pulled, second_pulled)
 
 
 def finish(*operands):
@@ -661,7 +676,8 @@
         pl.pallas_call(
             finish_kernel,
             out_shape=[jax.ShapeDtypeStruct(shape, F32) for shape in shapes],
-            in_specs=[pl.BlockSpec(memory_space=pltpu.VMEM)] * len(operands),
+            in_specs=[pl.BlockSpec(memory_space=pltpu.VMEM)] * (len(operands) - 2)
+            + [pl.BlockSpec(memory_space=pl.ANY)] * 2,
             out_specs=[pl.BlockSpec(memory_space=pltpu.HBM)] * 2,
             scratch_shapes=[pltpu.VMEM(shape, F32) for shape in shapes]
             + [pltpu.SemaphoreType.DMA] * 2,
@@ -878,13 +894,13 @@
 def on_device(camera_jacobian, point_jacobian, residuals, observed_camera, track_length):
     operands = (camera_jacobian, point_jacobian, residuals, observed_camera, track_length)
     overflow, kept = by_slots(*operands)
-    return lax.cond(
+    dense = lax.cond(
         overflow > 0,
-        lambda given, unused: by_dense(*given),
-        lambda unused, found: finish(*found),
-        operands,
-        kept,
-    )
+        lambda *given: by_dense(*given),
+        lambda *given: (jnp.zeros((9, CAM_DEV), F32), jnp.zeros((3, PT_DEV), F32)),
+        *operands,
+    )
+    return finish(*kept, *dense)
 
 
 def solution(mesh):

time: 111 us -> 112 us (level); the launches traced: 112 us -> 112 us
  blocking collectives: 72.3 us -> 70.8 us
    all_to_all x4, blocking collectives: 72.3 us -> 70.8 us  [exchange(): lax.all_to_all(blocks, ('row', 'col'), split_axis=0, concat_axis=0, tiled...]
    unnamed x12 -> x10, local copies, waits for them, and re-layouts: 1.22 us -> 0.02 us
    another operation x0 -> x2, local copies, waits for them, and re-layouts: none -> 1.2 us
where the time goes in v7:
time: 112 us
  blocking collectives  70.8 us (63%)
  Pallas kernels  24.1 us (22%)
  waiting for transfers between devices  9.6 us (9%)
  starting transfers between devices  4.22 us (4%)
  between operations  1.58 us (1%)
  local copies, waits for them, and re-layouts  1.22 us (1%)
    all_to_all x4, blocking collectives, exchange(): lax.all_to_all(blocks, ('row', 'col'), split_axis=0, concat_axis=0, tiled...  70.8 us
    pallas_call x1, Pallas kernels, by_slots(): pl.pallas_call(prepare_kernel, out_shape=[jax.ShapeDtypeStruct(shape, dty...  11.7 us
    pallas_call x4, Pallas kernels, call(): pl.pallas_call(kernel, out_shape=[jax.ShapeDtypeStruct(shape, dtype) for...  11.5 us
    all_to_all x1, waiting for transfers between devices, exchange(): lax.all_to_all(blocks, ('row', 'col'), split_axis=0, concat_axis=0, tiled...  9.6 us
    all_to_all x1, starting transfers between devices, exchange(): lax.all_to_all(blocks, ('row', 'col'), split_axis=0, concat_axis=0, tiled...  4.22 us
  transfers between devices with their start and end apart: 1, of which 1 were waited for; matrix products, arithmetic and copies ran while one was open for 0% of the time, Pallas kernels for 0%

profile of v7, /device:TPU:1, one launch (start us, length us, event | category | flops | bytes accessed | tf_op | source)
XLA Modules:
  0.0 111.6 jit_solution(5838752776829701823)
XLA Ops:
  0.6 11.7 %shard_map.68 = (f32[1664,128]{1,0:T(8,128)S(1)}, s32[16,1024]{1,0:T(8,128)S(1)}, f32[16,1024]{1,0:T(8,128)S(1)}, f32[24,1024]{1,0:T(8,128)S(1)}, f32[128,128]{1...) custom-call(f32[18,8,1024]{2,1,0:T(8,128)} %camera_in.1, f32[6,8,1024]{2,1,0:T(8,128)} %point_in.1, ...), custom_call_target="tpu_custom_call" | custom-call | tf_op jit(solution)/shard_map/pallas_call | solution.py:625
  12.3 27.9 %all_to_all.54 = f32[128,1,1664]{2,1,0:T(1,128)S(1)} all-to-all(f32[128,1,1664]{2,1,0:T(1,128)S(1)} %bitcast.727), channel_id=1, replica_groups=mesh['row'=8,'col'=16] {'row','col'}, dimensions={0} | all-to-all | bytes 1703936 | tf_op jit(solution)/shard_map/all_to_all | solution.py:608
  40.3 0.0 copy-start
  40.3 0.0 copy-start.1
  40.3 0.0 copy-start.2
  40.3 0.0 copy-start.6
  40.3 4.7 %shard_map.69 = (f32[1680,128]{1,0:T(8,128)S(1)}, f32[360,128]{1,0:T(8,128)S(1)}, f32[88,128]{1,0:T(8,128)S(1)}, f32[256,128]{1,0:T(8,128)S(1)}, s32[1,1]{1,0:T(1,128)}) custom-call(f32[1664,128]{1,0:T(8,128)S(1)} %bitcast.726), custom_call_target="tpu_custom_call" | custom-call | tf_op jit(solution)/shard_map/pallas_call | solution.py:593
  45.0 14.5 %all_to_all.55 = f32[128,1,256]{2,1,0:T(1,128)S(1)} all-to-all(f32[128,1,256]{2,1,0:T(1,128)S(1)} %bitcast.732), channel_id=1, replica_groups=mesh['row'=8,'col'=16] {'row','col'}, dimensions={0} | all-to-all | bytes 262144 | tf_op jit(solution)/shard_map/all_to_all | solution.py:608
  59.5 2.7 %shard_map.70 = (f32[8,1024]{1,0:T(8,128)S(1)}, f32[256,128]{1,0:T(8,128)S(1)}) custom-call(f32[256,128]{1,0:T(8,128)S(1)} %bitcast.730, s32[16,1024]{1,0:T(8,128)S(1)} %get-tuple-element.43.route_ref, f32[6,8,1024]{2,1,0:T(8,128)S(1)} %get-tuple-element.44.masked_ref, f32[16,1024]{1,0:T(8,128)S(1)} %get-tuple-element.45.state_ref, ...), custom_call_target="tpu_custom_call" | custom-call | tf_op jit(solution)/shard_map/pallas_call | solution.py:593
  62.3 14.2 %all_to_all.56 = f32[128,1,256]{2,1,0:T(1,128)S(1)} all-to-all(f32[128,1,256]{2,1,0:T(1,128)S(1)} %bitcast.734), channel_id=1, replica_groups=mesh['row'=8,'col'=16] {'row','col'}, dimensions={0} | all-to-all | bytes 262144 | tf_op jit(solution)/shard_map/all_to_all | solution.py:608
  76.4 2.2 %shard_map.71 = (f32[72,128]{1,0:T(8,128)S(1)}, f32[256,128]{1,0:T(8,128)S(1)}) custom-call(f32[256,128]{1,0:T(8,128)S(1)} %bitcast.728, f32[1680,128]{1,0:T(8,128)S(1)} %get-tuple-element.50.feature_ref, f32[360,128]{1,0:T(8,128)S(1)} %get-tuple-element.51.factor_ref, f32[88,128]{1,0:T(8,128)S(1)} %get-tuple-element.52.first_ref), custom_call_target="tpu_custom_call" | custom-call | tf_op jit(solution)/shard_map/pallas_call | solution.py:593
  78.7 14.2 %all_to_all.57 = f32[128,1,256]{2,1,0:T(1,128)S(1)} all-to-all(f32[128,1,256]{2,1,0:T(1,128)S(1)} %bitcast.733), channel_id=1, replica_groups=mesh['row'=8,'col'=16] {'row','col'}, dimensions={0} | all-to-all | bytes 262144 | tf_op jit(solution)/shard_map/all_to_all | solution.py:608
  92.8 1.9 %shard_map.72 = (f32[8,1024]{1,0:T(8,128)S(1)}, f32[128,128]{1,0:T(8,128)}, f32[8,128]{1,0:T(8,128)S(1)}) custom-call(f32[256,128]{1,0:T(8,128)S(1)} %bitcast.729, s32[16,1024]{1,0:T(8,128)S(1)} %get-tuple-element.43.route_ref, f32[6,8,1024]{2,1,0:T(8,128)S(1)} %get-tuple-element.44.masked_ref, f32[16,1024]{1,0:T(8,128)S(1)} %get-tuple-element.45.state_ref, ...), custom_call_target="tpu_custom_call" | custom-call | tf_op jit(solution)/shard_map/pallas_call | solution.py:593
  94.7 4.2 %all-to-all-start.9 = ((f32[128,1,128]{2,1,0:T(1,128)}), f32[128,1,128]{2,1,0:T(1,128)S(1)}, u32[]{:S(2)}, u32[]{:S(2)}) async-start(f32[128,1,128]{2,1,0:T(1,128)} %bitcast.122), calls=%async_computation.9 | async-start | bytes 131072 | tf_op jit(solution)/shard_map/all_to_all | solution.py:608
  98.9 9.6 %all-to-all-done.9 = f32[128,1,128]{2,1,0:T(1,128)S(1)} async-done(((f32[128,1,128]{2,1,0:T(1,128)}), f32[128,1,128]{2,1,0:T(1,128)S(1)}, u32[]{:S(2)}, u32[]{:S(2)}) %all-to-all-start.9) | async-done | bytes 65568 | tf_op jit(solution)/shard_map/all_to_all | solution.py:608
  109.2 0.0 copy-done
  109.2 0.0 copy-done.1
  109.2 0.0 copy-done.2
  109.2 0.0 copy-done.3
  109.2 0.0 copy-done.6
  109.2 1.2 %conditional.1 = (f32[9,384]{1,0:T(8,128)}, f32[3,1024]{1,0:T(4,128)}) conditional(s32[]{:T(128)} %bitcast.124, () %tuple.17, (s32[8,1024]{1,0:T(8,128)S(1)}, f32[18,8,1024]{2,1,0:T(8,128)S(1)}, s32[1024]{0:T(1024)S(1)}, f32[6,8,1024]{2,1,0:T(8,128)S(1)}, f32[2,8,1024]{2,1,0:T(8,128)S(1)}) %tuple.378), branch_computations={%region_0.0_spmd, %region_1.0_spmd} | conditional | flops 12982441 | bytes 149947568 | solution.py:897
  109.3 0.6 broadcast.452
  109.9 0.6 broadcast.453
  110.5 0.9 shard_map.73
  (1 shorter events, 0.0 us)
Async XLA Ops:
  40.3 68.9 %copy-start = (f32[18,8,1024]{2,1,0:T(8,128)S(1)}, f32[18,8,1024]{2,1,0:T(8,128)}, u32[]{:S(2)}) copy-start(f32[18,8,1024]{2,1,0:T(8,128)} %camera_in.1) | copy-start | bytes 1769476
  40.3 68.9 %copy-start.1 = (f32[6,8,1024]{2,1,0:T(8,128)S(1)}, f32[6,8,1024]{2,1,0:T(8,128)}, u32[]{:S(2)}) copy-start(f32[6,8,1024]{2,1,0:T(8,128)} %point_in.1) | copy-start | bytes 589828
  40.3 69.0 %copy-start.2 = (f32[2,8,1024]{2,1,0:T(8,128)S(1)}, f32[2,8,1024]{2,1,0:T(8,128)}, u32[]{:S(2)}) copy-start(f32[2,8,1024]{2,1,0:T(8,128)} %error_in.1) | copy-start | bytes 196612
  40.3 69.0 %copy-start.3 = (s32[8,1024]{1,0:T(8,128)S(1)}, s32[8,1024]{1,0:T(8,128)}, u32[]{:S(2)}) copy-start(s32[8,1024]{1,0:T(8,128)} %index_ref.1) | copy-start | bytes 98308
  40.3 69.0 %copy-start.6 = (s32[1024]{0:T(1024)S(1)}, s32[1024]{0:T(1024)}, u32[]{:S(2)}) copy-start(s32[1024]{0:T(1024)} %param.11) | copy-start | bytes 12292
  94.7 13.8 %all-to-all-start.9 = ((f32[128,1,128]{2,1,0:T(1,128)}), f32[128,1,128]{2,1,0:T(1,128)S(1)}, u32[]{:S(2)}, u32[]{:S(2)}) async-start(f32[128,1,128]{2,1,0:T(1,128)} %bitcast.122), calls=%async_computation.9 | async-start | bytes 131072 | tf_op jit(solution)/shard_map/all_to_all | solution.py:608

commit v8 on v7

--- a/solution.py
+++ b/solution.py
@@ -82,17 +82,15 @@
     upto = jnp.where(iota((step, step), 0) <= iota((step, step), 1), 1.0, 0.0).astype(BF16)
     before = jnp.zeros((OWNERS, step), F32)
     names = iota((OWNERS, step), 0)
-    for chunk in range(PT_DEV // step):
-        lanes = slice(chunk * step, (chunk + 1) * step)
-        chosen = [names == route_ref[s : s + 1, lanes] for s in range(TRACK)]
-        hot = [jnp.where(here, 1.0, 0.0).astype(BF16) for here in chosen]
-        for s in range(TRACK):
-            owned_ref[s, :, lanes] = hot[s]
-        counts = dot(jnp.concatenate(hot, axis=0), upto)
-        for s in range(TRACK):
-            own = counts[s * OWNERS : (s + 1) * OWNERS, :]
-            rank = jnp.sum(jnp.where(chosen[s], own + before, 0.0), axis=0, keepdims=True) - 1.0
-            before = before + jnp.broadcast_to(own[:, step - 1 : step], (OWNERS, step))
+    for s in range(TRACK):
+        for chunk in range(PT_DEV // step):
+            lanes = slice(chunk * step, (chunk + 1) * step)
+            chosen = names == route_ref[s : s + 1, lanes]
+            hot = jnp.where(chosen, 1.0, 0.0).astype(BF16)
+            owned_ref[s, :, lanes] = hot
+            counts = dot(hot, upto)
+            rank = jnp.sum(jnp.where(chosen, counts + before, 0.0), axis=0, keepdims=True) - 1.0
+            before = before + jnp.broadcast_to(counts[:, step - 1 : step], (OWNERS, step))
             route_ref[TRACK + s : TRACK + s + 1, lanes] = rank.astype(jnp.int32)
 
     owner = route_ref[0:TRACK, :]
@@ -676,8 +674,7 @@
         pl.pallas_call(
             finish_kernel,
             out_shape=[jax.ShapeDtypeStruct(shape, F32) for shape in shapes],
-            in_specs=[pl.BlockSpec(memory_space=pltpu.VMEM)] * (len(operands) - 2)
-            + [pl.BlockSpec(memory_space=pl.ANY)] * 2,
+            in_specs=[pl.BlockSpec(memory_space=pltpu.VMEM)] * len(operands),
             out_specs=[pl.BlockSpec(memory_space=pltpu.HBM)] * 2,
             scratch_shapes=[pltpu.VMEM(shape, F32) for shape in shapes]
             + [pltpu.SemaphoreType.DMA] * 2,

time: 112 us -> 113 us (level)
  no operation moved by 1% of the time
where the time goes in v8:
time: 113 us
  blocking collectives  71.3 us (63%)
  Pallas kernels  24.8 us (22%)
  waiting for transfers between devices  9.6 us (8%)
  starting transfers between devices  4.22 us (4%)
  between operations  1.58 us (1%)
  local copies, waits for them, and re-layouts  1.22 us (1%)
    all_to_all x4, blocking collectives, exchange(): lax.all_to_all(blocks, ('row', 'col'), split_axis=0, concat_axis=0, tiled...  71.3 us
    pallas_call x1, Pallas kernels, by_slots(): pl.pallas_call(prepare_kernel, out_shape=[jax.ShapeDtypeStruct(shape, dty...  11.6 us
    pallas_call x4, Pallas kernels, call(): pl.pallas_call(kernel, out_shape=[jax.ShapeDtypeStruct(shape, dtype) for...  11.5 us
    all_to_all x1, waiting for transfers between devices, exchange(): lax.all_to_all(blocks, ('row', 'col'), split_axis=0, concat_axis=0, tiled...  9.6 us
    all_to_all x1, starting transfers between devices, exchange(): lax.all_to_all(blocks, ('row', 'col'), split_axis=0, concat_axis=0, tiled...  4.22 us
  transfers between devices with their start and end apart: 1, of which 1 were waited for; matrix products, arithmetic and copies ran while one was open for 0% of the time, Pallas kernels for 0%

profile of v8, /device:TPU:1, one launch (start us, length us, event | category | flops | bytes accessed | tf_op | source)
XLA Modules:
  0.0 112.7 jit_solution(11584364892623323061)
XLA Ops:
  0.6 11.6 %shard_map.68 = (f32[1664,128]{1,0:T(8,128)S(1)}, s32[16,1024]{1,0:T(8,128)S(1)}, f32[16,1024]{1,0:T(8,128)S(1)}, f32[24,1024]{1,0:T(8,128)S(1)}, f32[128,128]{1...) custom-call(f32[18,8,1024]{2,1,0:T(8,128)} %camera_in.1, f32[6,8,1024]{2,1,0:T(8,128)} %point_in.1, ...), custom_call_target="tpu_custom_call" | custom-call | tf_op jit(solution)/shard_map/pallas_call | solution.py:623
  12.2 27.9 %all_to_all.54 = f32[128,1,1664]{2,1,0:T(1,128)S(1)} all-to-all(f32[128,1,1664]{2,1,0:T(1,128)S(1)} %bitcast.727), channel_id=1, replica_groups=mesh['row'=8,'col'=16] {'row','col'}, dimensions={0} | all-to-all | bytes 1703936 | tf_op jit(solution)/shard_map/all_to_all | solution.py:606
  40.2 0.0 copy-start
  40.2 0.0 copy-start.1
  40.2 0.0 copy-start.2
  40.2 0.0 copy-start.6
  40.2 4.8 %shard_map.69 = (f32[1680,128]{1,0:T(8,128)S(1)}, f32[360,128]{1,0:T(8,128)S(1)}, f32[88,128]{1,0:T(8,128)S(1)}, f32[256,128]{1,0:T(8,128)S(1)}, s32[1,1]{1,0:T(1,128)}) custom-call(f32[1664,128]{1,0:T(8,128)S(1)} %bitcast.726), custom_call_target="tpu_custom_call" | custom-call | tf_op jit(solution)/shard_map/pallas_call | solution.py:591
  45.0 15.0 %all_to_all.55 = f32[128,1,256]{2,1,0:T(1,128)S(1)} all-to-all(f32[128,1,256]{2,1,0:T(1,128)S(1)} %bitcast.732), channel_id=1, replica_groups=mesh['row'=8,'col'=16] {'row','col'}, dimensions={0} | all-to-all | bytes 262144 | tf_op jit(solution)/shard_map/all_to_all | solution.py:606
  60.0 2.7 %shard_map.70 = (f32[8,1024]{1,0:T(8,128)S(1)}, f32[256,128]{1,0:T(8,128)S(1)}) custom-call(f32[256,128]{1,0:T(8,128)S(1)} %bitcast.730, s32[16,1024]{1,0:T(8,128)S(1)} %get-tuple-element.43.route_ref, f32[6,8,1024]{2,1,0:T(8,128)S(1)} %get-tuple-element.44.masked_ref, f32[16,1024]{1,0:T(8,128)S(1)} %get-tuple-element.45.state_ref, ...), custom_call_target="tpu_custom_call" | custom-call | tf_op jit(solution)/shard_map/pallas_call | solution.py:591
  62.7 14.2 %all_to_all.56 = f32[128,1,256]{2,1,0:T(1,128)S(1)} all-to-all(f32[128,1,256]{2,1,0:T(1,128)S(1)} %bitcast.734), channel_id=1, replica_groups=mesh['row'=8,'col'=16] {'row','col'}, dimensions={0} | all-to-all | bytes 262144 | tf_op jit(solution)/shard_map/all_to_all | solution.py:606
  76.9 2.2 %shard_map.71 = (f32[72,128]{1,0:T(8,128)S(1)}, f32[256,128]{1,0:T(8,128)S(1)}) custom-call(f32[256,128]{1,0:T(8,128)S(1)} %bitcast.728, f32[1680,128]{1,0:T(8,128)S(1)} %get-tuple-element.50.feature_ref, f32[360,128]{1,0:T(8,128)S(1)} %get-tuple-element.51.factor_ref, f32[88,128]{1,0:T(8,128)S(1)} %get-tuple-element.52.first_ref), custom_call_target="tpu_custom_call" | custom-call | tf_op jit(solution)/shard_map/pallas_call | solution.py:591
  79.1 14.2 %all_to_all.57 = f32[128,1,256]{2,1,0:T(1,128)S(1)} all-to-all(f32[128,1,256]{2,1,0:T(1,128)S(1)} %bitcast.733), channel_id=1, replica_groups=mesh['row'=8,'col'=16] {'row','col'}, dimensions={0} | all-to-all | bytes 262144 | tf_op jit(solution)/shard_map/all_to_all | solution.py:606
  93.3 1.9 %shard_map.72 = (f32[8,1024]{1,0:T(8,128)S(1)}, f32[128,128]{1,0:T(8,128)}, f32[8,128]{1,0:T(8,128)S(1)}) custom-call(f32[256,128]{1,0:T(8,128)S(1)} %bitcast.729, s32[16,1024]{1,0:T(8,128)S(1)} %get-tuple-element.43.route_ref, f32[6,8,1024]{2,1,0:T(8,128)S(1)} %get-tuple-element.44.masked_ref, f32[16,1024]{1,0:T(8,128)S(1)} %get-tuple-element.45.state_ref, ...), custom_call_target="tpu_custom_call" | custom-call | tf_op jit(solution)/shard_map/pallas_call | solution.py:591
  95.1 4.2 %all-to-all-start.9 = ((f32[128,1,128]{2,1,0:T(1,128)}), f32[128,1,128]{2,1,0:T(1,128)S(1)}, u32[]{:S(2)}, u32[]{:S(2)}) async-start(f32[128,1,128]{2,1,0:T(1,128)} %bitcast.122), calls=%async_computation.9 | async-start | bytes 131072 | tf_op jit(solution)/shard_map/all_to_all | solution.py:606
  99.4 9.6 %all-to-all-done.9 = f32[128,1,128]{2,1,0:T(1,128)S(1)} async-done(((f32[128,1,128]{2,1,0:T(1,128)}), f32[128,1,128]{2,1,0:T(1,128)S(1)}, u32[]{:S(2)}, u32[]{:S(2)}) %all-to-all-start.9) | async-done | bytes 65568 | tf_op jit(solution)/shard_map/all_to_all | solution.py:606
  109.6 0.0 copy-done
  109.6 0.0 copy-done.1
  109.6 0.0 copy-done.2
  109.6 0.0 copy-done.3
  109.7 0.0 copy-done.6
  109.7 1.2 %conditional.1 = (f32[9,384]{1,0:T(8,128)}, f32[3,1024]{1,0:T(4,128)}) conditional(s32[]{:T(128)} %bitcast.124, () %tuple.17, (s32[8,1024]{1,0:T(8,128)S(1)}, f32[18,8,1024]{2,1,0:T(8,128)S(1)}, s32[1024]{0:T(1024)S(1)}, f32[6,8,1024]{2,1,0:T(8,128)S(1)}, f32[2,8,1024]{2,1,0:T(8,128)S(1)}) %tuple.378), branch_computations={%region_0.0_spmd, %region_1.0_spmd} | conditional | flops 12982441 | bytes 149947568 | solution.py:894
  109.7 0.6 broadcast.452
  110.3 0.6 broadcast.453
  110.9 1.6 %shard_map.73 = (f32[9,384]{1,0:T(8,128)}, f32[3,1024]{1,0:T(4,128)}) custom-call(f32[128,128]{1,0:T(8,128)S(1)} %bitcast.731, f32[8,128]{1,0:T(8,128)S(1)} %get-tuple-element.56.scalar_ref, f32[88,128]{1,0:T(8,128)S(1)} %get-tuple-element.52.first_ref, f32[72,128]{1,0:T(8,128)S(1)} %get-tuple-element.57.second_ref, ...), custom_call_target="tpu_custom_call" | custom-call | tf_op jit(solution)/shard_map/pallas_call | solution.py:674
  (1 shorter events, 0.0 us)
Async XLA Ops:
  40.2 69.4 %copy-start = (f32[18,8,1024]{2,1,0:T(8,128)S(1)}, f32[18,8,1024]{2,1,0:T(8,128)}, u32[]{:S(2)}) copy-start(f32[18,8,1024]{2,1,0:T(8,128)} %camera_in.1) | copy-start | bytes 1769476
  40.2 69.4 %copy-start.1 = (f32[6,8,1024]{2,1,0:T(8,128)S(1)}, f32[6,8,1024]{2,1,0:T(8,128)}, u32[]{:S(2)}) copy-start(f32[6,8,1024]{2,1,0:T(8,128)} %point_in.1) | copy-start | bytes 589828
  40.2 69.5 %copy-start.2 = (f32[2,8,1024]{2,1,0:T(8,128)S(1)}, f32[2,8,1024]{2,1,0:T(8,128)}, u32[]{:S(2)}) copy-start(f32[2,8,1024]{2,1,0:T(8,128)} %error_in.1) | copy-start | bytes 196612
  40.2 69.5 %copy-start.3 = (s32[8,1024]{1,0:T(8,128)S(1)}, s32[8,1024]{1,0:T(8,128)}, u32[]{:S(2)}) copy-start(s32[8,1024]{1,0:T(8,128)} %index_ref.1) | copy-start | bytes 98308
  40.2 69.5 %copy-start.6 = (s32[1024]{0:T(1024)S(1)}, s32[1024]{0:T(1024)}, u32[]{:S(2)}) copy-start(s32[1024]{0:T(1024)} %param.11) | copy-start | bytes 12292
  95.1 13.8 %all-to-all-start.9 = ((f32[128,1,128]{2,1,0:T(1,128)}), f32[128,1,128]{2,1,0:T(1,128)S(1)}, u32[]{:S(2)}, u32[]{:S(2)}) async-start(f32[128,1,128]{2,1,0:T(1,128)} %bitcast.122), calls=%async_computation.9 | async-start | bytes 131072 | tf_op jit(solution)/shard_map/all_to_all | solution.py:606
